TPU v7x, 128 devices: a whole 4x4x4 slice. The times are simulated.
128 devices in a mesh: row: 8 (over x_lo, y), col: 8 (over x_hi, z), depth: 2 (over core).
Axes of the slice: x: 4 (x_hi: 2, x_lo: 2; x = x_hi * 2 + x_lo), y: 4, z: 4, core: 2. Of those that a mesh axis runs over, the one named last changes fastest.
Arguments:
- half_slabs: bfloat16 [4, 12000, 1536], P('depth', 'row', 'col'), may hold values from -0.67578125 to 0.67578125
Outputs:
- exchange_matrix: float32 [12000, 12000], P('row', ('col', 'depth'))
All inputs are finite; a program needn't handle non-finite values.
Results may differ from a plain program's by a relative error of at most 0.0003.
Values may be sent and summed in bfloat16 or wider, within the bound.
No kernel may reach another device: no remote copies, remote signals or barrier semaphores. Data moves between devices by JAX's collectives and lax.ppermute only.
A program may use at most 128 MiB of HBM per device.

v0:
```python
import jax
import jax.numpy as jnp
from jax import lax
from jax.sharding import PartitionSpec as P


def spread(block, axis, source):
    block = jnp.where(lax.axis_index(axis) == source, block, jnp.zeros_like(block))
    return lax.psum(block, axis)


def body(half_slabs):
    window_part = lax.all_gather(half_slabs, "depth", axis=0, tiled=True)
    mine_rows = lax.all_gather(window_part, "col", axis=2, tiled=True)
    half_rows = mine_rows.shape[1] // lax.axis_size("depth")
    partner_part = lax.dynamic_slice_in_dim(
        mine_rows, lax.axis_index("depth") * half_rows, half_rows, 1
    )
    partner_rows = spread(partner_part, "row", lax.axis_index("col"))
    block_sum = jnp.einsum(
        "qmi,qni->mn", mine_rows, partner_rows, preferred_element_type=jnp.float32
    )
    return block_sum


def solution(mesh):
    placed = (P("depth", "row", "col"),)
    return jax.shard_map(
        body, mesh=mesh, in_specs=placed, out_specs=P("row", ("col", "depth")), check_vma=False
    )
```

profile of v0, /device:TPU:1, one launch (start us, length us, event | category | flops | bytes accessed | tf_op | source)
XLA Modules:
  0.0 480.7 jit_solution(5311449943529152044)
XLA Ops:
  6.5 0.0 all-gather.3.cloned.1.call-start
  6.5 0.7 all-gather.3.cloned.1.call-update
  7.3 0.0 all-gather.5.cloned.1.call-start
  7.3 19.1 %all-gather.3.cloned.1.call-done = bf16[4,1500,192]{1,2,0:T(8,128)(2,1)} async-done(((bf16[2,1500,192]{1,2,0:T(8,128)(2,1)}), bf16[4,1500,192]{1,2,0:T(8,128)(2,1)}) %all-gather.3.cloned.1.call-update) | async-done | bytes 2304016 | tf_op jit(solution)/shard_map/all_gather | solution.py:13
  26.4 0.0 all-gather.5.cloned.1.call-update
  26.4 0.0 all-reduce.2.cloned.1.call-start
  26.4 204.6 %all-gather.5.cloned.1.call-done = bf16[4,1500,1536]{1,2,0:T(8,128)(2,1)} async-done(((bf16[4,1500,192]{1,2,0:T(8,128)(2,1)}), bf16[4,1500,1536]{1,2,0:T(8,128)(2,1)}) %all-gather.5.cloned.1.call-update) | async-done | bytes 18432016 | tf_op jit(solution)/shard_map/all_gather | solution.py:14
  231.0 13.8 %dynamic-slice_select_fusion = bf16[4,750,1536]{1,2,0:T(8,128)(2,1)} fusion(bf16[4,1500,1536]{1,2,0:T(8,128)(2,1)} %all-gather.5.cloned.1.call-done, s32[]{:T(128)S(6)} %select_n.12, pred[]{:T(512)S(6)} %eq.3), kind=kLoop, calls=%fused_computation | loop fusion | flops 4608000 | bytes 18432004 | tf_op jit(solution)/shard_map/jit(_where)/select_n | solution.py:8
  244.9 0.0 all-reduce.2.cloned.1.call-update
  244.9 202.4 %all-reduce.2.cloned.1.call-done = bf16[4,750,1536]{1,2,0:T(8,128)(2,1)} async-done(((bf16[4,750,1536]{1,2,0:T(8,128)(2,1)}), bf16[4,750,1536]{1,2,0:T(8,128)(2,1)}) %all-reduce.2.cloned.1.call-update) | async-done | bytes 9216016 | tf_op jit(solution)/shard_map/psum | solution.py:9
  447.3 20.9 %convolution_bitcast_fusion = f32[1500,750]{0,1:T(8,128)} fusion(bf16[4,750,1536]{1,2,0:T(8,128)(2,1)} %all-reduce.2.cloned.1.call-done, bf16[4,1500,1536]{1,2,0:T(8,128)(2,1)} %all-gather.5.cloned.1.call-done), kind=kOutput, calls=%fused_computation.1 | convolution fusion | flops 13824000000 | bytes 32148000 | tf_op jit(solution)/shard_map/qmi,qni->mn/dot_general | solution.py:20
  468.2 6.0 %copy.5 = f32[1500,750]{1,0:T(8,128)} copy(f32[1500,750]{0,1:T(8,128)} %convolution_bitcast_fusion) | data formatting | bytes 9000000 | tf_op jit(solution)/shard_map/qmi,qni->mn/dot_general | solution.py:20
Async XLA Ops:
  6.5 19.8 %all-gather.3.cloned.1.call-start = ((), (), s32[]{:S(2)}) async-start(), calls=%async_computation | async-start | bytes 3538944 | tf_op jit(solution)/shard_map/all_gather | solution.py:13
  7.3 223.8 %all-gather.5.cloned.1.call-start = ((), (), s32[]{:S(2)}) async-start(), calls=%async_computation.1 | async-start | bytes 21233664 | tf_op jit(solution)/shard_map/all_gather | solution.py:14
  26.4 420.9 %all-reduce.2.cloned.1.call-start = ((), (), s32[]{:S(2)}) async-start(), calls=%async_computation.2 | async-start | bytes 18874368 | tf_op jit(solution)/shard_map/psum | solution.py:9
Sparse Core Ops, SparseCore 0:
  9.0 17.2 all-gather.2
  28.7 202.3 all-gather.4
  245.0 202.2 all-reduce.1
where the time goes:
time: 481 us
  waiting for transfers between devices  427 us (89%)
  matrix products  20.9 us (4%)
  other arithmetic  13.8 us (3%)
  between operations  13.1 us (3%)
  local copies, waits for them, and re-layouts  5.99 us (1%)
    all_gather x1, waiting for transfers between devices, body(): mine_rows = lax.all_gather(window_part, 'col', axis=2, tiled=True)  205 us
    psum x1, waiting for transfers between devices, spread(): return lax.psum(block, axis)  202 us
    dot_general x1, matrix products, body(): jnp.einsum('qmi,qni->mn', mine_rows, partner_rows, preferred_element_type...  20.9 us
    all_gather x1, waiting for transfers between devices, body(): window_part = lax.all_gather(half_slabs, 'depth', axis=0, tiled=True)  19.1 us
    select_n x1, other arithmetic, spread(): jnp.where(lax.axis_index(axis) == source, block, jnp.zeros_like(block))  13.8 us
  transfers between devices with their start and end apart: 3, of which 3 were waited for; matrix products, arithmetic and copies ran while one was open for 0% of the time, Pallas kernels for 0%

commit v1 on v0

v1 whole, which is shorter than its diff:
```python
import itertools

import jax
import jax.numpy as jnp
import numpy as np
from jax import lax
from jax.experimental import pallas as pl
from jax.experimental.pallas import tpu as pltpu
from jax.sharding import Mesh
from jax.sharding import PartitionSpec as P

AXES = ("xl", "y", "xh", "z", "d")
SIZES = (2, 4, 2, 4, 2)
GAMMA = (0, 2)
ROWS, COLS, PART = 1536, 768, 384
TILE = 256


def perm(target):
    out = []
    for at in itertools.product(*map(range, SIZES)):
        to = target(*at)
        out.append((int(np.ravel_multi_index(at, SIZES)), int(np.ravel_multi_index(to, SIZES))))
    return out


def turn(cross):
    def target(xl, y, xh, z, d):
        e = 1 - d if cross else d
        return xh ^ e, (GAMMA[e] - y - z) % 4, xl, y, e

    return perm(target)


Z_RING = perm(lambda xl, y, xh, z, d: (xl, y, xh, (z + 1 - 2 * d) % 4, d))
Y_RING = perm(lambda xl, y, xh, z, d: (xl, (y + 1 - 2 * d) % 4, xh, z, d))
X_FAR = perm(lambda xl, y, xh, z, d: (xl, y, 1 - xh, z, d))
X_NEAR = perm(lambda xl, y, xh, z, d: (1 - xl, y, xh, z, d))
CORES = perm(lambda xl, y, xh, z, d: (xl, y, xh, z, 1 - d))


def send(block, pairs):
    return lax.ppermute(block, AXES, pairs)


def multiply_kernel(which, *refs):
    own, other, columns = refs[:8], refs[8:16], refs[16:24]
    out, lhs, rhs, lhs_sem, rhs_sem = refs[24:]
    tile = pl.program_id(0)
    tiles = pl.num_programs(0)

    def lhs_copy(part, source, at):
        rows = pl.ds(at * TILE, TILE)
        return pltpu.make_async_copy(
            source.at[rows], lhs.at[rows, pl.ds(part * PART, PART)], lhs_sem.at[part, at]
        )

    def rhs_copy(piece):
        return pltpu.make_async_copy(
            columns[piece], rhs.at[pl.ds(piece * 2 * PART, 2 * PART)], rhs_sem.at[piece]
        )

    @pl.when(tile == 0)
    def _():
        for piece in range(8):
            rhs_copy(piece).start()
        for at in range(ROWS // TILE):
            for piece in range(8):
                for side, sources in enumerate((own, other)):
                    for k in range(8):
                        @pl.when(which[2 * piece + side] == k)
                        def _():
                            lhs_copy(2 * piece + side, sources[k], at).start()
        for piece in range(8):
            rhs_copy(piece).wait()

    for part in range(16):
        lhs_copy(part, own[0], tile).wait()
    out[...] = jnp.dot(
        lhs[pl.ds(pl.multiple_of(tile * TILE, TILE), TILE), :], rhs[...],
        preferred_element_type=jnp.float32,
    )[:, :750]


def multiply(which, own, other, columns):
    return pl.pallas_call(
        multiply_kernel,
        grid=(ROWS // TILE,),
        out_shape=jax.ShapeDtypeStruct((1500, 750), jnp.float32),
        in_specs=[pl.BlockSpec(memory_space=pltpu.SMEM)] + [pl.BlockSpec(memory_space=pl.ANY)] * 24,
        out_specs=pl.BlockSpec((TILE, 750), lambda i: (i, 0)),
        scratch_shapes=[
            pltpu.VMEM((ROWS, 16 * PART), jnp.bfloat16),
            pltpu.VMEM((16 * PART, COLS), jnp.bfloat16),
            pltpu.SemaphoreType.DMA((16, ROWS // TILE)),
            pltpu.SemaphoreType.DMA((8,)),
        ],
        compiler_params=pltpu.CompilerParams(vmem_limit_bytes=48 << 20),
        cost_estimate=pl.CostEstimate(
            flops=2 * 1500 * 750 * 6144, bytes_accessed=33 << 20, transcendentals=0
        ),
    )(which, *own, *other, *columns)


def ring(block, pairs, steps=3):
    out = [block]
    for _ in range(steps):
        out.append(send(out[-1], pairs))
    return out


def body(half_slabs):
    xl, y, xh, z, d = (lax.axis_index(a) for a in AXES)
    rows = jnp.transpose(half_slabs, (1, 0, 2)).reshape(1500, PART)
    rows = jnp.pad(rows, ((0, ROWS - 1500), (0, 0)))
    turned = jnp.transpose(half_slabs, (0, 2, 1)).reshape(PART, 1500)
    low = jnp.pad(turned[:, :750], ((0, 0), (0, COLS - 750)))
    high = jnp.pad(turned[:, 750:], ((0, 0), (0, COLS - 750)))
    keep = jnp.where(d == 0, low, high)
    give = jnp.where(d == 0, high, low)

    near = jnp.concatenate([send(keep, turn(False)), send(give, turn(True))], axis=0)
    far = send(near, X_NEAR)
    columns = ring(near, Y_RING) + ring(far, Y_RING)
    own = ring(rows, Z_RING) + ring(send(rows, X_FAR), Z_RING)
    other = [send(block, CORES) for block in own]

    gamma = jnp.where(d == 0, GAMMA[0], GAMMA[1])
    way = 1 - 2 * d
    which = []
    for half in range(2):
        high_orbital = xl ^ d ^ half
        for step in range(4):
            orbital = gamma - y - z + way * step
            for side in range(2):
                way_of_rows = way if side == 0 else -way
                which.append(4 * (high_orbital ^ xh) + (way_of_rows * (z - orbital)) % 4)
    which = jnp.stack(which).astype(jnp.int32)
    return multiply(which, own, other, columns)


def solution(mesh):
    fine = Mesh(mesh.devices.reshape(SIZES), AXES)
    return jax.shard_map(
        body,
        mesh=fine,
        in_specs=P("d", ("xl", "y"), ("xh", "z")),
        out_specs=P(("xl", "y"), ("xh", "z", "d")),
        check_vma=False,
    )
```

time: 481 us -> 174 us (0.36)
  waiting for transfers between devices: 427 us -> 102 us
  starting transfers between devices: 0.08 us -> 39.6 us
  Pallas kernels: 0 us -> 22.7 us
  matrix products: 20.9 us -> 0 us
  between operations: 13.1 us -> 0.31 us
  other arithmetic: 13.8 us -> 1.31 us
    all_gather x2 -> x0, waiting for transfers between devices: 224 us -> none  [the longest x1 205 us: body(): mine_rows = lax.all_gather(window_part, 'col', axis=2, tiled=True)]
    psum x1 -> x0, waiting for transfers between devices: 202 us -> none  [spread(): return lax.psum(block, axis)]
    ppermute x0 -> x24, waiting for transfers between devices: none -> 102 us  [send(): return lax.ppermute(block, AXES, pairs)]
    ppermute x0 -> x24, starting transfers between devices: none -> 39.6 us  [send(): return lax.ppermute(block, AXES, pairs)]
    pallas_call x0 -> x1, Pallas kernels: none -> 22.7 us  [multiply(): pl.pallas_call(multiply_kernel, grid=(ROWS // TILE,), out_shape=jax.Shape...]
    dot_general x1 -> x0, matrix products: 20.9 us -> none  [body(): jnp.einsum('qmi,qni->mn', mine_rows, partner_rows, preferred_element_type...]
    select_n x1, other arithmetic: 13.8 us -> 1.31 us  [body(): give = jnp.where(d == 0, high, low)]
    dot_general x1 -> x0, local copies, waits for them, and re-layouts: 5.99 us -> none  [body(): jnp.einsum('qmi,qni->mn', mine_rows, partner_rows, preferred_element_type...]
  transfers between devices with their start and end apart: 3 -> 24, of which waited for: 3 -> 11; matrix products, arithmetic and copies ran while one was open for 0% -> 1% of each run, Pallas kernels for 0% -> 0%
where the time goes in v1:
time: 174 us; the launch traced here: 172 us
  waiting for transfers between devices  102 us (59%)
  starting transfers between devices  39.6 us (23%)
  Pallas kernels  22.7 us (13%)
  local copies, waits for them, and re-layouts  5.99 us (3%)
    ppermute x24, waiting for transfers between devices, send(): return lax.ppermute(block, AXES, pairs)  102 us
    ppermute x24, starting transfers between devices, send(): return lax.ppermute(block, AXES, pairs)  39.6 us
    pallas_call x1, Pallas kernels, multiply(): pl.pallas_call(multiply_kernel, grid=(ROWS // TILE,), out_shape=jax.Shape...  22.7 us
  transfers between devices with their start and end apart: 24, of which 11 were waited for; matrix products, arithmetic and copies ran while one was open for 1% of the time, Pallas kernels for 0%

profile of v1, /device:TPU:1, one launch (start us, length us, event | category | flops | bytes accessed | tf_op | source)
XLA Modules:
  0.0 172.0 jit_solution(11941846952012831770)
XLA Ops:
  0.0 2.3 %copy.3 = bf16[1500,384]{1,0:T(8,128)(2,1)S(1)} copy(bf16[1500,384]{0,1:T(8,128)(2,1)} %bitcast.22) | data formatting | bytes 2304000 | tf_op jit(solution)/shard_map/reshape | solution.py:114
  2.5 3.7 %collective-permute-start.3 = (bf16[1536,384]{1,0:T(8,128)(2,1)S(1)}, bf16[1536,384]{1,0:T(8,128)(2,1)S(1)}, u32[]{:S(2)}, u32[]{:S(2)}) collective-permute-start(bf16[1536,384]{1,0:T(8,128)(2,1)S(1)} %pad.11.refs_0_), channel_id=1, source_target_pairs={{0,8},{1,9},{2,10},{3,11},{4,12},{5,13},{6,14},{7,15},{8,0},{9,1},... | collective-permute-start | bytes 3538952 | tf_op jit(solution)/shard_map/ppermute | solution.py:43
  6.1 1.0 collective-permute-start.7
  7.1 1.1 slice.10
  8.2 1.3 broadcast_select_fusion
  9.5 4.9 %collective-permute-start.15 = (bf16[384,768]{1,0:T(8,128)(2,1)S(1)}, bf16[384,768]{1,0:T(8,128)(2,1)S(1)}, u32[]{:S(2)}, u32[]{:S(2)}) collective-permute-start(bf16[384,768]{1,0:T(8,128)(2,1)S(1)} %get-tuple-element.6), channel_id=1, source_target_pairs={{0,0},{1,97},{2,48},{3,81},{4,32},{5,65},{6,16},{7,113},{8,64},{9,... | collective-permute-start | bytes 1769480 | tf_op jit(solution)/shard_map/ppermute | solution.py:43
  14.4 4.3 %collective-permute-start = (bf16[1536,384]{1,0:T(8,128)(2,1)S(1)}, bf16[1536,384]{1,0:T(8,128)(2,1)S(1)}, u32[]{:S(2)}, u32[]{:S(2)}) collective-permute-start(bf16[1536,384]{1,0:T(8,128)(2,1)S(1)} %pad.11.refs_0_), channel_id=1, source_target_pairs={{0,2},{1,7},{2,4},{3,1},{4,6},{5,3},{6,0},{7,5},{8,10},{9,15},{10,... | collective-permute-start | bytes 3538952 | tf_op jit(solution)/shard_map/ppermute | solution.py:43
  18.7 28.8 %collective-permute-done.15 = bf16[384,768]{1,0:T(8,128)(2,1)S(1)} collective-permute-done((bf16[384,768]{1,0:T(8,128)(2,1)S(1)}, bf16[384,768]{1,0:T(8,128)(2,1)S(1)}, u32[]{:S(2)}, u32[]{:S(2)}) %collective-permute-start.15) | collective-permute-done | bytes 589856 | tf_op jit(solution)/shard_map/ppermute | solution.py:43
  47.5 1.1 collective-permute-done.16
  48.7 1.3 collective-permute-start.20
  49.9 2.6 %collective-permute-start.17 = (bf16[768,768]{1,0:T(8,128)(2,1)S(1)}, bf16[768,768]{1,0:T(8,128)(2,1)S(1)}, u32[]{:S(2)}, u32[]{:S(2)}) collective-permute-start(bf16[768,768]{1,0:T(8,128)(2,1)S(1)} %constant_dynamic-update-slice_fusion.refs_16_), channel_id=1, source_target_pairs={{0,16},{1,49},{2,18},{3,51},{4,20},{5,53},{6,22},{7,55},{8,24},{9,... | collective-permute-start | bytes 3538952 | tf_op jit(solution)/shard_map/ppermute | solution.py:43
  52.5 1.2 collective-permute-start.4
  53.8 19.8 %collective-permute-done.20.refs_20_ = bf16[768,768]{1,0:T(8,128)(2,1)S(1)} collective-permute-done((bf16[768,768]{1,0:T(8,128)(2,1)S(1)}, bf16[768,768]{1,0:T(8,128)(2,1)S(1)}, u32[]{:S(2)}, u32[]{:S(2)}) %collective-permute-start.20) | collective-permute-done | bytes 1179680 | tf_op jit(solution)/shard_map/ppermute | solution.py:43
  73.7 5.4 %collective-permute-start.1 = (bf16[1536,384]{1,0:T(8,128)(2,1)S(1)}, bf16[1536,384]{1,0:T(8,128)(2,1)S(1)}, u32[]{:S(2)}, u32[]{:S(2)}) collective-permute-start(bf16[1536,384]{1,0:T(8,128)(2,1)S(1)} %collective-permute-done.refs_1_), channel_id=1, source_target_pairs={{0,2},{1,7},{2,4},{3,1},{4,6},{5,3},{6,0},{7,5},{8,10},{9,15},{10,... | collective-permute-start | bytes 3538952 | tf_op jit(solution)/shard_map/ppermute | solution.py:43
  79.1 1.3 collective-permute-start.18
  80.7 11.5 %collective-permute-done.1.refs_2_ = bf16[1536,384]{1,0:T(8,128)(2,1)S(1)} collective-permute-done((bf16[1536,384]{1,0:T(8,128)(2,1)S(1)}, bf16[1536,384]{1,0:T(8,128)(2,1)S(1)}, u32[]{:S(2)}, u32[]{:S(2)}) %collective-permute-start.1) | collective-permute-done | bytes 1179680 | tf_op jit(solution)/shard_map/ppermute | solution.py:43
  92.2 2.2 %collective-permute-start.9 = (bf16[1536,384]{1,0:T(8,128)(2,1)S(1)}, bf16[1536,384]{1,0:T(8,128)(2,1)S(1)}, u32[]{:S(2)}, u32[]{:S(2)}) collective-permute-start(bf16[1536,384]{1,0:T(8,128)(2,1)S(1)} %collective-permute-done.1.refs_2_), channel_id=1, source_target_pairs={{0,1},{1,0},{2,3},{3,2},{4,5},{5,4},{6,7},{7,6},{8,9},{9,8},{10,11... | collective-permute-start | bytes 3538952 | tf_op jit(solution)/shard_map/ppermute | solution.py:43
  94.5 1.7 collective-permute-start.2
  96.2 1.0 copy-done
  97.2 10.0 %collective-permute-done.18.refs_18_ = bf16[768,768]{1,0:T(8,128)(2,1)} collective-permute-done((bf16[768,768]{1,0:T(8,128)(2,1)S(1)}, bf16[768,768]{1,0:T(8,128)(2,1)}, u32[]{:S(2)}, u32[]{:S(2)}) %collective-permute-start.18) | collective-permute-done | bytes 1179680 | tf_op jit(solution)/shard_map/ppermute | solution.py:43
  107.2 1.2 collective-permute-start.22
  108.6 1.1 collective-permute-start.13
  109.7 7.8 %collective-permute-done.2.refs_3_ = bf16[1536,384]{1,0:T(8,128)(2,1)} collective-permute-done((bf16[1536,384]{1,0:T(8,128)(2,1)S(1)}, bf16[1536,384]{1,0:T(8,128)(2,1)}, u32[]{:S(2)}, u32[]{:S(2)}) %collective-permute-start.2) | collective-permute-done | bytes 1179680 | tf_op jit(solution)/shard_map/ppermute | solution.py:43
  117.5 2.3 %collective-permute-start.10 = (bf16[1536,384]{1,0:T(8,128)(2,1)}, bf16[1536,384]{1,0:T(8,128)(2,1)}, u32[]{:S(2)}, u32[]{:S(2)}) collective-permute-start(bf16[1536,384]{1,0:T(8,128)(2,1)} %collective-permute-done.2.refs_3_), channel_id=1, source_target_pairs={{0,1},{1,0},{2,3},{3,2},{4,5},{5,4},{6,7},{7,6},{8,9},{9,8},{10,11... | collective-permute-start | bytes 3538952 | tf_op jit(solution)/shard_map/ppermute | solution.py:43
  119.8 2.8 %collective-permute-done.22.refs_22_ = bf16[768,768]{1,0:T(8,128)(2,1)} collective-permute-done((bf16[768,768]{1,0:T(8,128)(2,1)S(1)}, bf16[768,768]{1,0:T(8,128)(2,1)}, u32[]{:S(2)}, u32[]{:S(2)}) %collective-permute-start.22) | collective-permute-done | bytes 1179680 | tf_op jit(solution)/shard_map/ppermute | solution.py:43
  122.6 2.4 %collective-permute-start.23 = (bf16[768,768]{1,0:T(8,128)(2,1)}, bf16[768,768]{1,0:T(8,128)(2,1)}, u32[]{:S(2)}, u32[]{:S(2)}) collective-permute-start(bf16[768,768]{1,0:T(8,128)(2,1)} %collective-permute-done.22.refs_22_), channel_id=1, source_target_pairs={{0,16},{1,49},{2,18},{3,51},{4,20},{5,53},{6,22},{7,55},{8,24},{9,... | collective-permute-start | bytes 3538952 | tf_op jit(solution)/shard_map/ppermute | solution.py:43
  125.0 5.2 %collective-permute-done.6.refs_7_ = bf16[1536,384]{1,0:T(8,128)(2,1)} collective-permute-done((bf16[1536,384]{1,0:T(8,128)(2,1)}, bf16[1536,384]{1,0:T(8,128)(2,1)}, u32[]{:S(2)}, u32[]{:S(2)}) %collective-permute-start.6) | collective-permute-done | bytes 1179680 | tf_op jit(solution)/shard_map/ppermute | solution.py:43
  130.3 2.5 %collective-permute-start.14 = (bf16[1536,384]{1,0:T(8,128)(2,1)}, bf16[1536,384]{1,0:T(8,128)(2,1)}, u32[]{:S(2)}, u32[]{:S(2)}) collective-permute-start(bf16[1536,384]{1,0:T(8,128)(2,1)} %collective-permute-done.6.refs_7_), channel_id=1, source_target_pairs={{0,1},{1,0},{2,3},{3,2},{4,5},{5,4},{6,7},{7,6},{8,9},{9,8},{10,11... | collective-permute-start | bytes 3538952 | tf_op jit(solution)/shard_map/ppermute | solution.py:43
  132.8 2.4 %collective-permute-done.19.refs_19_ = bf16[768,768]{1,0:T(8,128)(2,1)} collective-permute-done((bf16[768,768]{1,0:T(8,128)(2,1)}, bf16[768,768]{1,0:T(8,128)(2,1)}, u32[]{:S(2)}, u32[]{:S(2)}) %collective-permute-start.19) | collective-permute-done | bytes 1179680 | tf_op jit(solution)/shard_map/ppermute | solution.py:43
  135.3 12.6 %collective-permute-done.23.refs_23_ = bf16[768,768]{1,0:T(8,128)(2,1)} collective-permute-done((bf16[768,768]{1,0:T(8,128)(2,1)}, bf16[768,768]{1,0:T(8,128)(2,1)}, u32[]{:S(2)}, u32[]{:S(2)}) %collective-permute-start.23) | collective-permute-done | bytes 1179680 | tf_op jit(solution)/shard_map/ppermute | solution.py:43
  147.9 1.3 copy-done.1
  149.2 22.7 %shard_map.17 = f32[1500,750]{1,0:T(8,128)} custom-call(s32[16]{0:T(128)S(1)} %stack.67.which, bf16[1536,384]{1,0:T(8,128)(2,1)S(1)} %pad.11.refs_0_, bf16[1536,384]{1,0:T(8,128)(2,1)S(1)} %collective-permute-done.refs_1_, bf16[1536,384]{1,0:T(8,128)(2,1)S(1)} %copy-done.1, bf16[1536,384]{1,0:T(8,128)(2,1)} %collective-permute-done.2.refs_3_, ...), custom_call_target="tpu_custom_call" | custom-call | flops 13824000000 | bytes 34603008 | tf_op jit(solution)/shard_map/pallas_call | solution.py:86
  (50 shorter events, 1.1 us)
Async XLA Ops:
  2.5 50.0 %collective-permute-start.3 = (bf16[1536,384]{1,0:T(8,128)(2,1)S(1)}, bf16[1536,384]{1,0:T(8,128)(2,1)S(1)}, u32[]{:S(2)}, u32[]{:S(2)}) collective-permute-start(bf16[1536,384]{1,0:T(8,128)(2,1)S(1)} %pad.11.refs_0_), channel_id=1, source_target_pairs={{0,8},{1,9},{2,10},{3,11},{4,12},{5,13},{6,14},{7,15},{8,0},{9,1},... | collective-permute-start | bytes 3538952 | tf_op jit(solution)/shard_map/ppermute | solution.py:43
  6.1 46.4 %collective-permute-start.7 = (bf16[1536,384]{1,0:T(8,128)(2,1)S(1)}, bf16[1536,384]{1,0:T(8,128)(2,1)}, u32[]{:S(2)}, u32[]{:S(2)}) collective-permute-start(bf16[1536,384]{1,0:T(8,128)(2,1)S(1)} %pad.11.refs_0_), channel_id=1, source_target_pairs={{0,1},{1,0},{2,3},{3,2},{4,5},{5,4},{6,7},{7,6},{8,9},{9,8},{10,11... | collective-permute-start | bytes 3538952 | tf_op jit(solution)/shard_map/ppermute | solution.py:43
  9.5 38.0 %collective-permute-start.15 = (bf16[384,768]{1,0:T(8,128)(2,1)S(1)}, bf16[384,768]{1,0:T(8,128)(2,1)S(1)}, u32[]{:S(2)}, u32[]{:S(2)}) collective-permute-start(bf16[384,768]{1,0:T(8,128)(2,1)S(1)} %get-tuple-element.6), channel_id=1, source_target_pairs={{0,0},{1,97},{2,48},{3,81},{4,32},{5,65},{6,16},{7,113},{8,64},{9,... | collective-permute-start | bytes 1769480 | tf_op jit(solution)/shard_map/ppermute | solution.py:43
  14.3 34.3 %collective-permute-start.16 = (bf16[384,768]{1,0:T(8,128)(2,1)S(1)}, bf16[384,768]{1,0:T(8,128)(2,1)S(1)}, u32[]{:S(2)}, u32[]{:S(2)}) collective-permute-start(bf16[384,768]{1,0:T(8,128)(2,1)S(1)} %get-tuple-element.5), channel_id=1, source_target_pairs={{0,97},{1,0},{2,81},{3,48},{4,65},{5,32},{6,113},{7,16},{8,33},{9,... | collective-permute-start | bytes 1769480 | tf_op jit(solution)/shard_map/ppermute | solution.py:43
  14.4 39.3 %collective-permute-start = (bf16[1536,384]{1,0:T(8,128)(2,1)S(1)}, bf16[1536,384]{1,0:T(8,128)(2,1)S(1)}, u32[]{:S(2)}, u32[]{:S(2)}) collective-permute-start(bf16[1536,384]{1,0:T(8,128)(2,1)S(1)} %pad.11.refs_0_), channel_id=1, source_target_pairs={{0,2},{1,7},{2,4},{3,1},{4,6},{5,3},{6,0},{7,5},{8,10},{9,15},{10,... | collective-permute-start | bytes 3538952 | tf_op jit(solution)/shard_map/ppermute | solution.py:43
  48.7 68.8 %copy-start.3 = (bf16[768,768]{1,0:T(8,128)(2,1)}, bf16[768,768]{1,0:T(8,128)(2,1)S(1)}, u32[]{:S(2)}) copy-start(bf16[768,768]{1,0:T(8,128)(2,1)S(1)} %constant_dynamic-update-slice_fusion.refs_16_) | copy-start | bytes 3538948
  48.7 25.0 %collective-permute-start.20 = (bf16[768,768]{1,0:T(8,128)(2,1)S(1)}, bf16[768,768]{1,0:T(8,128)(2,1)S(1)}, u32[]{:S(2)}, u32[]{:S(2)}) collective-permute-start(bf16[768,768]{1,0:T(8,128)(2,1)S(1)} %constant_dynamic-update-slice_fusion.refs_16_), channel_id=1, source_target_pairs={{0,64},{1,65},{2,66},{3,67},{4,68},{5,69},{6,70},{7,71},{8,72},{9,... | collective-permute-start | bytes 3538952 | tf_op jit(solution)/shard_map/ppermute | solution.py:43
  49.9 29.1 %collective-permute-start.17 = (bf16[768,768]{1,0:T(8,128)(2,1)S(1)}, bf16[768,768]{1,0:T(8,128)(2,1)S(1)}, u32[]{:S(2)}, u32[]{:S(2)}) collective-permute-start(bf16[768,768]{1,0:T(8,128)(2,1)S(1)} %constant_dynamic-update-slice_fusion.refs_16_), channel_id=1, source_target_pairs={{0,16},{1,49},{2,18},{3,51},{4,20},{5,53},{6,22},{7,55},{8,24},{9,... | collective-permute-start | bytes 3538952 | tf_op jit(solution)/shard_map/ppermute | solution.py:43
  52.5 26.6 %collective-permute-start.11 = (bf16[1536,384]{1,0:T(8,128)(2,1)S(1)}, bf16[1536,384]{1,0:T(8,128)(2,1)S(1)}, u32[]{:S(2)}, u32[]{:S(2)}) collective-permute-start(bf16[1536,384]{1,0:T(8,128)(2,1)S(1)} %collective-permute-done.3.refs_4_), channel_id=1, source_target_pairs={{0,1},{1,0},{2,3},{3,2},{4,5},{5,4},{6,7},{7,6},{8,9},{9,8},{10,11... | collective-permute-start | bytes 3538952 | tf_op jit(solution)/shard_map/ppermute | solution.py:43
  52.5 27.9 %collective-permute-start.4 = (bf16[1536,384]{1,0:T(8,128)(2,1)S(1)}, bf16[1536,384]{1,0:T(8,128)(2,1)S(1)}, u32[]{:S(2)}, u32[]{:S(2)}) collective-permute-start(bf16[1536,384]{1,0:T(8,128)(2,1)S(1)} %collective-permute-done.3.refs_4_), channel_id=1, source_target_pairs={{0,2},{1,7},{2,4},{3,1},{4,6},{5,3},{6,0},{7,5},{8,10},{9,15},{10,... | collective-permute-start | bytes 3538952 | tf_op jit(solution)/shard_map/ppermute | solution.py:43
  53.7 26.8 %collective-permute-start.8 = (bf16[1536,384]{1,0:T(8,128)(2,1)S(1)}, bf16[1536,384]{1,0:T(8,128)(2,1)S(1)}, u32[]{:S(2)}, u32[]{:S(2)}) collective-permute-start(bf16[1536,384]{1,0:T(8,128)(2,1)S(1)} %collective-permute-done.refs_1_), channel_id=1, source_target_pairs={{0,1},{1,0},{2,3},{3,2},{4,5},{5,4},{6,7},{7,6},{8,9},{9,8},{10,11... | collective-permute-start | bytes 3538952 | tf_op jit(solution)/shard_map/ppermute | solution.py:43
  73.7 46.2 %copy-start.5 = (bf16[768,768]{1,0:T(8,128)(2,1)}, bf16[768,768]{1,0:T(8,128)(2,1)S(1)}, u32[]{:S(2)}) copy-start(bf16[768,768]{1,0:T(8,128)(2,1)S(1)} %collective-permute-done.20.refs_20_) | copy-start | bytes 3538948
  73.7 18.6 %collective-permute-start.1 = (bf16[1536,384]{1,0:T(8,128)(2,1)S(1)}, bf16[1536,384]{1,0:T(8,128)(2,1)S(1)}, u32[]{:S(2)}, u32[]{:S(2)}) collective-permute-start(bf16[1536,384]{1,0:T(8,128)(2,1)S(1)} %collective-permute-done.refs_1_), channel_id=1, source_target_pairs={{0,2},{1,7},{2,4},{3,1},{4,6},{5,3},{6,0},{7,5},{8,10},{9,15},{10,... | collective-permute-start | bytes 3538952 | tf_op jit(solution)/shard_map/ppermute | solution.py:43
  79.1 43.6 %copy-start.6 = (bf16[768,768]{1,0:T(8,128)(2,1)}, bf16[768,768]{1,0:T(8,128)(2,1)S(1)}, u32[]{:S(2)}) copy-start(bf16[768,768]{1,0:T(8,128)(2,1)S(1)} %collective-permute-done.17.refs_17_) | copy-start | bytes 3538948
  79.1 15.5 %collective-permute-start.21 = (bf16[768,768]{1,0:T(8,128)(2,1)S(1)}, bf16[768,768]{1,0:T(8,128)(2,1)S(1)}, u32[]{:S(2)}, u32[]{:S(2)}) collective-permute-start(bf16[768,768]{1,0:T(8,128)(2,1)S(1)} %collective-permute-done.20.refs_20_), channel_id=1, source_target_pairs={{0,16},{1,49},{2,18},{3,51},{4,20},{5,53},{6,22},{7,55},{8,24},{9,... | collective-permute-start | bytes 3538952 | tf_op jit(solution)/shard_map/ppermute | solution.py:43
  79.1 46.0 %copy-start.7 = (bf16[1536,384]{1,0:T(8,128)(2,1)}, bf16[1536,384]{1,0:T(8,128)(2,1)S(1)}, u32[]{:S(2)}) copy-start(bf16[1536,384]{1,0:T(8,128)(2,1)S(1)} %collective-permute-done.11.refs_12_) | copy-start | bytes 3538948
  79.1 28.1 %collective-permute-start.18 = (bf16[768,768]{1,0:T(8,128)(2,1)S(1)}, bf16[768,768]{1,0:T(8,128)(2,1)}, u32[]{:S(2)}, u32[]{:S(2)}) collective-permute-start(bf16[768,768]{1,0:T(8,128)(2,1)S(1)} %collective-permute-done.17.refs_17_), channel_id=1, source_target_pairs={{0,16},{1,49},{2,18},{3,51},{4,20},{5,53},{6,22},{7,55},{8,24},{9,... | collective-permute-start | bytes 3538952 | tf_op jit(solution)/shard_map/ppermute | solution.py:43
  80.4 49.8 %copy-start.8 = (bf16[1536,384]{1,0:T(8,128)(2,1)}, bf16[1536,384]{1,0:T(8,128)(2,1)S(1)}, u32[]{:S(2)}) copy-start(bf16[1536,384]{1,0:T(8,128)(2,1)S(1)} %collective-permute-done.4.refs_5_) | copy-start | bytes 3538948
  80.4 28.0 %collective-permute-start.5 = (bf16[1536,384]{1,0:T(8,128)(2,1)S(1)}, bf16[1536,384]{1,0:T(8,128)(2,1)}, u32[]{:S(2)}, u32[]{:S(2)}) collective-permute-start(bf16[1536,384]{1,0:T(8,128)(2,1)S(1)} %collective-permute-done.4.refs_5_), channel_id=1, source_target_pairs={{0,2},{1,7},{2,4},{3,1},{4,6},{5,3},{6,0},{7,5},{8,10},{9,15},{10,... | collective-permute-start | bytes 3538952 | tf_op jit(solution)/shard_map/ppermute | solution.py:43
  80.5 49.7 %copy-start.9 = (bf16[1536,384]{1,0:T(8,128)(2,1)}, bf16[1536,384]{1,0:T(8,128)(2,1)S(1)}, u32[]{:S(2)}) copy-start(bf16[1536,384]{1,0:T(8,128)(2,1)S(1)} %collective-permute-done.8.refs_9_) | copy-start | bytes 3538948
  80.5 27.9 %collective-permute-start.12 = (bf16[1536,384]{1,0:T(8,128)(2,1)S(1)}, bf16[1536,384]{1,0:T(8,128)(2,1)S(1)}, u32[]{:S(2)}, u32[]{:S(2)}) collective-permute-start(bf16[1536,384]{1,0:T(8,128)(2,1)S(1)} %collective-permute-done.4.refs_5_), channel_id=1, source_target_pairs={{0,1},{1,0},{2,3},{3,2},{4,5},{5,4},{6,7},{7,6},{8,9},{9,8},{10,11... | collective-permute-start | bytes 3538952 | tf_op jit(solution)/shard_map/ppermute | solution.py:43
  92.2 16.4 %collective-permute-start.9 = (bf16[1536,384]{1,0:T(8,128)(2,1)S(1)}, bf16[1536,384]{1,0:T(8,128)(2,1)S(1)}, u32[]{:S(2)}, u32[]{:S(2)}) collective-permute-start(bf16[1536,384]{1,0:T(8,128)(2,1)S(1)} %collective-permute-done.1.refs_2_), channel_id=1, source_target_pairs={{0,1},{1,0},{2,3},{3,2},{4,5},{5,4},{6,7},{7,6},{8,9},{9,8},{10,11... | collective-permute-start | bytes 3538952 | tf_op jit(solution)/shard_map/ppermute | solution.py:43
  94.5 35.7 %copy-start.10 = (bf16[768,768]{1,0:T(8,128)(2,1)}, bf16[768,768]{1,0:T(8,128)(2,1)S(1)}, u32[]{:S(2)}) copy-start(bf16[768,768]{1,0:T(8,128)(2,1)S(1)} %collective-permute-done.21.refs_21_) | copy-start | bytes 3538948
  94.5 23.0 %collective-permute-start.2 = (bf16[1536,384]{1,0:T(8,128)(2,1)S(1)}, bf16[1536,384]{1,0:T(8,128)(2,1)}, u32[]{:S(2)}, u32[]{:S(2)}) collective-permute-start(bf16[1536,384]{1,0:T(8,128)(2,1)S(1)} %collective-permute-done.1.refs_2_), channel_id=1, source_target_pairs={{0,2},{1,7},{2,4},{3,1},{4,6},{5,3},{6,0},{7,5},{8,10},{9,15},{10,... | collective-permute-start | bytes 3538952 | tf_op jit(solution)/shard_map/ppermute | solution.py:43
  107.2 15.5 %collective-permute-start.22 = (bf16[768,768]{1,0:T(8,128)(2,1)S(1)}, bf16[768,768]{1,0:T(8,128)(2,1)}, u32[]{:S(2)}, u32[]{:S(2)}) collective-permute-start(bf16[768,768]{1,0:T(8,128)(2,1)S(1)} %collective-permute-done.21.refs_21_), channel_id=1, source_target_pairs={{0,16},{1,49},{2,18},{3,51},{4,20},{5,53},{6,22},{7,55},{8,24},{9,... | collective-permute-start | bytes 3538952 | tf_op jit(solution)/shard_map/ppermute | solution.py:43
  108.4 21.9 %collective-permute-start.6 = (bf16[1536,384]{1,0:T(8,128)(2,1)}, bf16[1536,384]{1,0:T(8,128)(2,1)}, u32[]{:S(2)}, u32[]{:S(2)}) collective-permute-start(bf16[1536,384]{1,0:T(8,128)(2,1)} %collective-permute-done.5.refs_6_), channel_id=1, source_target_pairs={{0,2},{1,7},{2,4},{3,1},{4,6},{5,3},{6,0},{7,5},{8,10},{9,15},{10,... | collective-permute-start | bytes 3538952 | tf_op jit(solution)/shard_map/ppermute | solution.py:43
  108.4 21.9 %copy-start.11 = (bf16[1536,384]{1,0:T(8,128)(2,1)}, bf16[1536,384]{1,0:T(8,128)(2,1)S(1)}, u32[]{:S(2)}) copy-start(bf16[1536,384]{1,0:T(8,128)(2,1)S(1)} %collective-permute-done.12.refs_13_) | copy-start | bytes 3538948
  108.4 26.9 %collective-permute-start.19 = (bf16[768,768]{1,0:T(8,128)(2,1)}, bf16[768,768]{1,0:T(8,128)(2,1)}, u32[]{:S(2)}, u32[]{:S(2)}) collective-permute-start(bf16[768,768]{1,0:T(8,128)(2,1)} %collective-permute-done.18.refs_18_), channel_id=1, source_target_pairs={{0,16},{1,49},{2,18},{3,51},{4,20},{5,53},{6,22},{7,55},{8,24},{9,... | collective-permute-start | bytes 3538952 | tf_op jit(solution)/shard_map/ppermute | solution.py:43
  108.6 26.7 %collective-permute-start.13 = (bf16[1536,384]{1,0:T(8,128)(2,1)}, bf16[1536,384]{1,0:T(8,128)(2,1)}, u32[]{:S(2)}, u32[]{:S(2)}) collective-permute-start(bf16[1536,384]{1,0:T(8,128)(2,1)} %collective-permute-done.5.refs_6_), channel_id=1, source_target_pairs={{0,1},{1,0},{2,3},{3,2},{4,5},{5,4},{6,7},{7,6},{8,9},{9,8},{10,11... | collective-permute-start | bytes 3538952 | tf_op jit(solution)/shard_map/ppermute | solution.py:43
  117.5 17.8 %collective-permute-start.10 = (bf16[1536,384]{1,0:T(8,128)(2,1)}, bf16[1536,384]{1,0:T(8,128)(2,1)}, u32[]{:S(2)}, u32[]{:S(2)}) collective-permute-start(bf16[1536,384]{1,0:T(8,128)(2,1)} %collective-permute-done.2.refs_3_), channel_id=1, source_target_pairs={{0,1},{1,0},{2,3},{3,2},{4,5},{5,4},{6,7},{7,6},{8,9},{9,8},{10,11... | collective-permute-start | bytes 3538952 | tf_op jit(solution)/shard_map/ppermute | solution.py:43
  122.6 25.3 %collective-permute-start.23 = (bf16[768,768]{1,0:T(8,128)(2,1)}, bf16[768,768]{1,0:T(8,128)(2,1)}, u32[]{:S(2)}, u32[]{:S(2)}) collective-permute-start(bf16[768,768]{1,0:T(8,128)(2,1)} %collective-permute-done.22.refs_22_), channel_id=1, source_target_pairs={{0,16},{1,49},{2,18},{3,51},{4,20},{5,53},{6,22},{7,55},{8,24},{9,... | collective-permute-start | bytes 3538952 | tf_op jit(solution)/shard_map/ppermute | solution.py:43
  130.3 17.6 %collective-permute-start.14 = (bf16[1536,384]{1,0:T(8,128)(2,1)}, bf16[1536,384]{1,0:T(8,128)(2,1)}, u32[]{:S(2)}, u32[]{:S(2)}) collective-permute-start(bf16[1536,384]{1,0:T(8,128)(2,1)} %collective-permute-done.6.refs_7_), channel_id=1, source_target_pairs={{0,1},{1,0},{2,3},{3,2},{4,5},{5,4},{6,7},{7,6},{8,9},{9,8},{10,11... | collective-permute-start | bytes 3538952 | tf_op jit(solution)/shard_map/ppermute | solution.py:43
  (5 other events, 34.5 us)

commit v2 on v1

v2 whole, which is shorter than its diff:
```python
import itertools

import jax
import jax.numpy as jnp
import numpy as np
from jax import lax
from jax.experimental import pallas as pl
from jax.experimental.pallas import tpu as pltpu
from jax.sharding import Mesh
from jax.sharding import PartitionSpec as P

AXES = ("xl", "y", "xh", "z", "d")
SIZES = (2, 4, 2, 4, 2)
GAMMA = (0, 2)
ROWS, COLS, PART = 1536, 768, 384
TILE = 256
COLUMN_STAGE = (0, 0, 1, 0, 0, 1, 2, 1)
ROW_STAGE = ((0, 0, 1, 0, 0, 0, 1, 0), (0, 0, 2, 0, 0, 0, 2, 0))


def perm(target):
    out = []
    for at in itertools.product(*map(range, SIZES)):
        to = target(*at)
        out.append((int(np.ravel_multi_index(at, SIZES)), int(np.ravel_multi_index(to, SIZES))))
    return out


def turn(cross, swap=0):
    def target(xl, y, xh, z, d):
        e = 1 - d if cross else d
        return xh ^ e ^ swap, (GAMMA[e] - y - z) % 4, xl, y, e

    return perm(target)


Z_RING = perm(lambda xl, y, xh, z, d: (xl, y, xh, (z + 1 - 2 * d) % 4, d))
Y_RING = perm(lambda xl, y, xh, z, d: (xl, (y + 1 - 2 * d) % 4, xh, z, d))
Z_BACK = perm(lambda xl, y, xh, z, d: (xl, y, xh, (z - 1 + 2 * d) % 4, d))
Y_BACK = perm(lambda xl, y, xh, z, d: (xl, (y - 1 + 2 * d) % 4, xh, z, d))
X_FAR = perm(lambda xl, y, xh, z, d: (xl, y, 1 - xh, z, d))
X_NEAR = perm(lambda xl, y, xh, z, d: (1 - xl, y, xh, z, d))
CORES = perm(lambda xl, y, xh, z, d: (xl, y, xh, z, 1 - d))


def send(block, pairs):
    return lax.ppermute(block, AXES, pairs)


def multiply_kernel(slots, places, column_places, n_columns, has_total, select, *refs):
    n_rows = 1 + max(place[0] for place in places.values())
    arrays, refs = refs[:n_rows], refs[n_rows:]
    columns, refs = refs[:n_columns], refs[n_columns:]
    total, refs = (refs[0], refs[1:]) if has_total else (None, refs)
    out, lhs, rhs, lhs_sem, rhs_sem = refs
    tile = pl.program_id(0)
    spans = ((0, TILE), (TILE, ROWS - TILE))

    def lhs_copy(slot, place, span):
        start, size = spans[span]
        array, offset = place
        return pltpu.make_async_copy(
            arrays[array].at[pl.ds(offset + start, size)],
            lhs.at[pl.ds(start, size), pl.ds(slot * PART, PART)],
            lhs_sem.at[slot, span],
        )

    def rhs_copy(slot, column):
        return pltpu.make_async_copy(
            columns[column_places[column][0]].at[pl.ds(column_places[column][1] + slots[slot][0] * PART, PART)],
            rhs.at[pl.ds(slot * PART, PART)],
            rhs_sem.at[slot],
        )

    @pl.when(tile == 0)
    def _():
        for span in range(2):
            for slot, (side, row_options, column_options) in enumerate(slots):
                for row in row_options:
                    @pl.when(select[2 * slot] == row)
                    def _():
                        lhs_copy(slot, places[side, row], span).start()
                if span == 0:
                    for column in column_options:
                        @pl.when(select[2 * slot + 1] == column)
                        def _():
                            rhs_copy(slot, column).start()
        for slot, (side, row_options, column_options) in enumerate(slots):
            @pl.when(select[2 * slot] < 0)
            def _():
                lhs[:, slot * PART:(slot + 1) * PART] = jnp.zeros((ROWS, PART), jnp.bfloat16)

    for span in range(2):
        @pl.when(tile == span)
        def _():
            for slot, (side, row_options, column_options) in enumerate(slots):
                if span == 0:
                    rhs_copy(slot, column_options[0]).wait()

                @pl.when(select[2 * slot] >= 0)
                def _():
                    lhs_copy(slot, places[side, row_options[0]], span).wait()

    product = jnp.dot(
        lhs[pl.ds(pl.multiple_of(tile * TILE, TILE), TILE), :], rhs[...],
        preferred_element_type=jnp.float32,
    )[:, :750]
    out[...] = product + total[...] if has_total else product


def multiply(slots, select, places, arrays, column_places, columns, total=None):
    depth = len(slots) * PART
    has_total = total is not None
    block = pl.BlockSpec((TILE, 750), lambda i: (i, 0))
    anywhere = pl.BlockSpec(memory_space=pl.ANY)

    def kernel(*refs):
        multiply_kernel(slots, places, column_places, len(columns), has_total, *refs)

    return pl.pallas_call(
        kernel,
        grid=(ROWS // TILE,),
        out_shape=jax.ShapeDtypeStruct((1500, 750), jnp.float32),
        in_specs=[pl.BlockSpec(memory_space=pltpu.SMEM)]
        + [anywhere] * (len(arrays) + len(columns)) + [block] * has_total,
        out_specs=block,
        scratch_shapes=[
            pltpu.VMEM((ROWS, depth), jnp.bfloat16),
            pltpu.VMEM((depth, COLS), jnp.bfloat16),
            pltpu.SemaphoreType.DMA((len(slots), 2)),
            pltpu.SemaphoreType.DMA((len(slots),)),
        ],
        compiler_params=pltpu.CompilerParams(vmem_limit_bytes=60 << 20),
        cost_estimate=pl.CostEstimate(
            flops=2 * 1500 * 750 * depth,
            bytes_accessed=2 * depth * (ROWS + COLS) + (1 + has_total) * 4 * 1500 * 750,
            transcendentals=0,
        ),
    )(select, *arrays, *columns, *([total] if has_total else []))


def body(half_slabs):
    xl, y, xh, z, d = (lax.axis_index(a) for a in AXES)
    turned = jnp.transpose(half_slabs, (0, 2, 1)).reshape(PART, 1500)
    low = jnp.pad(turned[:, :750], ((0, 0), (0, COLS - 750)))
    high = jnp.pad(turned[:, 750:], ((0, 0), (0, COLS - 750)))
    keep = jnp.where(d == 0, low, high)
    give = jnp.where(d == 0, high, low)
    rows = jnp.transpose(half_slabs, (1, 0, 2)).reshape(1500, PART)
    rows = jnp.pad(rows, ((0, ROWS - 1500), (0, 0)))

    gamma = jnp.where(d == 0, GAMMA[0], GAMMA[1])
    way = 1 - 2 * d

    def row_of(side, column):
        half, step = divmod(column, 4)
        orbital = gamma - z - (y - step * way if half == 0 else y - step * way)
        way_of_rows = way if side == 0 else -way
        return 4 * (xl ^ d ^ half ^ xh) + (way_of_rows * (z - orbital)) % 4

    places = {
        (0, 0): (0, 0), (0, 1): (1, 0), (0, 2): (6, 0), (0, 3): (2, 0),
        (0, 4): (3, 0), (0, 5): (4, 0), (0, 6): (6, ROWS), (0, 7): (5, 0),
        (1, 0): (7, 0), (1, 1): (8, 0), (1, 2): (11, 0), (1, 3): (8, ROWS),
        (1, 4): (9, 0), (1, 5): (9, ROWS), (1, 6): (11, ROWS), (1, 7): (10, 0),
    }
    column_places = [(0, 0), (1, 0), (4, 2 * PART), (2, 0), (3, 0), (4, 0), (6, 0), (5, 0)]

    def add_up(stage, arrays, columns, total=None):
        slots, select = [], []
        for side in range(2):
            for column in range(8):
                if COLUMN_STAGE[column] != stage:
                    continue
                row = row_of(side, column)
                for r in range(8):
                    if ROW_STAGE[side][r] > stage:
                        row = jnp.where(row == r, -1, row)
                slots.append((side, tuple(r for r in range(8) if ROW_STAGE[side][r] <= stage), (column,)))
                select += [row, column]
            for row in range(8):
                options = tuple(c for c in range(8) if COLUMN_STAGE[c] < stage)
                if ROW_STAGE[side][row] != stage or not options:
                    continue
                column, here = options[0], -1
                for c in options:
                    meets = row_of(side, c) == row
                    column, here = jnp.where(meets, c, column), jnp.where(meets, row, here)
                slots.append((side, (row,), options))
                select += [here, column]
        place = {
            key: at for key, at in places.items() if ROW_STAGE[key[0]][key[1]] <= stage
        }
        column_place = {
            c: at for c, at in enumerate(column_places) if COLUMN_STAGE[c] <= stage
        }
        kept = sorted({at[0] for at in place.values()})
        kept_columns = sorted({at[0] for at in column_place.values()})
        return multiply(
            slots,
            jnp.stack([jnp.asarray(v, jnp.int32) for v in select]),
            {key: (kept.index(at[0]), at[1]) for key, at in place.items()},
            [arrays[k] for k in kept],
            {c: (kept_columns.index(at[0]), at[1]) for c, at in column_place.items()},
            [columns[k] for k in kept_columns],
            total,
        )

    def after(block, done):
        return lax.optimization_barrier((block, done))[0]

    rows, keep, give = lax.optimization_barrier((rows, keep, give))
    near, near_other, a1, b0, e0 = send(keep, turn(False)), send(give, turn(True)), send(rows, Z_RING), send(rows, X_FAR), send(rows, CORES)
    a3 = send(after(rows, e0), Z_BACK)
    near, near_other, a1, a3, b0, e0 = lax.optimization_barrier((near, near_other, a1, a3, b0, e0))
    c0 = jnp.concatenate([near, near_other], axis=0)
    d0, c1, c3, b1, e1 = send(c0, X_NEAR), send(c0, Y_RING), send(c0, Y_BACK), send(b0, Z_RING), send(jnp.concatenate([a1, a3]), CORES)
    b3 = send(after(b0, e1), Z_BACK)
    d0, c1, c3, b1, b3, e1 = lax.optimization_barrier((d0, c1, c3, b1, b3, e1))
    up, across, along = send(jnp.concatenate([d0, c1]), Y_RING), send(c3, X_NEAR), send(jnp.concatenate([a1, b1]), Z_RING)
    e2, e3 = send(jnp.concatenate([b0, b1]), CORES), send(b3, CORES)
    total = add_up(0, [rows, a1, a3, b0, b1, b3, None, e0, e1, e2, e3, None], [c0, c1, c3, d0, None, None, None])
    total, up, across, along = lax.optimization_barrier((total, up, across, along))
    d2, e4 = send(up[:2 * PART], Y_RING), send(along, CORES)
    total = add_up(1, [rows, a1, a3, b0, b1, b3, along, e0, e1, e2, e3, None], [c0, c1, c3, d0, up, across, None], total)
    return add_up(2, [rows, a1, a3, b0, b1, b3, along, e0, e1, e2, e3, e4], [c0, c1, c3, d0, up, across, d2], total)


def solution(mesh):
    fine = Mesh(mesh.devices.reshape(SIZES), AXES)
    return jax.shard_map(
        body,
        mesh=fine,
        in_specs=P("d", ("xl", "y"), ("xh", "z")),
        out_specs=P(("xl", "y"), ("xh", "z", "d")),
        check_vma=False,
    )
```

time: 174 us -> 157 us (0.902); the launches traced: 172 us -> 157 us
  waiting for transfers between devices: 102 us -> 72.5 us
  Pallas kernels: 22.7 us -> 41.1 us
  starting transfers between devices: 39.6 us -> 26.5 us
  local copies, waits for them, and re-layouts: 5.99 us -> 11.7 us
  other arithmetic: 1.31 us -> 4.71 us
    ppermute x24 -> x19, waiting for transfers between devices: 102 us -> 72.5 us  [send(): return lax.ppermute(block, AXES, pairs)]
    pallas_call x1 -> x3, Pallas kernels: 22.7 us -> 41.1 us  [multiply(): pl.pallas_call(kernel, grid=(ROWS // TILE,), out_shape=jax.ShapeDtypeStru...]
    ppermute x24 -> x19, starting transfers between devices: 39.6 us -> 26.5 us  [send(): return lax.ppermute(block, AXES, pairs)]
    concatenate x0 -> x3, other arithmetic: none -> 4.46 us  [the longest x1 2.61 us: body(): jnp.concatenate([a1, b1])]
    another operation x1 -> x3, local copies, waits for them, and re-layouts: 0.09 us -> 1.93 us  [add_up(): jnp.stack([jnp.asarray(v, jnp.int32) for v in select])]
    unnamed x27 -> x33, local copies, waits for them, and re-layouts: 2.37 us -> 3.97 us
  transfers between devices with their start and end apart: 24 -> 19, of which waited for: 11 -> 10; matrix products, arithmetic and copies ran while one was open for 1% -> 3% of each run, Pallas kernels for 0% -> 19%
where the time goes in v2:
time: 157 us
  waiting for transfers between devices  72.5 us (46%)
  Pallas kernels  41.1 us (26%)
  starting transfers between devices  26.5 us (17%)
  local copies, waits for them, and re-layouts  11.7 us (7%)
  other arithmetic  4.71 us (3%)
    ppermute x19, waiting for transfers between devices, send(): return lax.ppermute(block, AXES, pairs)  72.5 us
    pallas_call x3, Pallas kernels, multiply(): pl.pallas_call(kernel, grid=(ROWS // TILE,), out_shape=jax.ShapeDtypeStru...  41.1 us
    ppermute x19, starting transfers between devices, send(): return lax.ppermute(block, AXES, pairs)  26.5 us
    unnamed x33, local copies, waits for them, and re-layouts  3.97 us
  transfers between devices with their start and end apart: 19, of which 10 were waited for; matrix products, arithmetic and copies ran while one was open for 3% of the time, Pallas kernels for 19%

profile of v2, /device:TPU:1, one launch (start us, length us, event | category | flops | bytes accessed | tf_op | source)
XLA Modules:
  0.0 156.9 jit_solution(14373684872684111553)
XLA Ops:
  0.0 2.2 %slice.14 = bf16[384,750]{1,0:T(8,128)(2,1)} slice(bf16[384,1500]{1,0:T(8,128)(2,1)} %bitcast.30), slice={[0:384], [750:1500]} | slice | bytes 1152000 | tf_op jit(solution)/shard_map/slice | solution.py:146
  2.2 2.4 %copy.3 = bf16[1500,384]{1,0:T(8,128)(2,1)S(1)} copy(bf16[1500,384]{0,1:T(8,128)(2,1)} %bitcast.31) | data formatting | bytes 2304000 | tf_op jit(solution)/shard_map/reshape | solution.py:149
  4.7 0.9 copy-done.13
  5.9 1.5 collective-permute-start.3
  7.4 2.8 %collective-permute-start.5 = (bf16[1536,384]{1,0:T(8,128)(2,1)S(1)}, bf16[1536,384]{1,0:T(8,128)(2,1)S(1)}, u32[]{:S(2)}, u32[]{:S(2)}) collective-permute-start(bf16[1536,384]{1,0:T(8,128)(2,1)S(1)} %pad.11.refs_1_), channel_id=1, source_target_pairs={{0,8},{1,9},{2,10},{3,11},{4,12},{5,13},{6,14},{7,15},{8,0},{9,1},... | collective-permute-start | bytes 3538952 | tf_op jit(solution)/shard_map/ppermute | solution.py:47
  10.2 3.8 %collective-permute-start.2 = (bf16[1536,384]{1,0:T(8,128)(2,1)S(1)}, bf16[1536,384]{1,0:T(8,128)(2,1)S(1)}, u32[]{:S(2)}, u32[]{:S(2)}) collective-permute-start(bf16[1536,384]{1,0:T(8,128)(2,1)S(1)} %pad.11.refs_1_), channel_id=1, source_target_pairs={{0,2},{1,7},{2,4},{3,1},{4,6},{5,3},{6,0},{7,5},{8,10},{9,15},{10,... | collective-permute-start | bytes 3538952 | tf_op jit(solution)/shard_map/ppermute | solution.py:47
  14.0 4.9 %collective-permute-start = (bf16[384,768]{1,0:T(8,128)(2,1)S(1)}, bf16[384,768]{1,0:T(8,128)(2,1)S(1)}, u32[]{:S(2)}, u32[]{:S(2)}) collective-permute-start(bf16[384,768]{1,0:T(8,128)(2,1)S(1)} %get-tuple-element.27), channel_id=1, source_target_pairs={{0,0},{1,97},{2,48},{3,81},{4,32},{5,65},{6,16},{7,113},{8,64},{9,... | collective-permute-start | bytes 1769480 | tf_op jit(solution)/shard_map/ppermute | solution.py:47
  18.9 33.4 %collective-permute-done = bf16[384,768]{1,0:T(8,128)(2,1)S(1)} collective-permute-done((bf16[384,768]{1,0:T(8,128)(2,1)S(1)}, bf16[384,768]{1,0:T(8,128)(2,1)S(1)}, u32[]{:S(2)}, u32[]{:S(2)}) %collective-permute-start) | collective-permute-done | bytes 589856 | tf_op jit(solution)/shard_map/ppermute | solution.py:47
  53.7 0.9 copy-done.4
  54.7 1.2 collective-permute-start.8
  55.9 1.5 collective-permute-start.7
  58.0 3.4 %collective-permute-start.9 = (bf16[1536,384]{1,0:T(8,128)(2,1)S(1)}, bf16[1536,384]{1,0:T(8,128)(2,1)S(1)}, u32[]{:S(2)}, u32[]{:S(2)}) collective-permute-start(bf16[1536,384]{1,0:T(8,128)(2,1)S(1)} %collective-permute-done.5.refs_4_), channel_id=1, source_target_pairs={{0,2},{1,7},{2,4},{3,1},{4,6},{5,3},{6,0},{7,5},{8,10},{9,15},{10,... | collective-permute-start | bytes 3538952 | tf_op jit(solution)/shard_map/ppermute | solution.py:47
  61.4 18.7 %collective-permute-done.8.refs_13_.refs_14_.refs_15_ = bf16[768,768]{1,0:T(8,128)(2,1)} collective-permute-done((bf16[768,768]{1,0:T(8,128)(2,1)S(1)}, bf16[768,768]{1,0:T(8,128)(2,1)}, u32[]{:S(2)}, u32[]{:S(2)}) %collective-permute-start.8) | collective-permute-done | bytes 1179680 | tf_op jit(solution)/shard_map/ppermute | solution.py:47
  80.1 3.8 %collective-permute-done.7.refs_12_.refs_13_.refs_14_ = bf16[768,768]{1,0:T(8,128)(2,1)S(1)} collective-permute-done((bf16[768,768]{1,0:T(8,128)(2,1)S(1)}, bf16[768,768]{1,0:T(8,128)(2,1)S(1)}, u32[]{:S(2)}, u32[]{:S(2)}) %collective-permute-start.7) | collective-permute-done | bytes 1179680 | tf_op jit(solution)/shard_map/ppermute | solution.py:47
  84.4 2.0 %collective-permute-done.9.refs_5_ = bf16[1536,384]{1,0:T(8,128)(2,1)S(1)} collective-permute-done((bf16[1536,384]{1,0:T(8,128)(2,1)S(1)}, bf16[1536,384]{1,0:T(8,128)(2,1)S(1)}, u32[]{:S(2)}, u32[]{:S(2)}) %collective-permute-start.9) | collective-permute-done | bytes 1179680 | tf_op jit(solution)/shard_map/ppermute | solution.py:47
  86.4 2.0 %collective-permute-done.11.refs_6_ = bf16[1536,384]{1,0:T(8,128)(2,1)} collective-permute-done((bf16[1536,384]{1,0:T(8,128)(2,1)S(1)}, bf16[1536,384]{1,0:T(8,128)(2,1)}, u32[]{:S(2)}, u32[]{:S(2)}) %collective-permute-start.11) | collective-permute-done | bytes 1179680 | tf_op jit(solution)/shard_map/ppermute | solution.py:47
  88.3 2.6 %pad_maximum_fusion = (bf16[3072,384]{1,0:T(8,128)(2,1)}, bf16[3072,384]{1,0:T(8,128)(2,1)}) fusion(bf16[1536,384]{1,0:T(8,128)(2,1)S(1)} %collective-permute-done.2.refs_2_, bf16[1536,384]{1,0:T(8,128)(2,1)S(1)} %collective-permute-done.9.refs_5_, bf16[1536,384]{1,0:T(8,128)(2,1)S(1)} %collective-permute-done.5.refs_4_), kind=kLoop, calls=%fused_computation | loop fusion | flops 8257536 | bytes 8257536 | tf_op jit(solution)/shard_map/concatenate | solution.py:220
  91.0 1.6 %pad_maximum_fusion.3 = bf16[1536,768]{1,0:T(8,128)(2,1)} fusion(bf16[768,768]{1,0:T(8,128)(2,1)S(1)} %collective-permute-done.7.refs_12_.refs_13_.refs_14_, bf16[768,768]{1,0:T(8,128)(2,1)S(1)} %collective-permute-done.6.refs_14_.refs_15_.refs_16_), kind=kLoop, calls=%fused_computation.3 | loop fusion | flops 4718592 | bytes 4718592 | tf_op jit(solution)/shard_map/concatenate | solution.py:220
  92.6 3.2 %collective-permute-start.14 = (bf16[1536,768]{1,0:T(8,128)(2,1)}, bf16[1536,768]{1,0:T(8,128)(2,1)S(1)}, u32[]{:S(2)}, u32[]{:S(2)}) collective-permute-start(bf16[1536,768]{1,0:T(8,128)(2,1)} %pad_maximum_fusion.3), channel_id=1, source_target_pairs={{0,16},{1,49},{2,18},{3,51},{4,20},{5,53},{6,22},{7,55},{8,24},{9,... | collective-permute-start | bytes 7077896 | tf_op jit(solution)/shard_map/ppermute | solution.py:47
  95.8 1.0 collective-permute-start.16
  97.1 0.6 stack.96.refs_0_
  97.8 2.1 %collective-permute-done.13.refs_10_.refs_11_ = bf16[1536,384]{1,0:T(8,128)(2,1)S(1)} collective-permute-done((bf16[1536,384]{1,0:T(8,128)(2,1)}, bf16[1536,384]{1,0:T(8,128)(2,1)S(1)}, u32[]{:S(2)}, u32[]{:S(2)}) %collective-permute-start.13) | collective-permute-done | bytes 1179680 | tf_op jit(solution)/shard_map/ppermute | solution.py:47
  99.9 1.0 copy-done.11
  100.9 14.2 %shard_map.17.refs_18_ = f32[1500,750]{1,0:T(8,128)} custom-call(s32[16]{0:T(128)} %stack.96.refs_0_, bf16[1536,384]{1,0:T(8,128)(2,1)} %copy-done.2, bf16[1536,384]{1,0:T(8,128)(2,1)} %copy-done, bf16[1536,384]{1,0:T(8,128)(2,1)} %copy-done.4, bf16[1536,384]{1,0:T(8,128)(2,1)} %copy-done.3, bf16[1536,384]{1,0:T(8,128)(2,1)} %copy-done.7, ...), custom_call_target="tpu_custom_call" | custom-call | flops 6912000000 | bytes 18655776 | tf_op jit(solution)/shard_map/pallas_call | solution.py:120
  115.1 9.0 %collective-permute-done.15.refs_17_.refs_18_ = bf16[768,768]{1,0:T(8,128)(2,1)} collective-permute-done((bf16[768,768]{1,0:T(8,128)(2,1)}, bf16[768,768]{1,0:T(8,128)(2,1)}, u32[]{:S(2)}, u32[]{:S(2)}) %collective-permute-start.15) | collective-permute-done | bytes 1179680 | tf_op jit(solution)/shard_map/ppermute | solution.py:47
  124.2 1.4 collective-permute-start.17
  125.6 1.1 slice.12
  126.7 0.8 collective-permute-start.18
  128.1 0.7 stack.107.refs_0_
  128.8 16.1 %shard_map.18.refs_20_ = f32[1500,750]{1,0:T(8,128)} custom-call(s32[16]{0:T(128)} %stack.107.refs_0_, bf16[1536,384]{1,0:T(8,128)(2,1)} %copy-done.2, bf16[1536,384]{1,0:T(8,128)(2,1)} %copy-done, bf16[1536,384]{1,0:T(8,128)(2,1)} %copy-done.4, bf16[1536,384]{1,0:T(8,128)(2,1)} %copy-done.3, bf16[1536,384]{1,0:T(8,128)(2,1)} %copy-done.7, ...), custom_call_target="tpu_custom_call" | custom-call | flops 6912000000 | bytes 23155776 | tf_op jit(solution)/shard_map/pallas_call | solution.py:120
  144.9 1.0 copy-done.14
  146.0 10.8 %shard_map.19 = f32[1500,750]{1,0:T(8,128)} custom-call(s32[8]{0:T(128)} %stack.87.refs_0_, bf16[1536,384]{1,0:T(8,128)(2,1)} %copy-done.2, bf16[1536,384]{1,0:T(8,128)(2,1)} %copy-done, bf16[1536,384]{1,0:T(8,128)(2,1)} %copy-done.4, bf16[1536,384]{1,0:T(8,128)(2,1)} %copy-done.3, bf16[1536,384]{1,0:T(8,128)(2,1)} %copy-done.7, ...), custom_call_target="tpu_custom_call" | custom-call | flops 3456000000 | bytes 16077888 | tf_op jit(solution)/shard_map/pallas_call | solution.py:120
  (54 shorter events, 3.9 us)
Async XLA Ops:
  2.2 2.6 %copy-start.12 = (bf16[2,1500,192]{1,2,0:T(8,128)(2,1)S(1)}, bf16[2,1500,192]{1,2,0:T(8,128)(2,1)}, u32[]{:S(2)}) copy-start(bf16[2,1500,192]{1,2,0:T(8,128)(2,1)} %param.1) | copy-start | bytes 3456004
  2.2 2.6 %copy-start.15 = (pred[768]{0:T(1024)(128)(4,1)S(1)}, pred[768]{0:T(1024)(128)(4,1)}, u32[]{:S(2)}) copy-start(pred[768]{0:T(1024)(128)(4,1)} %constant.146.clone.1) | copy-start | bytes 2308
  5.6 48.0 %copy-start.2 = (bf16[1536,384]{1,0:T(8,128)(2,1)}, bf16[1536,384]{1,0:T(8,128)(2,1)S(1)}, u32[]{:S(2)}) copy-start(bf16[1536,384]{1,0:T(8,128)(2,1)S(1)} %pad.11.refs_1_) | copy-start | bytes 3538948
  5.9 8.1 %collective-permute-start.3 = (bf16[1536,384]{1,0:T(8,128)(2,1)S(1)}, bf16[1536,384]{1,0:T(8,128)(2,1)S(1)}, u32[]{:S(2)}, u32[]{:S(2)}) collective-permute-start(bf16[1536,384]{1,0:T(8,128)(2,1)S(1)} %pad.11.refs_1_), channel_id=1, source_target_pairs={{0,1},{1,0},{2,3},{3,2},{4,5},{5,4},{6,7},{7,6},{8,9},{9,8},{10,11... | collective-permute-start | bytes 3538952 | tf_op jit(solution)/shard_map/ppermute | solution.py:47
  7.4 45.4 %collective-permute-start.5 = (bf16[1536,384]{1,0:T(8,128)(2,1)S(1)}, bf16[1536,384]{1,0:T(8,128)(2,1)S(1)}, u32[]{:S(2)}, u32[]{:S(2)}) collective-permute-start(bf16[1536,384]{1,0:T(8,128)(2,1)S(1)} %pad.11.refs_1_), channel_id=1, source_target_pairs={{0,8},{1,9},{2,10},{3,11},{4,12},{5,13},{6,14},{7,15},{8,0},{9,1},... | collective-permute-start | bytes 3538952 | tf_op jit(solution)/shard_map/ppermute | solution.py:47
  10.2 42.6 %collective-permute-start.2 = (bf16[1536,384]{1,0:T(8,128)(2,1)S(1)}, bf16[1536,384]{1,0:T(8,128)(2,1)S(1)}, u32[]{:S(2)}, u32[]{:S(2)}) collective-permute-start(bf16[1536,384]{1,0:T(8,128)(2,1)S(1)} %pad.11.refs_1_), channel_id=1, source_target_pairs={{0,2},{1,7},{2,4},{3,1},{4,6},{5,3},{6,0},{7,5},{8,10},{9,15},{10,... | collective-permute-start | bytes 3538952 | tf_op jit(solution)/shard_map/ppermute | solution.py:47
  14.0 38.8 %copy-start.10 = (bf16[1536,384]{1,0:T(8,128)(2,1)}, bf16[1536,384]{1,0:T(8,128)(2,1)S(1)}, u32[]{:S(2)}) copy-start(bf16[1536,384]{1,0:T(8,128)(2,1)S(1)} %collective-permute-done.3.refs_7_.refs_8_) | copy-start | bytes 3538948
  14.0 39.4 %collective-permute-start.4 = (bf16[1536,384]{1,0:T(8,128)(2,1)S(1)}, bf16[1536,384]{1,0:T(8,128)(2,1)S(1)}, u32[]{:S(2)}, u32[]{:S(2)}) collective-permute-start(bf16[1536,384]{1,0:T(8,128)(2,1)S(1)} %pad.11.refs_1_), channel_id=1, source_target_pairs={{0,6},{1,3},{2,0},{3,5},{4,2},{5,7},{6,4},{7,1},{8,14},{9,11},{10,... | collective-permute-start | bytes 3538952 | tf_op jit(solution)/shard_map/ppermute | solution.py:47
  14.0 38.3 %collective-permute-start = (bf16[384,768]{1,0:T(8,128)(2,1)S(1)}, bf16[384,768]{1,0:T(8,128)(2,1)S(1)}, u32[]{:S(2)}, u32[]{:S(2)}) collective-permute-start(bf16[384,768]{1,0:T(8,128)(2,1)S(1)} %get-tuple-element.27), channel_id=1, source_target_pairs={{0,0},{1,97},{2,48},{3,81},{4,32},{5,65},{6,16},{7,113},{8,64},{9,... | collective-permute-start | bytes 1769480 | tf_op jit(solution)/shard_map/ppermute | solution.py:47
  18.9 33.9 %collective-permute-start.1 = (bf16[384,768]{1,0:T(8,128)(2,1)S(1)}, bf16[384,768]{1,0:T(8,128)(2,1)S(1)}, u32[]{:S(2)}, u32[]{:S(2)}) collective-permute-start(bf16[384,768]{1,0:T(8,128)(2,1)S(1)} %get-tuple-element.28), channel_id=1, source_target_pairs={{0,97},{1,0},{2,81},{3,48},{4,65},{5,32},{6,113},{7,16},{8,33},{9,... | collective-permute-start | bytes 1769480 | tf_op jit(solution)/shard_map/ppermute | solution.py:47
  52.8 35.5 %copy-start.3 = (bf16[1536,384]{1,0:T(8,128)(2,1)}, bf16[1536,384]{1,0:T(8,128)(2,1)S(1)}, u32[]{:S(2)}) copy-start(bf16[1536,384]{1,0:T(8,128)(2,1)S(1)} %collective-permute-done.5.refs_4_) | copy-start | bytes 3538948
  52.8 35.5 %copy-start = (bf16[1536,384]{1,0:T(8,128)(2,1)}, bf16[1536,384]{1,0:T(8,128)(2,1)S(1)}, u32[]{:S(2)}) copy-start(bf16[1536,384]{1,0:T(8,128)(2,1)S(1)} %collective-permute-done.2.refs_2_) | copy-start | bytes 3538948
  53.4 1.2 copy-start.4
  54.6 6.8 %collective-permute-start.10 = (bf16[3072,384]{1,0:T(8,128)(2,1)S(1)}, bf16[3072,384]{1,0:T(8,128)(2,1)S(1)}, u32[]{:S(2)}, u32[]{:S(2)}) collective-permute-start(bf16[3072,384]{1,0:T(8,128)(2,1)S(1)} %pad_maximum_fusion.1), channel_id=1, source_target_pairs={{0,1},{1,0},{2,3},{3,2},{4,5},{5,4},{6,7},{7,6},{8,9},{9,8},{10,11... | collective-permute-start | bytes 7077896 | tf_op jit(solution)/shard_map/ppermute | solution.py:47
  54.7 31.7 %copy-start.9 = (bf16[768,768]{1,0:T(8,128)(2,1)}, bf16[768,768]{1,0:T(8,128)(2,1)S(1)}, u32[]{:S(2)}) copy-start(bf16[768,768]{1,0:T(8,128)(2,1)S(1)} %constant_dynamic-update-slice_fusion.refs_11_.refs_12_.refs_13_) | copy-start | bytes 3538948
  54.7 25.4 %collective-permute-start.8 = (bf16[768,768]{1,0:T(8,128)(2,1)S(1)}, bf16[768,768]{1,0:T(8,128)(2,1)}, u32[]{:S(2)}, u32[]{:S(2)}) collective-permute-start(bf16[768,768]{1,0:T(8,128)(2,1)S(1)} %constant_dynamic-update-slice_fusion.refs_11_.refs_12_.refs_13_), channel_id=1, source_target_pairs={{0,48},{1,17},{2,50},{3,19},{4,52},{5,21},{6,54},{7,23},{8,56},{9,... | collective-permute-start | bytes 3538952 | tf_op jit(solution)/shard_map/ppermute | solution.py:47
  55.9 27.9 %collective-permute-start.7 = (bf16[768,768]{1,0:T(8,128)(2,1)S(1)}, bf16[768,768]{1,0:T(8,128)(2,1)S(1)}, u32[]{:S(2)}, u32[]{:S(2)}) collective-permute-start(bf16[768,768]{1,0:T(8,128)(2,1)S(1)} %constant_dynamic-update-slice_fusion.refs_11_.refs_12_.refs_13_), channel_id=1, source_target_pairs={{0,16},{1,49},{2,18},{3,51},{4,20},{5,53},{6,22},{7,55},{8,24},{9,... | collective-permute-start | bytes 3538952 | tf_op jit(solution)/shard_map/ppermute | solution.py:47
  57.4 26.9 %collective-permute-start.6 = (bf16[768,768]{1,0:T(8,128)(2,1)S(1)}, bf16[768,768]{1,0:T(8,128)(2,1)S(1)}, u32[]{:S(2)}, u32[]{:S(2)}) collective-permute-start(bf16[768,768]{1,0:T(8,128)(2,1)S(1)} %constant_dynamic-update-slice_fusion.refs_11_.refs_12_.refs_13_), channel_id=1, source_target_pairs={{0,64},{1,65},{2,66},{3,67},{4,68},{5,69},{6,70},{7,71},{8,72},{9,... | collective-permute-start | bytes 3538952 | tf_op jit(solution)/shard_map/ppermute | solution.py:47
  58.0 28.3 %collective-permute-start.9 = (bf16[1536,384]{1,0:T(8,128)(2,1)S(1)}, bf16[1536,384]{1,0:T(8,128)(2,1)S(1)}, u32[]{:S(2)}, u32[]{:S(2)}) collective-permute-start(bf16[1536,384]{1,0:T(8,128)(2,1)S(1)} %collective-permute-done.5.refs_4_), channel_id=1, source_target_pairs={{0,2},{1,7},{2,4},{3,1},{4,6},{5,3},{6,0},{7,5},{8,10},{9,15},{10,... | collective-permute-start | bytes 3538952 | tf_op jit(solution)/shard_map/ppermute | solution.py:47
  61.4 24.9 %copy-start.8 = (bf16[3072,384]{1,0:T(8,128)(2,1)}, bf16[3072,384]{1,0:T(8,128)(2,1)S(1)}, u32[]{:S(2)}) copy-start(bf16[3072,384]{1,0:T(8,128)(2,1)S(1)} %collective-permute-done.10.refs_8_.refs_9_) | copy-start | bytes 7077892
  61.4 26.9 %collective-permute-start.11 = (bf16[1536,384]{1,0:T(8,128)(2,1)S(1)}, bf16[1536,384]{1,0:T(8,128)(2,1)}, u32[]{:S(2)}, u32[]{:S(2)}) collective-permute-start(bf16[1536,384]{1,0:T(8,128)(2,1)S(1)} %collective-permute-done.5.refs_4_), channel_id=1, source_target_pairs={{0,6},{1,3},{2,0},{3,5},{4,2},{5,7},{6,4},{7,1},{8,14},{9,11},{10,... | collective-permute-start | bytes 3538952 | tf_op jit(solution)/shard_map/ppermute | solution.py:47
  83.8 7.1 %copy-start.5 = (bf16[768,768]{1,0:T(8,128)(2,1)}, bf16[768,768]{1,0:T(8,128)(2,1)S(1)}, u32[]{:S(2)}) copy-start(bf16[768,768]{1,0:T(8,128)(2,1)S(1)} %collective-permute-done.7.refs_12_.refs_13_.refs_14_) | copy-start | bytes 3538948
  84.4 6.6 %copy-start.6 = (bf16[768,768]{1,0:T(8,128)(2,1)}, bf16[768,768]{1,0:T(8,128)(2,1)S(1)}, u32[]{:S(2)}) copy-start(bf16[768,768]{1,0:T(8,128)(2,1)S(1)} %collective-permute-done.6.refs_14_.refs_15_.refs_16_) | copy-start | bytes 3538948
  86.3 4.6 %copy-start.7 = (bf16[1536,384]{1,0:T(8,128)(2,1)}, bf16[1536,384]{1,0:T(8,128)(2,1)S(1)}, u32[]{:S(2)}) copy-start(bf16[1536,384]{1,0:T(8,128)(2,1)S(1)} %collective-permute-done.9.refs_5_) | copy-start | bytes 3538948
  90.9 8.9 %collective-permute-start.12 = (bf16[3072,384]{1,0:T(8,128)(2,1)}, bf16[3072,384]{1,0:T(8,128)(2,1)}, u32[]{:S(2)}, u32[]{:S(2)}) collective-permute-start(bf16[3072,384]{1,0:T(8,128)(2,1)} %get-tuple-element.50), channel_id=1, source_target_pairs={{0,1},{1,0},{2,3},{3,2},{4,5},{5,4},{6,7},{7,6},{8,9},{9,8},{10,11... | collective-permute-start | bytes 7077896 | tf_op jit(solution)/shard_map/ppermute | solution.py:47
  92.6 31.6 %collective-permute-start.14 = (bf16[1536,768]{1,0:T(8,128)(2,1)}, bf16[1536,768]{1,0:T(8,128)(2,1)S(1)}, u32[]{:S(2)}, u32[]{:S(2)}) collective-permute-start(bf16[1536,768]{1,0:T(8,128)(2,1)} %pad_maximum_fusion.3), channel_id=1, source_target_pairs={{0,16},{1,49},{2,18},{3,51},{4,20},{5,53},{6,22},{7,55},{8,24},{9,... | collective-permute-start | bytes 7077896 | tf_op jit(solution)/shard_map/ppermute | solution.py:47
  95.8 28.3 %collective-permute-start.16 = (bf16[3072,384]{1,0:T(8,128)(2,1)}, bf16[3072,384]{1,0:T(8,128)(2,1)}, u32[]{:S(2)}, u32[]{:S(2)}) collective-permute-start(bf16[3072,384]{1,0:T(8,128)(2,1)} %get-tuple-element.49), channel_id=1, source_target_pairs={{0,2},{1,7},{2,4},{3,1},{4,6},{5,3},{6,0},{7,5},{8,10},{9,15},{10,... | collective-permute-start | bytes 7077896 | tf_op jit(solution)/shard_map/ppermute | solution.py:47
  96.8 3.1 %collective-permute-start.13 = (bf16[1536,384]{1,0:T(8,128)(2,1)}, bf16[1536,384]{1,0:T(8,128)(2,1)S(1)}, u32[]{:S(2)}, u32[]{:S(2)}) collective-permute-start(bf16[1536,384]{1,0:T(8,128)(2,1)} %collective-permute-done.11.refs_6_), channel_id=1, source_target_pairs={{0,1},{1,0},{2,3},{3,2},{4,5},{5,4},{6,7},{7,6},{8,9},{9,8},{10,11... | collective-permute-start | bytes 3538952 | tf_op jit(solution)/shard_map/ppermute | solution.py:47
  96.8 27.3 %collective-permute-start.15 = (bf16[768,768]{1,0:T(8,128)(2,1)}, bf16[768,768]{1,0:T(8,128)(2,1)}, u32[]{:S(2)}, u32[]{:S(2)}) collective-permute-start(bf16[768,768]{1,0:T(8,128)(2,1)} %collective-permute-done.8.refs_13_.refs_14_.refs_15_), channel_id=1, source_target_pairs={{0,64},{1,65},{2,66},{3,67},{4,68},{5,69},{6,70},{7,71},{8,72},{9,... | collective-permute-start | bytes 3538952 | tf_op jit(solution)/shard_map/ppermute | solution.py:47
  124.2 4.7 %copy-start.1 = (bf16[1536,768]{1,0:T(8,128)(2,1)}, bf16[1536,768]{1,0:T(8,128)(2,1)S(1)}, u32[]{:S(2)}) copy-start(bf16[1536,768]{1,0:T(8,128)(2,1)S(1)} %collective-permute-done.14.refs_16_.refs_17_) | copy-start | bytes 7077892
  124.2 20.7 %collective-permute-start.17 = (bf16[3072,384]{1,0:T(8,128)(2,1)}, bf16[3072,384]{1,0:T(8,128)(2,1)}, u32[]{:S(2)}, u32[]{:S(2)}) collective-permute-start(bf16[3072,384]{1,0:T(8,128)(2,1)} %collective-permute-done.16.refs_7_), channel_id=1, source_target_pairs={{0,1},{1,0},{2,3},{3,2},{4,5},{5,4},{6,7},{7,6},{8,9},{9,8},{10,11... | collective-permute-start | bytes 7077896 | tf_op jit(solution)/shard_map/ppermute | solution.py:47
  126.7 18.2 %collective-permute-start.18 = (bf16[768,768]{1,0:T(8,128)(2,1)}, bf16[768,768]{1,0:T(8,128)(2,1)S(1)}, u32[]{:S(2)}, u32[]{:S(2)}) collective-permute-start(bf16[768,768]{1,0:T(8,128)(2,1)} %slice.12), channel_id=1, source_target_pairs={{0,16},{1,49},{2,18},{3,51},{4,20},{5,53},{6,22},{7,55},{8,24},{9,... | collective-permute-start | bytes 3538952 | tf_op jit(solution)/shard_map/ppermute | solution.py:47
  (3 other events, 3.1 us)

commit v3 on v2

v3 whole, which is shorter than its diff:
```python
import itertools

import jax
import jax.numpy as jnp
import numpy as np
from jax import lax
from jax.experimental import pallas as pl
from jax.experimental.pallas import tpu as pltpu
from jax.sharding import Mesh
from jax.sharding import PartitionSpec as P

AXES = ("xl", "y", "xh", "z", "d")
SIZES = (2, 4, 2, 4, 2)
BASIS, HALF = 1500, 750
ROWS, COLS, PART = 1536, 768, 384
TILE = 512

ROW_STAGE = ((0, 0, 0, 0, 0, 0, 1, 0), (0, 0, 0, 0, 0, 0, 1, 0))
COLUMN_STAGE = (0, 0, 0, 0, 0, 1, 1, 1)
PLACES = {(0, row): (row, 0) for row in range(8)}
PLACES.update({
    (1, 0): (8, 0), (1, 1): (9, 0), (1, 3): (9, ROWS), (1, 4): (10, 0),
    (1, 5): (10, ROWS), (1, 7): (11, 0), (1, 2): (11, ROWS), (1, 6): (12, 0),
})


def perm(target):
    out = []
    for at in itertools.product(*map(range, SIZES)):
        to = target(*at)
        out.append((int(np.ravel_multi_index(at, SIZES)), int(np.ravel_multi_index(to, SIZES))))
    return out


def turn(cross):
    def target(xl, y, xh, z, d):
        e = 1 - d if cross else d
        return xh ^ e, (2 * e - y - z) % 4, xl, y, e

    return perm(target)


Z_RING = perm(lambda xl, y, xh, z, d: (xl, y, xh, (z + 1 - 2 * d) % 4, d))
Y_RING = perm(lambda xl, y, xh, z, d: (xl, (y + 1 - 2 * d) % 4, xh, z, d))
Z_BACK = perm(lambda xl, y, xh, z, d: (xl, y, xh, (z - 1 + 2 * d) % 4, d))
Y_BACK = perm(lambda xl, y, xh, z, d: (xl, (y - 1 + 2 * d) % 4, xh, z, d))
X_FAR = perm(lambda xl, y, xh, z, d: (xl, y, 1 - xh, z, d))
X_NEAR = perm(lambda xl, y, xh, z, d: (1 - xl, y, xh, z, d))
CORES = perm(lambda xl, y, xh, z, d: (xl, y, xh, z, 1 - d))


def send(block, pairs):
    return lax.ppermute(block, AXES, pairs)


def after(block, done):
    return lax.optimization_barrier((block, done))[0]


def prepare_kernel(spot, slab, rows, keep, give):
    block = slab[...]
    rows[...] = jnp.pad(block, ((0, 0), (0, ROWS - BASIS))).T
    low = jnp.pad(block[:, :HALF], ((0, 0), (0, COLS - HALF)))
    high = jnp.pad(block[:, HALF:], ((0, 0), (0, COLS - HALF)))

    @pl.when(spot[4] == 0)
    def _():
        keep[...] = low
        give[...] = high

    @pl.when(spot[4] == 1)
    def _():
        keep[...] = high
        give[...] = low


def prepare(spot, slab):
    whole = pl.BlockSpec(memory_space=pltpu.VMEM)
    half = jax.ShapeDtypeStruct((PART, COLS), jnp.bfloat16)
    return pl.pallas_call(
        prepare_kernel,
        out_shape=[jax.ShapeDtypeStruct((ROWS, PART), jnp.bfloat16), half, half],
        in_specs=[pl.BlockSpec(memory_space=pltpu.SMEM), whole],
        out_specs=[whole] * 3,
        compiler_params=pltpu.CompilerParams(vmem_limit_bytes=32 << 20),
    )(spot, slab)


def meeting_row(spot, side, column):
    xl, y, xh, z, d = (spot[k] for k in range(5))
    half, step = divmod(column, 4)
    way = 1 - 2 * d
    orbital = 2 * d - y - z + way * step
    steps = (way if side == 0 else -way) * (z - orbital)
    return 4 * (xl ^ d ^ half ^ xh) + (steps & 3)


def slots_of(stage):
    slots = []
    for side in range(2):
        here = tuple(r for r in range(8) if ROW_STAGE[side][r] <= stage)
        slots += [(side, here, (c,)) for c in range(8) if COLUMN_STAGE[c] == stage]
        earlier = tuple(c for c in range(8) if COLUMN_STAGE[c] < stage)
        if earlier:
            slots += [(side, (r,), earlier) for r in here if ROW_STAGE[side][r] == stage]
    return slots


def multiply_kernel(slots, places, column_places, n_columns, has_total, spot, *refs):
    n_rows = 1 + max(place[0] for place in places.values())
    arrays, refs = refs[:n_rows], refs[n_rows:]
    columns, refs = refs[:n_columns], refs[n_columns:]
    total, refs = (refs[0], refs[1:]) if has_total else (None, refs)
    out, lhs, rhs, lhs_sem, rhs_sem = refs
    tile = pl.program_id(0)
    spans = ((0, TILE), (TILE, ROWS - TILE))

    taken = []
    for side, row_options, column_options in slots:
        if len(column_options) == 1:
            met = meeting_row(spot, side, column_options[0])
            row = jnp.int32(-1)
            for r in row_options:
                row = jnp.where(met == r, r, row)
            taken.append((row, jnp.int32(column_options[0])))
        else:
            row, column = jnp.int32(-1), jnp.int32(column_options[0])
            for c in column_options:
                meets = meeting_row(spot, side, c) == row_options[0]
                row = jnp.where(meets, row_options[0], row)
                column = jnp.where(meets, c, column)
            taken.append((row, column))

    def lhs_copy(slot, place, span):
        start, size = spans[span]
        array, offset = place
        return pltpu.make_async_copy(
            arrays[array].at[pl.ds(offset + start, size)],
            lhs.at[pl.ds(start, size), pl.ds(slot * PART, PART)],
            lhs_sem.at[slot, span],
        )

    def rhs_copy(slot, column):
        return pltpu.make_async_copy(
            columns[column_places[column]].at[pl.ds(slots[slot][0] * PART, PART)],
            rhs.at[pl.ds(slot * PART, PART)],
            rhs_sem.at[slot],
        )

    @pl.when(tile == 0)
    def _():
        for span in range(2):
            for slot, (side, row_options, column_options) in enumerate(slots):
                for row in row_options:
                    @pl.when(taken[slot][0] == row)
                    def _():
                        lhs_copy(slot, places[side, row], span).start()
                if span == 0:
                    for column in column_options:
                        @pl.when(taken[slot][1] == column)
                        def _():
                            rhs_copy(slot, column).start()
        for slot in range(len(slots)):
            @pl.when(taken[slot][0] < 0)
            def _():
                lhs[:, slot * PART:(slot + 1) * PART] = jnp.zeros((ROWS, PART), jnp.bfloat16)

    for span in range(2):
        @pl.when(tile == span)
        def _():
            for slot, (side, row_options, column_options) in enumerate(slots):
                if span == 0:
                    rhs_copy(slot, column_options[0]).wait()

                @pl.when(taken[slot][0] >= 0)
                def _():
                    lhs_copy(slot, places[side, row_options[0]], span).wait()

    product = jnp.dot(
        lhs[pl.ds(pl.multiple_of(tile * TILE, TILE), TILE), :], rhs[...],
        preferred_element_type=jnp.float32,
    )[:, :HALF]
    out[...] = product + total[...] if has_total else product


def multiply(stage, spot, arrays, columns, total=None):
    slots = slots_of(stage)
    depth = len(slots) * PART
    has_total = total is not None
    places = {key: at for key, at in PLACES.items() if ROW_STAGE[key[0]][key[1]] <= stage}
    kept = sorted({at[0] for at in places.values()})
    places = {key: (kept.index(at[0]), at[1]) for key, at in places.items()}
    arrays = [arrays[k] for k in kept]
    kept = [c for c in range(8) if COLUMN_STAGE[c] <= stage]
    column_places = {c: k for k, c in enumerate(kept)}
    columns = [columns[c] for c in kept]
    block = pl.BlockSpec((TILE, HALF), lambda i: (i, 0))
    anywhere = pl.BlockSpec(memory_space=pl.ANY)

    def kernel(*refs):
        multiply_kernel(slots, places, column_places, len(columns), has_total, *refs)

    return pl.pallas_call(
        kernel,
        grid=(ROWS // TILE,),
        out_shape=jax.ShapeDtypeStruct((BASIS, HALF), jnp.float32),
        in_specs=[pl.BlockSpec(memory_space=pltpu.SMEM)]
        + [anywhere] * (len(arrays) + len(columns)) + [block] * has_total,
        out_specs=block,
        scratch_shapes=[
            pltpu.VMEM((ROWS, depth), jnp.bfloat16),
            pltpu.VMEM((depth, COLS), jnp.bfloat16),
            pltpu.SemaphoreType.DMA((len(slots), 2)),
            pltpu.SemaphoreType.DMA((len(slots),)),
        ],
        compiler_params=pltpu.CompilerParams(vmem_limit_bytes=60 << 20),
        cost_estimate=pl.CostEstimate(
            flops=2 * BASIS * HALF * depth,
            bytes_accessed=2 * depth * (ROWS + COLS) + (1 + has_total) * 4 * BASIS * HALF,
            transcendentals=0,
        ),
    )(spot, *arrays, *columns, *([total] if has_total else []))


def body(half_slabs):
    spot = jnp.stack([lax.axis_index(a).astype(jnp.int32) for a in AXES])
    slab = jnp.transpose(half_slabs, (0, 2, 1)).reshape(PART, BASIS)
    a0, keep, give = prepare(spot, slab)

    c0, c0_cross, a1, b0, e0 = (
        send(keep, turn(False)), send(give, turn(True)), send(a0, Z_RING), send(a0, X_FAR), send(a0, CORES)
    )
    a3 = send(after(a0, e0), Z_BACK)
    c0, c0_cross, a1, a3, b0, e0 = lax.optimization_barrier((c0, c0_cross, a1, a3, b0, e0))
    c0 = jnp.concatenate([c0, c0_cross], axis=0)

    d0, c1, b1, e1 = (
        send(c0, X_NEAR), send(c0, Y_RING), send(b0, Z_RING), send(jnp.concatenate([a1, a3]), CORES)
    )
    c3, b3 = send(after(c0, e1), Y_BACK), send(after(b0, e1), Z_BACK)
    c2, a2 = send(c1, Y_RING), send(after(a1, b1), Z_RING)
    e2 = send(jnp.concatenate([b0, after(b1, d0)]), CORES)
    d0, c1, c2, c3, b1, b3, a2 = lax.optimization_barrier((d0, c1, c2, c3, b1, b3, a2))

    d1, d3, d2, b2 = send(d0, Y_RING), send(d0, Y_BACK), send(c2, X_NEAR), send(b1, Z_RING)
    e3 = send(jnp.concatenate([b3, a2]), CORES)
    total = multiply(0, spot, [a0, a1, a2, a3, b0, b1, None, b3, e0, e1, e2, e3, None], [c0, c1, c2, c3, d0, None, None, None])
    total, b2 = lax.optimization_barrier((total, b2))
    e4 = send(b2, CORES)
    arrays = [a0, a1, a2, a3, b0, b1, b2, b3, e0, e1, e2, e3, e4]
    return multiply(1, spot, arrays, [c0, c1, c2, c3, d0, d1, d2, d3], total)


def solution(mesh):
    fine = Mesh(mesh.devices.reshape(SIZES), AXES)
    return jax.shard_map(
        body,
        mesh=fine,
        in_specs=P("d", ("xl", "y"), ("xh", "z")),
        out_specs=P(("xl", "y"), ("xh", "z", "d")),
        check_vma=False,
    )
```

time: 157 us -> 151 us (0.962)
  Pallas kernels: 41.1 us -> 34.3 us
  starting transfers between devices: 26.5 us -> 32.5 us
  other arithmetic: 4.71 us -> 0.71 us
  local copies, waits for them, and re-layouts: 11.7 us -> 8.08 us
  waiting for transfers between devices: 72.5 us -> 74.9 us
    pallas_call x3 -> x2, Pallas kernels: 41.1 us -> 33.1 us  [multiply(): pl.pallas_call(kernel, grid=(ROWS // TILE,), out_shape=jax.ShapeDtypeStru...]
    ppermute x19 -> x21, starting transfers between devices: 26.5 us -> 32.5 us  [send(): return lax.ppermute(block, AXES, pairs)]
    unnamed x33, local copies, waits for them, and re-layouts: 3.97 us -> 7.95 us
    concatenate x2, other arithmetic: 4.23 us -> 0.47 us  [the longest x1 0.24 us: body(): e2 = send(jnp.concatenate([b0, after(b1, d0)]), CORES)]
    slice x2 -> x0, local copies, waits for them, and re-layouts: 3.28 us -> none  [the longest x1 2.16 us: body(): high = jnp.pad(turned[:, 750:], ((0, 0), (0, COLS - 750)))]
    ppermute x19 -> x21, waiting for transfers between devices: 72.5 us -> 74.9 us  [send(): return lax.ppermute(block, AXES, pairs)]
    reshape x1 -> x0, local copies, waits for them, and re-layouts: 2.4 us -> none  [body(): rows = jnp.transpose(half_slabs, (1, 0, 2)).reshape(1500, PART)]
    another operation x3 -> x1, local copies, waits for them, and re-layouts: 1.93 us -> 0.08 us  [body(): spot = jnp.stack([lax.axis_index(a).astype(jnp.int32) for a in AXES])]
  transfers between devices with their start and end apart: 19 -> 21, of which waited for: 10 -> 8; matrix products, arithmetic and copies ran while one was open for 3% -> 0% of each run, Pallas kernels for 19% -> 12%
where the time goes in v3:
time: 151 us
  waiting for transfers between devices  74.9 us (50%)
  Pallas kernels  34.3 us (23%)
  starting transfers between devices  32.5 us (22%)
  local copies, waits for them, and re-layouts  8.08 us (5%)
    ppermute x21, waiting for transfers between devices, send(): return lax.ppermute(block, AXES, pairs)  74.9 us
    pallas_call x2, Pallas kernels, multiply(): pl.pallas_call(kernel, grid=(ROWS // TILE,), out_shape=jax.ShapeDtypeStru...  33.1 us
    ppermute x21, starting transfers between devices, send(): return lax.ppermute(block, AXES, pairs)  32.5 us
    unnamed x33, local copies, waits for them, and re-layouts  7.95 us
  transfers between devices with their start and end apart: 21, of which 8 were waited for; matrix products, arithmetic and copies ran while one was open for 0% of the time, Pallas kernels for 12%

profile of v3, /device:TPU:1, one launch (start us, length us, event | category | flops | bytes accessed | tf_op | source)
XLA Modules:
  0.0 150.8 jit_solution(18408730043119057233)
XLA Ops:
  0.1 1.3 copy-done.1
  1.4 1.2 shard_map.17
  2.5 1.5 collective-permute-start.3
  4.1 2.8 %collective-permute-start.5 = (bf16[1536,384]{1,0:T(8,128)(2,1)S(1)}, bf16[1536,384]{1,0:T(8,128)(2,1)S(1)}, u32[]{:S(2)}, u32[]{:S(2)}) collective-permute-start(bf16[1536,384]{1,0:T(8,128)(2,1)S(1)} %get-tuple-element.31.refs_1_), channel_id=1, source_target_pairs={{0,8},{1,9},{2,10},{3,11},{4,12},{5,13},{6,14},{7,15},{8,0},{9,1},... | collective-permute-start | bytes 3538952 | tf_op jit(solution)/shard_map/ppermute | solution.py:53
  6.9 3.8 %collective-permute-start.2 = (bf16[1536,384]{1,0:T(8,128)(2,1)S(1)}, bf16[1536,384]{1,0:T(8,128)(2,1)S(1)}, u32[]{:S(2)}, u32[]{:S(2)}) collective-permute-start(bf16[1536,384]{1,0:T(8,128)(2,1)S(1)} %get-tuple-element.31.refs_1_), channel_id=1, source_target_pairs={{0,2},{1,7},{2,4},{3,1},{4,6},{5,3},{6,0},{7,5},{8,10},{9,15},{10,... | collective-permute-start | bytes 3538952 | tf_op jit(solution)/shard_map/ppermute | solution.py:53
  10.7 4.9 %collective-permute-start = (bf16[384,768]{1,0:T(8,128)(2,1)S(1)}, bf16[384,768]{1,0:T(8,128)(2,1)S(1)}, u32[]{:S(2)}, u32[]{:S(2)}) collective-permute-start(bf16[384,768]{1,0:T(8,128)(2,1)S(1)} %get-tuple-element.29), channel_id=1, source_target_pairs={{0,0},{1,97},{2,48},{3,81},{4,32},{5,65},{6,16},{7,113},{8,64},{9,... | collective-permute-start | bytes 1769480 | tf_op jit(solution)/shard_map/ppermute | solution.py:53
  15.6 33.4 %collective-permute-done = bf16[384,768]{1,0:T(8,128)(2,1)S(1)} collective-permute-done((bf16[384,768]{1,0:T(8,128)(2,1)S(1)}, bf16[384,768]{1,0:T(8,128)(2,1)S(1)}, u32[]{:S(2)}, u32[]{:S(2)}) %collective-permute-start) | collective-permute-done | bytes 589856 | tf_op jit(solution)/shard_map/ppermute | solution.py:53
  49.0 0.5 collective-permute-done.1
  49.5 0.6 collective-permute-done.4.refs_4_
  50.3 0.9 copy-done.5
  51.3 2.6 %collective-permute-start.11 = (bf16[1536,384]{1,0:T(8,128)(2,1)S(1)}, bf16[1536,384]{1,0:T(8,128)(2,1)S(1)}, u32[]{:S(2)}, u32[]{:S(2)}) collective-permute-start(bf16[1536,384]{1,0:T(8,128)(2,1)S(1)} %collective-permute-done.5.refs_5_), channel_id=1, source_target_pairs={{0,2},{1,7},{2,4},{3,1},{4,6},{5,3},{6,0},{7,5},{8,10},{9,15},{10,... | collective-permute-start | bytes 3538952 | tf_op jit(solution)/shard_map/ppermute | solution.py:53
  54.0 2.8 %collective-permute-start.7 = (bf16[768,768]{1,0:T(8,128)(2,1)S(1)}, bf16[768,768]{1,0:T(8,128)(2,1)S(1)}, u32[]{:S(2)}, u32[]{:S(2)}) collective-permute-start(bf16[768,768]{1,0:T(8,128)(2,1)S(1)} %constant_dynamic-update-slice_fusion.refs_12_.refs_14_), channel_id=1, source_target_pairs={{0,16},{1,49},{2,18},{3,51},{4,20},{5,53},{6,22},{7,55},{8,24},{9,... | collective-permute-start | bytes 3538952 | tf_op jit(solution)/shard_map/ppermute | solution.py:53
  56.8 0.3 collective-permute-start.6
  57.1 9.9 %collective-permute-done.11.refs_6_ = bf16[1536,384]{1,0:T(8,128)(2,1)S(1)} collective-permute-done((bf16[1536,384]{1,0:T(8,128)(2,1)S(1)}, bf16[1536,384]{1,0:T(8,128)(2,1)S(1)}, u32[]{:S(2)}, u32[]{:S(2)}) %collective-permute-start.11) | collective-permute-done | bytes 1179680 | tf_op jit(solution)/shard_map/ppermute | solution.py:53
  67.1 3.4 %collective-permute-start.13 = (bf16[1536,384]{1,0:T(8,128)(2,1)S(1)}, bf16[1536,384]{1,0:T(8,128)(2,1)S(1)}, u32[]{:S(2)}, u32[]{:S(2)}) collective-permute-start(bf16[1536,384]{1,0:T(8,128)(2,1)S(1)} %collective-permute-done.2.refs_2_), channel_id=1, source_target_pairs={{0,2},{1,7},{2,4},{3,1},{4,6},{5,3},{6,0},{7,5},{8,10},{9,15},{10,... | collective-permute-start | bytes 3538952 | tf_op jit(solution)/shard_map/ppermute | solution.py:53
  70.5 2.6 %collective-permute-start.8 = (bf16[768,768]{1,0:T(8,128)(2,1)S(1)}, bf16[768,768]{1,0:T(8,128)(2,1)}, u32[]{:S(2)}, u32[]{:S(2)}) collective-permute-start(bf16[768,768]{1,0:T(8,128)(2,1)S(1)} %collective-permute-done.7.refs_13_.refs_15_), channel_id=1, source_target_pairs={{0,16},{1,49},{2,18},{3,51},{4,20},{5,53},{6,22},{7,55},{8,24},{9,... | collective-permute-start | bytes 3538952 | tf_op jit(solution)/shard_map/ppermute | solution.py:53
  73.1 1.4 copy-done.10
  74.6 7.4 %collective-permute-done.6.refs_16_.refs_18_ = bf16[768,768]{1,0:T(8,128)(2,1)} collective-permute-done((bf16[768,768]{1,0:T(8,128)(2,1)S(1)}, bf16[768,768]{1,0:T(8,128)(2,1)}, u32[]{:S(2)}, u32[]{:S(2)}) %collective-permute-start.6) | collective-permute-done | bytes 1179680 | tf_op jit(solution)/shard_map/ppermute | solution.py:53
  82.3 15.3 %collective-permute-done.8.refs_14_.refs_16_ = bf16[768,768]{1,0:T(8,128)(2,1)} collective-permute-done((bf16[768,768]{1,0:T(8,128)(2,1)S(1)}, bf16[768,768]{1,0:T(8,128)(2,1)}, u32[]{:S(2)}, u32[]{:S(2)}) %collective-permute-start.8) | collective-permute-done | bytes 1179680 | tf_op jit(solution)/shard_map/ppermute | solution.py:53
  97.6 1.2 collective-permute-done.10.refs_15_.refs_17_
  98.7 1.0 copy-done.14
  100.0 0.8 copy-done.8
  100.8 0.5 collective-permute-start.15
  101.3 2.4 %collective-permute-start.16 = (bf16[1536,384]{1,0:T(8,128)(2,1)S(1)}, bf16[1536,384]{1,0:T(8,128)(2,1)}, u32[]{:S(2)}, u32[]{:S(2)}) collective-permute-start(bf16[1536,384]{1,0:T(8,128)(2,1)S(1)} %collective-permute-done.11.refs_6_), channel_id=1, source_target_pairs={{0,2},{1,7},{2,4},{3,1},{4,6},{5,3},{6,0},{7,5},{8,10},{9,15},{10,... | collective-permute-start | bytes 3538952 | tf_op jit(solution)/shard_map/ppermute | solution.py:53
  103.7 2.7 %collective-permute-start.18 = (bf16[768,768]{1,0:T(8,128)(2,1)}, bf16[768,768]{1,0:T(8,128)(2,1)}, u32[]{:S(2)}, u32[]{:S(2)}) collective-permute-start(bf16[768,768]{1,0:T(8,128)(2,1)} %collective-permute-done.6.refs_16_.refs_18_), channel_id=1, source_target_pairs={{0,16},{1,49},{2,18},{3,51},{4,20},{5,53},{6,22},{7,55},{8,24},{9,... | collective-permute-start | bytes 3538952 | tf_op jit(solution)/shard_map/ppermute | solution.py:53
  106.4 0.6 collective-permute-start.19
  107.0 1.4 copy-done.11
  108.4 17.4 %shard_map.18.refs_22_ = f32[1500,750]{1,0:T(8,128)} custom-call(s32[5]{0:T(128)} %copy-done.2, bf16[1536,384]{1,0:T(8,128)(2,1)} %copy-done, bf16[1536,384]{1,0:T(8,128)(2,1)} %copy-done.4, bf16[1536,384]{1,0:T(8,128)(2,1)} %copy-done.7, bf16[1536,384]{1,0:T(8,128)(2,1)} %copy-done.5, bf16[1536,384]{1,0:T(8,128)(2,1)} %copy-done.3, ...), custom_call_target="tpu_custom_call" | custom-call | flops 8640000000 | bytes 22194720 | tf_op jit(solution)/shard_map/pallas_call | solution.py:203
  125.8 1.4 collective-permute-start.17
  127.1 6.7 %collective-permute-done.19.refs_20_ = bf16[768,768]{1,0:T(8,128)(2,1)} collective-permute-done((bf16[768,768]{1,0:T(8,128)(2,1)}, bf16[768,768]{1,0:T(8,128)(2,1)}, u32[]{:S(2)}, u32[]{:S(2)}) %collective-permute-start.19) | collective-permute-done | bytes 1179680 | tf_op jit(solution)/shard_map/ppermute | solution.py:53
  133.9 1.0 copy-done.15
  134.9 15.7 %shard_map.19 = f32[1500,750]{1,0:T(8,128)} custom-call(s32[5]{0:T(128)} %copy-done.2, bf16[1536,384]{1,0:T(8,128)(2,1)} %copy-done, bf16[1536,384]{1,0:T(8,128)(2,1)} %copy-done.4, bf16[1536,384]{1,0:T(8,128)(2,1)} %copy-done.7, bf16[1536,384]{1,0:T(8,128)(2,1)} %copy-done.5, bf16[1536,384]{1,0:T(8,128)(2,1)} %copy-done.3, bf16[1536,384]{1,0:T(8,128)(2,1)} %copy-done.6, ...), custom_call_target="tpu_custom_call" | custom-call | flops 6912000000 | bytes 23155776 | tf_op jit(solution)/shard_map/pallas_call | solution.py:203
  (51 shorter events, 1.1 us)
Async XLA Ops:
  0.1 50.2 %copy-start.2 = (s32[5]{0:T(128)}, s32[5]{0:T(128)S(1)}, u32[]{:S(2)}) copy-start(s32[5]{0:T(128)S(1)} %stack.23.spot.refs_0_) | copy-start | bytes 64
  2.5 47.8 %copy-start = (bf16[1536,384]{1,0:T(8,128)(2,1)}, bf16[1536,384]{1,0:T(8,128)(2,1)S(1)}, u32[]{:S(2)}) copy-start(bf16[1536,384]{1,0:T(8,128)(2,1)S(1)} %get-tuple-element.31.refs_1_) | copy-start | bytes 3538948
  2.5 8.1 %collective-permute-start.3 = (bf16[1536,384]{1,0:T(8,128)(2,1)S(1)}, bf16[1536,384]{1,0:T(8,128)(2,1)S(1)}, u32[]{:S(2)}, u32[]{:S(2)}) collective-permute-start(bf16[1536,384]{1,0:T(8,128)(2,1)S(1)} %get-tuple-element.31.refs_1_), channel_id=1, source_target_pairs={{0,1},{1,0},{2,3},{3,2},{4,5},{5,4},{6,7},{7,6},{8,9},{9,8},{10,11... | collective-permute-start | bytes 3538952 | tf_op jit(solution)/shard_map/ppermute | solution.py:53
  4.1 45.4 %collective-permute-start.5 = (bf16[1536,384]{1,0:T(8,128)(2,1)S(1)}, bf16[1536,384]{1,0:T(8,128)(2,1)S(1)}, u32[]{:S(2)}, u32[]{:S(2)}) collective-permute-start(bf16[1536,384]{1,0:T(8,128)(2,1)S(1)} %get-tuple-element.31.refs_1_), channel_id=1, source_target_pairs={{0,8},{1,9},{2,10},{3,11},{4,12},{5,13},{6,14},{7,15},{8,0},{9,1},... | collective-permute-start | bytes 3538952 | tf_op jit(solution)/shard_map/ppermute | solution.py:53
  6.9 42.6 %collective-permute-start.2 = (bf16[1536,384]{1,0:T(8,128)(2,1)S(1)}, bf16[1536,384]{1,0:T(8,128)(2,1)S(1)}, u32[]{:S(2)}, u32[]{:S(2)}) collective-permute-start(bf16[1536,384]{1,0:T(8,128)(2,1)S(1)} %get-tuple-element.31.refs_1_), channel_id=1, source_target_pairs={{0,2},{1,7},{2,4},{3,1},{4,6},{5,3},{6,0},{7,5},{8,10},{9,15},{10,... | collective-permute-start | bytes 3538952 | tf_op jit(solution)/shard_map/ppermute | solution.py:53
  10.7 43.3 %copy-start.12 = (bf16[1536,384]{1,0:T(8,128)(2,1)}, bf16[1536,384]{1,0:T(8,128)(2,1)S(1)}, u32[]{:S(2)}) copy-start(bf16[1536,384]{1,0:T(8,128)(2,1)S(1)} %collective-permute-done.3.refs_8_.refs_9_) | copy-start | bytes 3538948
  10.7 39.4 %collective-permute-start.4 = (bf16[1536,384]{1,0:T(8,128)(2,1)S(1)}, bf16[1536,384]{1,0:T(8,128)(2,1)S(1)}, u32[]{:S(2)}, u32[]{:S(2)}) collective-permute-start(bf16[1536,384]{1,0:T(8,128)(2,1)S(1)} %get-tuple-element.31.refs_1_), channel_id=1, source_target_pairs={{0,6},{1,3},{2,0},{3,5},{4,2},{5,7},{6,4},{7,1},{8,14},{9,11},{10,... | collective-permute-start | bytes 3538952 | tf_op jit(solution)/shard_map/ppermute | solution.py:53
  10.7 38.3 %collective-permute-start = (bf16[384,768]{1,0:T(8,128)(2,1)S(1)}, bf16[384,768]{1,0:T(8,128)(2,1)S(1)}, u32[]{:S(2)}, u32[]{:S(2)}) collective-permute-start(bf16[384,768]{1,0:T(8,128)(2,1)S(1)} %get-tuple-element.29), channel_id=1, source_target_pairs={{0,0},{1,97},{2,48},{3,81},{4,32},{5,65},{6,16},{7,113},{8,64},{9,... | collective-permute-start | bytes 1769480 | tf_op jit(solution)/shard_map/ppermute | solution.py:53
  15.5 33.9 %collective-permute-start.1 = (bf16[384,768]{1,0:T(8,128)(2,1)S(1)}, bf16[384,768]{1,0:T(8,128)(2,1)S(1)}, u32[]{:S(2)}, u32[]{:S(2)}) collective-permute-start(bf16[384,768]{1,0:T(8,128)(2,1)S(1)} %get-tuple-element.30), channel_id=1, source_target_pairs={{0,97},{1,0},{2,81},{3,48},{4,65},{5,32},{6,113},{7,16},{8,33},{9,... | collective-permute-start | bytes 1769480 | tf_op jit(solution)/shard_map/ppermute | solution.py:53
  49.5 32.4 %copy-start.3 = (bf16[1536,384]{1,0:T(8,128)(2,1)}, bf16[1536,384]{1,0:T(8,128)(2,1)S(1)}, u32[]{:S(2)}) copy-start(bf16[1536,384]{1,0:T(8,128)(2,1)S(1)} %collective-permute-done.5.refs_5_) | copy-start | bytes 3538948
  49.5 17.6 %copy-start.4 = (bf16[1536,384]{1,0:T(8,128)(2,1)}, bf16[1536,384]{1,0:T(8,128)(2,1)S(1)}, u32[]{:S(2)}) copy-start(bf16[1536,384]{1,0:T(8,128)(2,1)S(1)} %collective-permute-done.2.refs_2_) | copy-start | bytes 3538948
  51.3 21.8 %collective-permute-start.9 = (bf16[3072,384]{1,0:T(8,128)(2,1)S(1)}, bf16[3072,384]{1,0:T(8,128)(2,1)S(1)}, u32[]{:S(2)}, u32[]{:S(2)}) collective-permute-start(bf16[3072,384]{1,0:T(8,128)(2,1)S(1)} %pad_maximum_fusion), channel_id=1, source_target_pairs={{0,1},{1,0},{2,3},{3,2},{4,5},{5,4},{6,7},{7,6},{8,9},{9,8},{10,11... | collective-permute-start | bytes 7077896 | tf_op jit(solution)/shard_map/ppermute | solution.py:53
  51.3 15.8 %collective-permute-start.11 = (bf16[1536,384]{1,0:T(8,128)(2,1)S(1)}, bf16[1536,384]{1,0:T(8,128)(2,1)S(1)}, u32[]{:S(2)}, u32[]{:S(2)}) collective-permute-start(bf16[1536,384]{1,0:T(8,128)(2,1)S(1)} %collective-permute-done.5.refs_5_), channel_id=1, source_target_pairs={{0,2},{1,7},{2,4},{3,1},{4,6},{5,3},{6,0},{7,5},{8,10},{9,15},{10,... | collective-permute-start | bytes 3538952 | tf_op jit(solution)/shard_map/ppermute | solution.py:53
  54.0 28.1 %copy-start.9 = (bf16[768,768]{1,0:T(8,128)(2,1)}, bf16[768,768]{1,0:T(8,128)(2,1)S(1)}, u32[]{:S(2)}) copy-start(bf16[768,768]{1,0:T(8,128)(2,1)S(1)} %constant_dynamic-update-slice_fusion.refs_12_.refs_14_) | copy-start | bytes 3538948
  54.0 16.5 %collective-permute-start.7 = (bf16[768,768]{1,0:T(8,128)(2,1)S(1)}, bf16[768,768]{1,0:T(8,128)(2,1)S(1)}, u32[]{:S(2)}, u32[]{:S(2)}) collective-permute-start(bf16[768,768]{1,0:T(8,128)(2,1)S(1)} %constant_dynamic-update-slice_fusion.refs_12_.refs_14_), channel_id=1, source_target_pairs={{0,16},{1,49},{2,18},{3,51},{4,20},{5,53},{6,22},{7,55},{8,24},{9,... | collective-permute-start | bytes 3538952 | tf_op jit(solution)/shard_map/ppermute | solution.py:53
  56.8 25.1 %collective-permute-start.6 = (bf16[768,768]{1,0:T(8,128)(2,1)S(1)}, bf16[768,768]{1,0:T(8,128)(2,1)}, u32[]{:S(2)}, u32[]{:S(2)}) collective-permute-start(bf16[768,768]{1,0:T(8,128)(2,1)S(1)} %constant_dynamic-update-slice_fusion.refs_12_.refs_14_), channel_id=1, source_target_pairs={{0,64},{1,65},{2,66},{3,67},{4,68},{5,69},{6,70},{7,71},{8,72},{9,... | collective-permute-start | bytes 3538952 | tf_op jit(solution)/shard_map/ppermute | solution.py:53
  67.1 34.3 %copy-start.6 = (bf16[1536,384]{1,0:T(8,128)(2,1)}, bf16[1536,384]{1,0:T(8,128)(2,1)S(1)}, u32[]{:S(2)}) copy-start(bf16[1536,384]{1,0:T(8,128)(2,1)S(1)} %collective-permute-done.11.refs_6_) | copy-start | bytes 3538948
  67.1 30.5 %collective-permute-start.13 = (bf16[1536,384]{1,0:T(8,128)(2,1)S(1)}, bf16[1536,384]{1,0:T(8,128)(2,1)S(1)}, u32[]{:S(2)}, u32[]{:S(2)}) collective-permute-start(bf16[1536,384]{1,0:T(8,128)(2,1)S(1)} %collective-permute-done.2.refs_2_), channel_id=1, source_target_pairs={{0,2},{1,7},{2,4},{3,1},{4,6},{5,3},{6,0},{7,5},{8,10},{9,15},{10,... | collective-permute-start | bytes 3538952 | tf_op jit(solution)/shard_map/ppermute | solution.py:53
  70.5 28.3 %copy-start.13 = (bf16[768,768]{1,0:T(8,128)(2,1)}, bf16[768,768]{1,0:T(8,128)(2,1)S(1)}, u32[]{:S(2)}) copy-start(bf16[768,768]{1,0:T(8,128)(2,1)S(1)} %collective-permute-done.7.refs_13_.refs_15_) | copy-start | bytes 3538948
  70.5 27.1 %collective-permute-start.8 = (bf16[768,768]{1,0:T(8,128)(2,1)S(1)}, bf16[768,768]{1,0:T(8,128)(2,1)}, u32[]{:S(2)}, u32[]{:S(2)}) collective-permute-start(bf16[768,768]{1,0:T(8,128)(2,1)S(1)} %collective-permute-done.7.refs_13_.refs_15_), channel_id=1, source_target_pairs={{0,16},{1,49},{2,18},{3,51},{4,20},{5,53},{6,22},{7,55},{8,24},{9,... | collective-permute-start | bytes 3538952 | tf_op jit(solution)/shard_map/ppermute | solution.py:53
  73.1 1.5 copy-start.10
  74.5 24.2 %collective-permute-start.10 = (bf16[768,768]{1,0:T(8,128)(2,1)S(1)}, bf16[768,768]{1,0:T(8,128)(2,1)S(1)}, u32[]{:S(2)}, u32[]{:S(2)}) collective-permute-start(bf16[768,768]{1,0:T(8,128)(2,1)S(1)} %constant_dynamic-update-slice_fusion.refs_12_.refs_14_), channel_id=1, source_target_pairs={{0,48},{1,17},{2,50},{3,19},{4,52},{5,21},{6,54},{7,23},{8,56},{9,... | collective-permute-start | bytes 3538952 | tf_op jit(solution)/shard_map/ppermute | solution.py:53
  74.5 25.2 %collective-permute-start.12 = (bf16[1536,384]{1,0:T(8,128)(2,1)S(1)}, bf16[1536,384]{1,0:T(8,128)(2,1)S(1)}, u32[]{:S(2)}, u32[]{:S(2)}) collective-permute-start(bf16[1536,384]{1,0:T(8,128)(2,1)S(1)} %collective-permute-done.5.refs_5_), channel_id=1, source_target_pairs={{0,6},{1,3},{2,0},{3,5},{4,2},{5,7},{6,4},{7,1},{8,14},{9,11},{10,... | collective-permute-start | bytes 3538952 | tf_op jit(solution)/shard_map/ppermute | solution.py:53
  82.2 24.3 %collective-permute-start.14 = (bf16[3072,384]{1,0:T(8,128)(2,1)S(1)}, bf16[3072,384]{1,0:T(8,128)(2,1)}, u32[]{:S(2)}, u32[]{:S(2)}) collective-permute-start(bf16[3072,384]{1,0:T(8,128)(2,1)S(1)} %pad_maximum_fusion.1), channel_id=1, source_target_pairs={{0,1},{1,0},{2,3},{3,2},{4,5},{5,4},{6,7},{7,6},{8,9},{9,8},{10,11... | collective-permute-start | bytes 7077896 | tf_op jit(solution)/shard_map/ppermute | solution.py:53
  97.6 2.4 %copy-start.7 = (bf16[1536,384]{1,0:T(8,128)(2,1)}, bf16[1536,384]{1,0:T(8,128)(2,1)S(1)}, u32[]{:S(2)}) copy-start(bf16[1536,384]{1,0:T(8,128)(2,1)S(1)} %collective-permute-done.13.refs_3_) | copy-start | bytes 3538948
  100.8 6.2 %collective-permute-start.15 = (bf16[3072,384]{1,0:T(8,128)(2,1)S(1)}, bf16[3072,384]{1,0:T(8,128)(2,1)S(1)}, u32[]{:S(2)}, u32[]{:S(2)}) collective-permute-start(bf16[3072,384]{1,0:T(8,128)(2,1)S(1)} %pad_maximum_fusion.2), channel_id=1, source_target_pairs={{0,1},{1,0},{2,3},{3,2},{4,5},{5,4},{6,7},{7,6},{8,9},{9,8},{10,11... | collective-permute-start | bytes 7077896 | tf_op jit(solution)/shard_map/ppermute | solution.py:53
  101.3 24.5 %collective-permute-start.16 = (bf16[1536,384]{1,0:T(8,128)(2,1)S(1)}, bf16[1536,384]{1,0:T(8,128)(2,1)}, u32[]{:S(2)}, u32[]{:S(2)}) collective-permute-start(bf16[1536,384]{1,0:T(8,128)(2,1)S(1)} %collective-permute-done.11.refs_6_), channel_id=1, source_target_pairs={{0,2},{1,7},{2,4},{3,1},{4,6},{5,3},{6,0},{7,5},{8,10},{9,15},{10,... | collective-permute-start | bytes 3538952 | tf_op jit(solution)/shard_map/ppermute | solution.py:53
  103.7 30.1 %collective-permute-start.20 = (bf16[768,768]{1,0:T(8,128)(2,1)}, bf16[768,768]{1,0:T(8,128)(2,1)}, u32[]{:S(2)}, u32[]{:S(2)}) collective-permute-start(bf16[768,768]{1,0:T(8,128)(2,1)} %collective-permute-done.6.refs_16_.refs_18_), channel_id=1, source_target_pairs={{0,48},{1,17},{2,50},{3,19},{4,52},{5,21},{6,54},{7,23},{8,56},{9,... | collective-permute-start | bytes 3538952 | tf_op jit(solution)/shard_map/ppermute | solution.py:53
  103.7 30.1 %collective-permute-start.18 = (bf16[768,768]{1,0:T(8,128)(2,1)}, bf16[768,768]{1,0:T(8,128)(2,1)}, u32[]{:S(2)}, u32[]{:S(2)}) collective-permute-start(bf16[768,768]{1,0:T(8,128)(2,1)} %collective-permute-done.6.refs_16_.refs_18_), channel_id=1, source_target_pairs={{0,16},{1,49},{2,18},{3,51},{4,20},{5,53},{6,22},{7,55},{8,24},{9,... | collective-permute-start | bytes 3538952 | tf_op jit(solution)/shard_map/ppermute | solution.py:53
  106.4 27.4 %collective-permute-start.19 = (bf16[768,768]{1,0:T(8,128)(2,1)}, bf16[768,768]{1,0:T(8,128)(2,1)}, u32[]{:S(2)}, u32[]{:S(2)}) collective-permute-start(bf16[768,768]{1,0:T(8,128)(2,1)} %collective-permute-done.8.refs_14_.refs_16_), channel_id=1, source_target_pairs={{0,64},{1,65},{2,66},{3,67},{4,68},{5,69},{6,70},{7,71},{8,72},{9,... | collective-permute-start | bytes 3538952 | tf_op jit(solution)/shard_map/ppermute | solution.py:53
  107.0 1.4 copy-start.11
  125.8 8.1 %collective-permute-start.17 = (bf16[1536,384]{1,0:T(8,128)(2,1)}, bf16[1536,384]{1,0:T(8,128)(2,1)S(1)}, u32[]{:S(2)}, u32[]{:S(2)}) collective-permute-start(bf16[1536,384]{1,0:T(8,128)(2,1)} %collective-permute-done.16.refs_7_), channel_id=1, source_target_pairs={{0,1},{1,0},{2,3},{3,2},{4,5},{5,4},{6,7},{7,6},{8,9},{9,8},{10,11... | collective-permute-start | bytes 3538952 | tf_op jit(solution)/shard_map/ppermute | solution.py:53
  (5 other events, 5.6 us)

commit v4 on v3

--- a/solution.py
+++ b/solution.py
@@ -82,7 +82,7 @@
         out_shape=[jax.ShapeDtypeStruct((ROWS, PART), jnp.bfloat16), half, half],
         in_specs=[pl.BlockSpec(memory_space=pltpu.SMEM), whole],
         out_specs=[whole] * 3,
-        compiler_params=pltpu.CompilerParams(vmem_limit_bytes=32 << 20),
+        compiler_params=pltpu.CompilerParams(vmem_limit_bytes=12 << 20),
     )(spot, slab)
 
 
@@ -213,7 +213,7 @@
             pltpu.SemaphoreType.DMA((len(slots), 2)),
             pltpu.SemaphoreType.DMA((len(slots),)),
         ],
-        compiler_params=pltpu.CompilerParams(vmem_limit_bytes=60 << 20),
+        compiler_params=pltpu.CompilerParams(vmem_limit_bytes=23 << 20),
         cost_estimate=pl.CostEstimate(
             flops=2 * BASIS * HALF * depth,
             bytes_accessed=2 * depth * (ROWS + COLS) + (1 + has_total) * 4 * BASIS * HALF,
@@ -237,10 +237,11 @@
     d0, c1, b1, e1 = (
         send(c0, X_NEAR), send(c0, Y_RING), send(b0, Z_RING), send(jnp.concatenate([a1, a3]), CORES)
     )
-    c3, b3 = send(after(c0, e1), Y_BACK), send(after(b0, e1), Z_BACK)
+    c3, b3 = send(c0, Y_BACK), send(b0, Z_BACK)
     c2, a2 = send(c1, Y_RING), send(after(a1, b1), Z_RING)
     e2 = send(jnp.concatenate([b0, after(b1, d0)]), CORES)
     d0, c1, c2, c3, b1, b3, a2 = lax.optimization_barrier((d0, c1, c2, c3, b1, b3, a2))
+
 
     d1, d3, d2, b2 = send(d0, Y_RING), send(d0, Y_BACK), send(c2, X_NEAR), send(b1, Z_RING)
     e3 = send(jnp.concatenate([b3, a2]), CORES)

time: 151 us -> 145 us (0.960)
  waiting for transfers between devices: 74.9 us -> 80.8 us
  local copies, waits for them, and re-layouts: 8.08 us -> 3.52 us
  Pallas kernels: 34.3 us -> 30 us
  starting transfers between devices: 32.5 us -> 28.9 us
    ppermute x21, waiting for transfers between devices: 74.9 us -> 80.8 us  [send(): return lax.ppermute(block, AXES, pairs)]
    unnamed x33 -> x5, local copies, waits for them, and re-layouts: 7.95 us -> 3.4 us
    pallas_call x2, Pallas kernels: 33.1 us -> 28.8 us  [multiply(): pl.pallas_call(kernel, grid=(ROWS // TILE,), out_shape=jax.ShapeDtypeStru...]
    ppermute x21, starting transfers between devices: 32.5 us -> 28.9 us  [send(): return lax.ppermute(block, AXES, pairs)]
  transfers between devices with their start and end apart: 21 -> 21, of which waited for: 8 -> 8; matrix products, arithmetic and copies ran while one was open for 0% -> 1% of each run, Pallas kernels for 12% -> 10%
where the time goes in v4:
time: 145 us; the launch traced here: 144 us
  waiting for transfers between devices  80.8 us (56%)
  Pallas kernels  30 us (21%)
  starting transfers between devices  28.9 us (20%)
  local copies, waits for them, and re-layouts  3.52 us (2%)
    ppermute x21, waiting for transfers between devices, send(): return lax.ppermute(block, AXES, pairs)  80.8 us
    ppermute x21, starting transfers between devices, send(): return lax.ppermute(block, AXES, pairs)  28.9 us
    pallas_call x2, Pallas kernels, multiply(): pl.pallas_call(kernel, grid=(ROWS // TILE,), out_shape=jax.ShapeDtypeStru...  28.8 us
    unnamed x5, local copies, waits for them, and re-layouts  3.4 us
  transfers between devices with their start and end apart: 21, of which 8 were waited for; matrix products, arithmetic and copies ran while one was open for 1% of the time, Pallas kernels for 10%

profile of v4, /device:TPU:1, one launch (start us, length us, event | category | flops | bytes accessed | tf_op | source)
XLA Modules:
  0.0 144.2 jit_solution(18307610497757511590)
XLA Ops:
  0.1 1.3 copy-done.1
  1.4 1.2 shard_map.17
  2.5 1.5 %collective-permute-start.3 = (bf16[1536,384]{1,0:T(8,128)(2,1)S(1)}, bf16[1536,384]{1,0:T(8,128)(2,1)S(1)}, u32[]{:S(2)}, u32[]{:S(2)}) collective-permute-start(bf16[1536,384]{1,0:T(8,128)(2,1)S(1)} %get-tuple-element.29.refs_1_), channel_id=1, source_target_pairs={{0,1},{1,0},{2,3},{3,2},{4,5},{5,4},{6,7},{7,6},{8,9},{9,8},{10,11... | collective-permute-start | bytes 3538952 | tf_op jit(solution)/shard_map/ppermute | solution.py:53
  4.0 2.8 %collective-permute-start.5 = (bf16[1536,384]{1,0:T(8,128)(2,1)S(1)}, bf16[1536,384]{1,0:T(8,128)(2,1)S(1)}, u32[]{:S(2)}, u32[]{:S(2)}) collective-permute-start(bf16[1536,384]{1,0:T(8,128)(2,1)S(1)} %get-tuple-element.29.refs_1_), channel_id=1, source_target_pairs={{0,8},{1,9},{2,10},{3,11},{4,12},{5,13},{6,14},{7,15},{8,0},{9,1},... | collective-permute-start | bytes 3538952 | tf_op jit(solution)/shard_map/ppermute | solution.py:53
  6.9 3.8 %collective-permute-start.2 = (bf16[1536,384]{1,0:T(8,128)(2,1)S(1)}, bf16[1536,384]{1,0:T(8,128)(2,1)S(1)}, u32[]{:S(2)}, u32[]{:S(2)}) collective-permute-start(bf16[1536,384]{1,0:T(8,128)(2,1)S(1)} %get-tuple-element.29.refs_1_), channel_id=1, source_target_pairs={{0,2},{1,7},{2,4},{3,1},{4,6},{5,3},{6,0},{7,5},{8,10},{9,15},{10,... | collective-permute-start | bytes 3538952 | tf_op jit(solution)/shard_map/ppermute | solution.py:53
  10.6 4.8 %collective-permute-start = (bf16[384,768]{1,0:T(8,128)(2,1)S(1)}, bf16[384,768]{1,0:T(8,128)(2,1)S(1)}, u32[]{:S(2)}, u32[]{:S(2)}) collective-permute-start(bf16[384,768]{1,0:T(8,128)(2,1)S(1)} %get-tuple-element.27), channel_id=1, source_target_pairs={{0,0},{1,97},{2,48},{3,81},{4,32},{5,65},{6,16},{7,113},{8,64},{9,... | collective-permute-start | bytes 1769480 | tf_op jit(solution)/shard_map/ppermute | solution.py:53
  15.6 33.4 %collective-permute-done = bf16[384,768]{1,0:T(8,128)(2,1)S(1)} collective-permute-done((bf16[384,768]{1,0:T(8,128)(2,1)S(1)}, bf16[384,768]{1,0:T(8,128)(2,1)S(1)}, u32[]{:S(2)}, u32[]{:S(2)}) %collective-permute-start) | collective-permute-done | bytes 589856 | tf_op jit(solution)/shard_map/ppermute | solution.py:53
  49.0 0.5 collective-permute-done.1
  49.5 0.6 collective-permute-done.4.refs_4_
  50.1 2.2 %collective-permute-start.10 = (bf16[1536,384]{1,0:T(8,128)(2,1)S(1)}, bf16[1536,384]{1,0:T(8,128)(2,1)S(1)}, u32[]{:S(2)}, u32[]{:S(2)}) collective-permute-start(bf16[1536,384]{1,0:T(8,128)(2,1)S(1)} %collective-permute-done.5.refs_5_), channel_id=1, source_target_pairs={{0,2},{1,7},{2,4},{3,1},{4,6},{5,3},{6,0},{7,5},{8,10},{9,15},{10,... | collective-permute-start | bytes 3538952 | tf_op jit(solution)/shard_map/ppermute | solution.py:53
  52.4 2.3 %collective-permute-start.7 = (bf16[768,768]{1,0:T(8,128)(2,1)S(1)}, bf16[768,768]{1,0:T(8,128)(2,1)S(1)}, u32[]{:S(2)}, u32[]{:S(2)}) collective-permute-start(bf16[768,768]{1,0:T(8,128)(2,1)S(1)} %constant_dynamic-update-slice_fusion.refs_12_.refs_14_), channel_id=1, source_target_pairs={{0,16},{1,49},{2,18},{3,51},{4,20},{5,53},{6,22},{7,55},{8,24},{9,... | collective-permute-start | bytes 3538952 | tf_op jit(solution)/shard_map/ppermute | solution.py:53
  54.6 0.3 collective-permute-start.6
  54.9 0.4 collective-permute-start.9
  55.4 16.6 %collective-permute-done.10.refs_6_ = bf16[1536,384]{1,0:T(8,128)(2,1)S(1)} collective-permute-done((bf16[1536,384]{1,0:T(8,128)(2,1)S(1)}, bf16[1536,384]{1,0:T(8,128)(2,1)S(1)}, u32[]{:S(2)}, u32[]{:S(2)}) %collective-permute-start.10) | collective-permute-done | bytes 1179680 | tf_op jit(solution)/shard_map/ppermute | solution.py:53
  72.0 6.4 %collective-permute-done.7.refs_13_.refs_15_ = bf16[768,768]{1,0:T(8,128)(2,1)S(1)} collective-permute-done((bf16[768,768]{1,0:T(8,128)(2,1)S(1)}, bf16[768,768]{1,0:T(8,128)(2,1)S(1)}, u32[]{:S(2)}, u32[]{:S(2)}) %collective-permute-start.7) | collective-permute-done | bytes 1179680 | tf_op jit(solution)/shard_map/ppermute | solution.py:53
  78.5 2.8 %collective-permute-start.8 = (bf16[768,768]{1,0:T(8,128)(2,1)S(1)}, bf16[768,768]{1,0:T(8,128)(2,1)S(1)}, u32[]{:S(2)}, u32[]{:S(2)}) collective-permute-start(bf16[768,768]{1,0:T(8,128)(2,1)S(1)} %collective-permute-done.7.refs_13_.refs_15_), channel_id=1, source_target_pairs={{0,16},{1,49},{2,18},{3,51},{4,20},{5,53},{6,22},{7,55},{8,24},{9,... | collective-permute-start | bytes 3538952 | tf_op jit(solution)/shard_map/ppermute | solution.py:53
  81.3 0.2 pad_maximum_fusion
  81.5 0.1 collective-permute-start.13
  81.6 0.2 pad_maximum_fusion.1
  81.9 0.6 collective-permute-start.14
  82.4 12.0 %collective-permute-done.8.refs_14_.refs_16_ = bf16[768,768]{1,0:T(8,128)(2,1)S(1)} collective-permute-done((bf16[768,768]{1,0:T(8,128)(2,1)S(1)}, bf16[768,768]{1,0:T(8,128)(2,1)S(1)}, u32[]{:S(2)}, u32[]{:S(2)}) %collective-permute-start.8) | collective-permute-done | bytes 1179680 | tf_op jit(solution)/shard_map/ppermute | solution.py:53
  94.4 2.2 %collective-permute-done.12.refs_3_ = bf16[1536,384]{1,0:T(8,128)(2,1)S(1)} collective-permute-done((bf16[1536,384]{1,0:T(8,128)(2,1)S(1)}, bf16[1536,384]{1,0:T(8,128)(2,1)S(1)}, u32[]{:S(2)}, u32[]{:S(2)}) %collective-permute-start.12) | collective-permute-done | bytes 1179680 | tf_op jit(solution)/shard_map/ppermute | solution.py:53
  96.6 0.2 pad_maximum_fusion.2
  96.8 1.0 collective-permute-start.15
  97.8 1.7 %collective-permute-start.16 = (bf16[1536,384]{1,0:T(8,128)(2,1)S(1)}, bf16[1536,384]{1,0:T(8,128)(2,1)S(1)}, u32[]{:S(2)}, u32[]{:S(2)}) collective-permute-start(bf16[1536,384]{1,0:T(8,128)(2,1)S(1)} %collective-permute-done.10.refs_6_), channel_id=1, source_target_pairs={{0,2},{1,7},{2,4},{3,1},{4,6},{5,3},{6,0},{7,5},{8,10},{9,15},{10,... | collective-permute-start | bytes 3538952 | tf_op jit(solution)/shard_map/ppermute | solution.py:53
  99.6 1.7 %collective-permute-start.20 = (bf16[768,768]{1,0:T(8,128)(2,1)S(1)}, bf16[768,768]{1,0:T(8,128)(2,1)S(1)}, u32[]{:S(2)}, u32[]{:S(2)}) collective-permute-start(bf16[768,768]{1,0:T(8,128)(2,1)S(1)} %collective-permute-done.6.refs_16_.refs_18_), channel_id=1, source_target_pairs={{0,48},{1,17},{2,50},{3,19},{4,52},{5,21},{6,54},{7,23},{8,56},{9,... | collective-permute-start | bytes 3538952 | tf_op jit(solution)/shard_map/ppermute | solution.py:53
  101.3 1.0 collective-permute-start.18
  102.3 1.7 %collective-permute-start.19 = (bf16[768,768]{1,0:T(8,128)(2,1)S(1)}, bf16[768,768]{1,0:T(8,128)(2,1)S(1)}, u32[]{:S(2)}, u32[]{:S(2)}) collective-permute-start(bf16[768,768]{1,0:T(8,128)(2,1)S(1)} %collective-permute-done.8.refs_14_.refs_16_), channel_id=1, source_target_pairs={{0,64},{1,65},{2,66},{3,67},{4,68},{5,69},{6,70},{7,71},{8,72},{9,... | collective-permute-start | bytes 3538952 | tf_op jit(solution)/shard_map/ppermute | solution.py:53
  104.0 14.6 %shard_map.18.refs_22_ = f32[1500,750]{1,0:T(8,128)S(1)} custom-call(s32[5]{0:T(128)S(1)} %stack.23.spot.refs_0_, bf16[1536,384]{1,0:T(8,128)(2,1)S(1)} %get-tuple-element.29.refs_1_, bf16[1536,384]{1,0:T(8,128)(2,1)S(1)} %collective-permute-done.2.refs_2_, bf16[1536,384]{1,0:T(8,128)(2,1)S(1)} %collective-permute-done.12.refs_3_, ...), custom_call_target="tpu_custom_call" | custom-call | flops 8640000000 | bytes 22194720 | tf_op jit(solution)/shard_map/pallas_call | solution.py:203
  118.7 2.1 %copy-done = f32[1500,750]{1,0:T(8,128)} copy-done((f32[1500,750]{1,0:T(8,128)}, f32[1500,750]{1,0:T(8,128)S(1)}, u32[]{:S(2)}) %copy-start) | copy-done | bytes 4500024
  120.8 9.1 %collective-permute-done.19.refs_20_ = bf16[768,768]{1,0:T(8,128)(2,1)S(1)} collective-permute-done((bf16[768,768]{1,0:T(8,128)(2,1)S(1)}, bf16[768,768]{1,0:T(8,128)(2,1)S(1)}, u32[]{:S(2)}, u32[]{:S(2)}) %collective-permute-start.19) | collective-permute-done | bytes 1179680 | tf_op jit(solution)/shard_map/ppermute | solution.py:53
  129.9 14.1 %shard_map.19 = f32[1500,750]{1,0:T(8,128)} custom-call(s32[5]{0:T(128)S(1)} %stack.23.spot.refs_0_, bf16[1536,384]{1,0:T(8,128)(2,1)S(1)} %get-tuple-element.29.refs_1_, bf16[1536,384]{1,0:T(8,128)(2,1)S(1)} %collective-permute-done.2.refs_2_, bf16[1536,384]{1,0:T(8,128)(2,1)S(1)} %collective-permute-done.12.refs_3_, ...), custom_call_target="tpu_custom_call" | custom-call | flops 6912000000 | bytes 23155776 | tf_op jit(solution)/shard_map/pallas_call | solution.py:203
  (23 shorter events, 0.3 us)
Async XLA Ops:
  0.1 1.3 copy-start.1
  2.5 8.1 %collective-permute-start.3 = (bf16[1536,384]{1,0:T(8,128)(2,1)S(1)}, bf16[1536,384]{1,0:T(8,128)(2,1)S(1)}, u32[]{:S(2)}, u32[]{:S(2)}) collective-permute-start(bf16[1536,384]{1,0:T(8,128)(2,1)S(1)} %get-tuple-element.29.refs_1_), channel_id=1, source_target_pairs={{0,1},{1,0},{2,3},{3,2},{4,5},{5,4},{6,7},{7,6},{8,9},{9,8},{10,11... | collective-permute-start | bytes 3538952 | tf_op jit(solution)/shard_map/ppermute | solution.py:53
  4.0 45.4 %collective-permute-start.5 = (bf16[1536,384]{1,0:T(8,128)(2,1)S(1)}, bf16[1536,384]{1,0:T(8,128)(2,1)S(1)}, u32[]{:S(2)}, u32[]{:S(2)}) collective-permute-start(bf16[1536,384]{1,0:T(8,128)(2,1)S(1)} %get-tuple-element.29.refs_1_), channel_id=1, source_target_pairs={{0,8},{1,9},{2,10},{3,11},{4,12},{5,13},{6,14},{7,15},{8,0},{9,1},... | collective-permute-start | bytes 3538952 | tf_op jit(solution)/shard_map/ppermute | solution.py:53
  6.9 42.6 %collective-permute-start.2 = (bf16[1536,384]{1,0:T(8,128)(2,1)S(1)}, bf16[1536,384]{1,0:T(8,128)(2,1)S(1)}, u32[]{:S(2)}, u32[]{:S(2)}) collective-permute-start(bf16[1536,384]{1,0:T(8,128)(2,1)S(1)} %get-tuple-element.29.refs_1_), channel_id=1, source_target_pairs={{0,2},{1,7},{2,4},{3,1},{4,6},{5,3},{6,0},{7,5},{8,10},{9,15},{10,... | collective-permute-start | bytes 3538952 | tf_op jit(solution)/shard_map/ppermute | solution.py:53
  10.6 39.4 %collective-permute-start.4 = (bf16[1536,384]{1,0:T(8,128)(2,1)S(1)}, bf16[1536,384]{1,0:T(8,128)(2,1)S(1)}, u32[]{:S(2)}, u32[]{:S(2)}) collective-permute-start(bf16[1536,384]{1,0:T(8,128)(2,1)S(1)} %get-tuple-element.29.refs_1_), channel_id=1, source_target_pairs={{0,6},{1,3},{2,0},{3,5},{4,2},{5,7},{6,4},{7,1},{8,14},{9,11},{10,... | collective-permute-start | bytes 3538952 | tf_op jit(solution)/shard_map/ppermute | solution.py:53
  10.6 38.3 %collective-permute-start = (bf16[384,768]{1,0:T(8,128)(2,1)S(1)}, bf16[384,768]{1,0:T(8,128)(2,1)S(1)}, u32[]{:S(2)}, u32[]{:S(2)}) collective-permute-start(bf16[384,768]{1,0:T(8,128)(2,1)S(1)} %get-tuple-element.27), channel_id=1, source_target_pairs={{0,0},{1,97},{2,48},{3,81},{4,32},{5,65},{6,16},{7,113},{8,64},{9,... | collective-permute-start | bytes 1769480 | tf_op jit(solution)/shard_map/ppermute | solution.py:53
  15.5 34.0 %collective-permute-start.1 = (bf16[384,768]{1,0:T(8,128)(2,1)S(1)}, bf16[384,768]{1,0:T(8,128)(2,1)S(1)}, u32[]{:S(2)}, u32[]{:S(2)}) collective-permute-start(bf16[384,768]{1,0:T(8,128)(2,1)S(1)} %get-tuple-element.28), channel_id=1, source_target_pairs={{0,97},{1,0},{2,81},{3,48},{4,65},{5,32},{6,113},{7,16},{8,33},{9,... | collective-permute-start | bytes 1769480 | tf_op jit(solution)/shard_map/ppermute | solution.py:53
  50.1 21.9 %collective-permute-start.10 = (bf16[1536,384]{1,0:T(8,128)(2,1)S(1)}, bf16[1536,384]{1,0:T(8,128)(2,1)S(1)}, u32[]{:S(2)}, u32[]{:S(2)}) collective-permute-start(bf16[1536,384]{1,0:T(8,128)(2,1)S(1)} %collective-permute-done.5.refs_5_), channel_id=1, source_target_pairs={{0,2},{1,7},{2,4},{3,1},{4,6},{5,3},{6,0},{7,5},{8,10},{9,15},{10,... | collective-permute-start | bytes 3538952 | tf_op jit(solution)/shard_map/ppermute | solution.py:53
  52.4 26.1 %collective-permute-start.7 = (bf16[768,768]{1,0:T(8,128)(2,1)S(1)}, bf16[768,768]{1,0:T(8,128)(2,1)S(1)}, u32[]{:S(2)}, u32[]{:S(2)}) collective-permute-start(bf16[768,768]{1,0:T(8,128)(2,1)S(1)} %constant_dynamic-update-slice_fusion.refs_12_.refs_14_), channel_id=1, source_target_pairs={{0,16},{1,49},{2,18},{3,51},{4,20},{5,53},{6,22},{7,55},{8,24},{9,... | collective-permute-start | bytes 3538952 | tf_op jit(solution)/shard_map/ppermute | solution.py:53
  54.6 26.9 %collective-permute-start.6 = (bf16[768,768]{1,0:T(8,128)(2,1)S(1)}, bf16[768,768]{1,0:T(8,128)(2,1)S(1)}, u32[]{:S(2)}, u32[]{:S(2)}) collective-permute-start(bf16[768,768]{1,0:T(8,128)(2,1)S(1)} %constant_dynamic-update-slice_fusion.refs_12_.refs_14_), channel_id=1, source_target_pairs={{0,64},{1,65},{2,66},{3,67},{4,68},{5,69},{6,70},{7,71},{8,72},{9,... | collective-permute-start | bytes 3538952 | tf_op jit(solution)/shard_map/ppermute | solution.py:53
  54.9 26.9 %collective-permute-start.9 = (bf16[768,768]{1,0:T(8,128)(2,1)S(1)}, bf16[768,768]{1,0:T(8,128)(2,1)S(1)}, u32[]{:S(2)}, u32[]{:S(2)}) collective-permute-start(bf16[768,768]{1,0:T(8,128)(2,1)S(1)} %constant_dynamic-update-slice_fusion.refs_12_.refs_14_), channel_id=1, source_target_pairs={{0,48},{1,17},{2,50},{3,19},{4,52},{5,21},{6,54},{7,23},{8,56},{9,... | collective-permute-start | bytes 3538952 | tf_op jit(solution)/shard_map/ppermute | solution.py:53
  55.4 27.0 %collective-permute-start.11 = (bf16[1536,384]{1,0:T(8,128)(2,1)S(1)}, bf16[1536,384]{1,0:T(8,128)(2,1)S(1)}, u32[]{:S(2)}, u32[]{:S(2)}) collective-permute-start(bf16[1536,384]{1,0:T(8,128)(2,1)S(1)} %collective-permute-done.5.refs_5_), channel_id=1, source_target_pairs={{0,6},{1,3},{2,0},{3,5},{4,2},{5,7},{6,4},{7,1},{8,14},{9,11},{10,... | collective-permute-start | bytes 3538952 | tf_op jit(solution)/shard_map/ppermute | solution.py:53
  78.5 15.9 %collective-permute-start.8 = (bf16[768,768]{1,0:T(8,128)(2,1)S(1)}, bf16[768,768]{1,0:T(8,128)(2,1)S(1)}, u32[]{:S(2)}, u32[]{:S(2)}) collective-permute-start(bf16[768,768]{1,0:T(8,128)(2,1)S(1)} %collective-permute-done.7.refs_13_.refs_15_), channel_id=1, source_target_pairs={{0,16},{1,49},{2,18},{3,51},{4,20},{5,53},{6,22},{7,55},{8,24},{9,... | collective-permute-start | bytes 3538952 | tf_op jit(solution)/shard_map/ppermute | solution.py:53
  81.2 15.3 %collective-permute-start.12 = (bf16[1536,384]{1,0:T(8,128)(2,1)S(1)}, bf16[1536,384]{1,0:T(8,128)(2,1)S(1)}, u32[]{:S(2)}, u32[]{:S(2)}) collective-permute-start(bf16[1536,384]{1,0:T(8,128)(2,1)S(1)} %collective-permute-done.2.refs_2_), channel_id=1, source_target_pairs={{0,2},{1,7},{2,4},{3,1},{4,6},{5,3},{6,0},{7,5},{8,10},{9,15},{10,... | collective-permute-start | bytes 3538952 | tf_op jit(solution)/shard_map/ppermute | solution.py:53
  81.5 19.8 %collective-permute-start.13 = (bf16[3072,384]{1,0:T(8,128)(2,1)S(1)}, bf16[3072,384]{1,0:T(8,128)(2,1)S(1)}, u32[]{:S(2)}, u32[]{:S(2)}) collective-permute-start(bf16[3072,384]{1,0:T(8,128)(2,1)S(1)} %pad_maximum_fusion), channel_id=1, source_target_pairs={{0,1},{1,0},{2,3},{3,2},{4,5},{5,4},{6,7},{7,6},{8,9},{9,8},{10,11... | collective-permute-start | bytes 7077896 | tf_op jit(solution)/shard_map/ppermute | solution.py:53
  81.9 20.4 %collective-permute-start.14 = (bf16[3072,384]{1,0:T(8,128)(2,1)S(1)}, bf16[3072,384]{1,0:T(8,128)(2,1)S(1)}, u32[]{:S(2)}, u32[]{:S(2)}) collective-permute-start(bf16[3072,384]{1,0:T(8,128)(2,1)S(1)} %pad_maximum_fusion.1), channel_id=1, source_target_pairs={{0,1},{1,0},{2,3},{3,2},{4,5},{5,4},{6,7},{7,6},{8,9},{9,8},{10,11... | collective-permute-start | bytes 7077896 | tf_op jit(solution)/shard_map/ppermute | solution.py:53
  96.8 7.2 %collective-permute-start.15 = (bf16[3072,384]{1,0:T(8,128)(2,1)S(1)}, bf16[3072,384]{1,0:T(8,128)(2,1)S(1)}, u32[]{:S(2)}, u32[]{:S(2)}) collective-permute-start(bf16[3072,384]{1,0:T(8,128)(2,1)S(1)} %pad_maximum_fusion.2), channel_id=1, source_target_pairs={{0,1},{1,0},{2,3},{3,2},{4,5},{5,4},{6,7},{7,6},{8,9},{9,8},{10,11... | collective-permute-start | bytes 7077896 | tf_op jit(solution)/shard_map/ppermute | solution.py:53
  97.8 22.9 %collective-permute-start.16 = (bf16[1536,384]{1,0:T(8,128)(2,1)S(1)}, bf16[1536,384]{1,0:T(8,128)(2,1)S(1)}, u32[]{:S(2)}, u32[]{:S(2)}) collective-permute-start(bf16[1536,384]{1,0:T(8,128)(2,1)S(1)} %collective-permute-done.10.refs_6_), channel_id=1, source_target_pairs={{0,2},{1,7},{2,4},{3,1},{4,6},{5,3},{6,0},{7,5},{8,10},{9,15},{10,... | collective-permute-start | bytes 3538952 | tf_op jit(solution)/shard_map/ppermute | solution.py:53
  99.6 30.3 %collective-permute-start.20 = (bf16[768,768]{1,0:T(8,128)(2,1)S(1)}, bf16[768,768]{1,0:T(8,128)(2,1)S(1)}, u32[]{:S(2)}, u32[]{:S(2)}) collective-permute-start(bf16[768,768]{1,0:T(8,128)(2,1)S(1)} %collective-permute-done.6.refs_16_.refs_18_), channel_id=1, source_target_pairs={{0,48},{1,17},{2,50},{3,19},{4,52},{5,21},{6,54},{7,23},{8,56},{9,... | collective-permute-start | bytes 3538952 | tf_op jit(solution)/shard_map/ppermute | solution.py:53
  101.3 28.5 %collective-permute-start.18 = (bf16[768,768]{1,0:T(8,128)(2,1)S(1)}, bf16[768,768]{1,0:T(8,128)(2,1)S(1)}, u32[]{:S(2)}, u32[]{:S(2)}) collective-permute-start(bf16[768,768]{1,0:T(8,128)(2,1)S(1)} %collective-permute-done.6.refs_16_.refs_18_), channel_id=1, source_target_pairs={{0,16},{1,49},{2,18},{3,51},{4,20},{5,53},{6,22},{7,55},{8,24},{9,... | collective-permute-start | bytes 3538952 | tf_op jit(solution)/shard_map/ppermute | solution.py:53
  102.3 27.6 %collective-permute-start.19 = (bf16[768,768]{1,0:T(8,128)(2,1)S(1)}, bf16[768,768]{1,0:T(8,128)(2,1)S(1)}, u32[]{:S(2)}, u32[]{:S(2)}) collective-permute-start(bf16[768,768]{1,0:T(8,128)(2,1)S(1)} %collective-permute-done.8.refs_14_.refs_16_), channel_id=1, source_target_pairs={{0,64},{1,65},{2,66},{3,67},{4,68},{5,69},{6,70},{7,71},{8,72},{9,... | collective-permute-start | bytes 3538952 | tf_op jit(solution)/shard_map/ppermute | solution.py:53
  118.7 2.1 %copy-start = (f32[1500,750]{1,0:T(8,128)}, f32[1500,750]{1,0:T(8,128)S(1)}, u32[]{:S(2)}) copy-start(f32[1500,750]{1,0:T(8,128)S(1)} %shard_map.18.refs_22_) | copy-start | bytes 13500004
  120.8 9.1 %collective-permute-start.17 = (bf16[1536,384]{1,0:T(8,128)(2,1)S(1)}, bf16[1536,384]{1,0:T(8,128)(2,1)S(1)}, u32[]{:S(2)}, u32[]{:S(2)}) collective-permute-start(bf16[1536,384]{1,0:T(8,128)(2,1)S(1)} %collective-permute-done.16.refs_7_), channel_id=1, source_target_pairs={{0,1},{1,0},{2,3},{3,2},{4,5},{5,4},{6,7},{7,6},{8,9},{9,8},{10,11... | collective-permute-start | bytes 3538952 | tf_op jit(solution)/shard_map/ppermute | solution.py:53

commit v5 on v4

--- a/solution.py
+++ b/solution.py
@@ -13,14 +13,14 @@
 SIZES = (2, 4, 2, 4, 2)
 BASIS, HALF = 1500, 750
 ROWS, COLS, PART = 1536, 768, 384
-TILE = 512
+TILE = 384
 
 ROW_STAGE = ((0, 0, 0, 0, 0, 0, 1, 0), (0, 0, 0, 0, 0, 0, 1, 0))
 COLUMN_STAGE = (0, 0, 0, 0, 0, 1, 1, 1)
 PLACES = {(0, row): (row, 0) for row in range(8)}
 PLACES.update({
-    (1, 0): (8, 0), (1, 1): (9, 0), (1, 3): (9, ROWS), (1, 4): (10, 0),
-    (1, 5): (10, ROWS), (1, 7): (11, 0), (1, 2): (11, ROWS), (1, 6): (12, 0),
+    (1, 0): (8, 0), (1, 1): (9, 0), (1, 2): (9, ROWS), (1, 3): (10, 0),
+    (1, 4): (10, ROWS), (1, 5): (11, 0), (1, 7): (11, ROWS), (1, 6): (12, 0),
 })
 
 
@@ -227,24 +227,24 @@
     slab = jnp.transpose(half_slabs, (0, 2, 1)).reshape(PART, BASIS)
     a0, keep, give = prepare(spot, slab)
 
-    c0, c0_cross, a1, b0, e0 = (
-        send(keep, turn(False)), send(give, turn(True)), send(a0, Z_RING), send(a0, X_FAR), send(a0, CORES)
+    c0, c0_cross, a1, e0 = (
+        send(keep, turn(False)), send(give, turn(True)), send(a0, Z_RING), send(a0, CORES)
     )
-    a3 = send(after(a0, e0), Z_BACK)
-    c0, c0_cross, a1, a3, b0, e0 = lax.optimization_barrier((c0, c0_cross, a1, a3, b0, e0))
+    own, c0, c0_cross, e0 = lax.optimization_barrier((a0, c0, c0_cross, e0))
     c0 = jnp.concatenate([c0, c0_cross], axis=0)
 
-    d0, c1, b1, e1 = (
-        send(c0, X_NEAR), send(c0, Y_RING), send(b0, Z_RING), send(jnp.concatenate([a1, a3]), CORES)
+    b0, c1, c3, a2, a3 = (
+        send(own, X_FAR), send(c0, Y_RING), send(c0, Y_BACK), send(after(a1, c0_cross), Z_RING), send(own, Z_BACK)
     )
-    c3, b3 = send(c0, Y_BACK), send(b0, Z_BACK)
-    c2, a2 = send(c1, Y_RING), send(after(a1, b1), Z_RING)
-    e2 = send(jnp.concatenate([b0, after(b1, d0)]), CORES)
-    d0, c1, c2, c3, b1, b3, a2 = lax.optimization_barrier((d0, c1, c2, c3, b1, b3, a2))
-
+    c0, b0, c1, c3, a2, a3 = lax.optimization_barrier((c0, b0, c1, c3, a2, a3))
+
+    d0, b1, c2 = send(c0, X_NEAR), send(b0, Z_RING), send(c1, Y_RING)
+    e1, e2 = send(jnp.concatenate([a1, a2]), CORES), send(jnp.concatenate([a3, b0]), CORES)
+    b3 = send(after(b0, e1), Z_BACK)
+    d0, b1, b3, c2, e1, e2 = lax.optimization_barrier((d0, b1, b3, c2, e1, e2))
 
     d1, d3, d2, b2 = send(d0, Y_RING), send(d0, Y_BACK), send(c2, X_NEAR), send(b1, Z_RING)
-    e3 = send(jnp.concatenate([b3, a2]), CORES)
+    e3 = send(jnp.concatenate([b1, b3]), CORES)
     total = multiply(0, spot, [a0, a1, a2, a3, b0, b1, None, b3, e0, e1, e2, e3, None], [c0, c1, c2, c3, d0, None, None, None])
     total, b2 = lax.optimization_barrier((total, b2))
     e4 = send(b2, CORES)

time: 145 us -> 141 us (0.972)
  waiting for transfers between devices: 80.8 us -> 74.4 us
  starting transfers between devices: 28.9 us -> 31.7 us
    ppermute x21, waiting for transfers between devices: 80.8 us -> 74.4 us  [send(): return lax.ppermute(block, AXES, pairs)]
    ppermute x21, starting transfers between devices: 28.9 us -> 31.7 us  [send(): return lax.ppermute(block, AXES, pairs)]
  transfers between devices with their start and end apart: 21 -> 21, of which waited for: 8 -> 8; matrix products, arithmetic and copies ran while one was open for 1% -> 0% of each run, Pallas kernels for 10% -> 11%
where the time goes in v5:
time: 141 us
  waiting for transfers between devices  74.4 us (53%)
  starting transfers between devices  31.7 us (22%)
  Pallas kernels  30.3 us (21%)
  local copies, waits for them, and re-layouts  3.52 us (2%)
    ppermute x21, waiting for transfers between devices, send(): return lax.ppermute(block, AXES, pairs)  74.4 us
    ppermute x21, starting transfers between devices, send(): return lax.ppermute(block, AXES, pairs)  31.7 us
    pallas_call x2, Pallas kernels, multiply(): pl.pallas_call(kernel, grid=(ROWS // TILE,), out_shape=jax.ShapeDtypeStru...  29.1 us
    unnamed x5, local copies, waits for them, and re-layouts  3.4 us
  transfers between devices with their start and end apart: 21, of which 8 were waited for; matrix products, arithmetic and copies ran while one was open for 0% of the time, Pallas kernels for 11%

profile of v5, /device:TPU:1, one launch (start us, length us, event | category | flops | bytes accessed | tf_op | source)
XLA Modules:
  0.0 140.9 jit_solution(10968887304604165644)
XLA Ops:
  0.0 0.1 stack.23.spot.refs_0_
  0.1 1.3 copy-done.1
  1.4 1.2 shard_map.17
  2.5 1.5 %collective-permute-start.3 = (bf16[1536,384]{1,0:T(8,128)(2,1)S(1)}, bf16[1536,384]{1,0:T(8,128)(2,1)S(1)}, u32[]{:S(2)}, u32[]{:S(2)}) collective-permute-start(bf16[1536,384]{1,0:T(8,128)(2,1)S(1)} %get-tuple-element.33.refs_1_), channel_id=1, source_target_pairs={{0,1},{1,0},{2,3},{3,2},{4,5},{5,4},{6,7},{7,6},{8,9},{9,8},{10,11... | collective-permute-start | bytes 3538952 | tf_op jit(solution)/shard_map/ppermute | solution.py:53
  4.0 3.8 %collective-permute-start = (bf16[1536,384]{1,0:T(8,128)(2,1)S(1)}, bf16[1536,384]{1,0:T(8,128)(2,1)S(1)}, u32[]{:S(2)}, u32[]{:S(2)}) collective-permute-start(bf16[1536,384]{1,0:T(8,128)(2,1)S(1)} %get-tuple-element.33.refs_1_), channel_id=1, source_target_pairs={{0,2},{1,7},{2,4},{3,1},{4,6},{5,3},{6,0},{7,5},{8,10},{9,15},{10,... | collective-permute-start | bytes 3538952 | tf_op jit(solution)/shard_map/ppermute | solution.py:53
  7.9 5.7 %collective-permute-start.1 = (bf16[384,768]{1,0:T(8,128)(2,1)S(1)}, bf16[384,768]{1,0:T(8,128)(2,1)S(1)}, u32[]{:S(2)}, u32[]{:S(2)}) collective-permute-start(bf16[384,768]{1,0:T(8,128)(2,1)S(1)} %get-tuple-element.29), channel_id=1, source_target_pairs={{0,0},{1,97},{2,48},{3,81},{4,32},{5,65},{6,16},{7,113},{8,64},{9,... | collective-permute-start | bytes 1769480 | tf_op jit(solution)/shard_map/ppermute | solution.py:53
  13.6 0.1 collective-permute-start.2
  13.7 11.1 %collective-permute-done.1 = bf16[384,768]{1,0:T(8,128)(2,1)S(1)} collective-permute-done((bf16[384,768]{1,0:T(8,128)(2,1)S(1)}, bf16[384,768]{1,0:T(8,128)(2,1)S(1)}, u32[]{:S(2)}, u32[]{:S(2)}) %collective-permute-start.1) | collective-permute-done | bytes 589856 | tf_op jit(solution)/shard_map/ppermute | solution.py:53
  24.8 4.0 %collective-permute-done.2 = bf16[384,768]{1,0:T(8,128)(2,1)S(1)} collective-permute-done((bf16[384,768]{1,0:T(8,128)(2,1)S(1)}, bf16[384,768]{1,0:T(8,128)(2,1)S(1)}, u32[]{:S(2)}, u32[]{:S(2)}) %collective-permute-start.2) | collective-permute-done | bytes 589856 | tf_op jit(solution)/shard_map/ppermute | solution.py:53
  29.0 0.7 collective-permute-start.6
  29.7 3.9 %collective-permute-start.5 = (bf16[768,768]{1,0:T(8,128)(2,1)S(1)}, bf16[768,768]{1,0:T(8,128)(2,1)S(1)}, u32[]{:S(2)}, u32[]{:S(2)}) collective-permute-start(bf16[768,768]{1,0:T(8,128)(2,1)S(1)} %constant_dynamic-update-slice_fusion.refs_12_.refs_14_), channel_id=1, source_target_pairs={{0,16},{1,49},{2,18},{3,51},{4,20},{5,53},{6,22},{7,55},{8,24},{9,... | collective-permute-start | bytes 3538952 | tf_op jit(solution)/shard_map/ppermute | solution.py:53
  33.6 1.2 collective-permute-start.4
  34.9 2.7 %collective-permute-start.7 = (bf16[1536,384]{1,0:T(8,128)(2,1)S(1)}, bf16[1536,384]{1,0:T(8,128)(2,1)S(1)}, u32[]{:S(2)}, u32[]{:S(2)}) collective-permute-start(bf16[1536,384]{1,0:T(8,128)(2,1)S(1)} %collective-permute-done.refs_2_), channel_id=1, source_target_pairs={{0,2},{1,7},{2,4},{3,1},{4,6},{5,3},{6,0},{7,5},{8,10},{9,15},{10,... | collective-permute-start | bytes 3538952 | tf_op jit(solution)/shard_map/ppermute | solution.py:53
  37.5 19.6 %collective-permute-done.6.refs_15_.refs_17_ = bf16[768,768]{1,0:T(8,128)(2,1)S(1)} collective-permute-done((bf16[768,768]{1,0:T(8,128)(2,1)S(1)}, bf16[768,768]{1,0:T(8,128)(2,1)S(1)}, u32[]{:S(2)}, u32[]{:S(2)}) %collective-permute-start.6) | collective-permute-done | bytes 1179680 | tf_op jit(solution)/shard_map/ppermute | solution.py:53
  57.2 5.6 %collective-permute-done.7.refs_3_ = bf16[1536,384]{1,0:T(8,128)(2,1)S(1)} collective-permute-done((bf16[1536,384]{1,0:T(8,128)(2,1)S(1)}, bf16[1536,384]{1,0:T(8,128)(2,1)S(1)}, u32[]{:S(2)}, u32[]{:S(2)}) %collective-permute-start.7) | collective-permute-done | bytes 1179680 | tf_op jit(solution)/shard_map/ppermute | solution.py:53
  62.8 0.2 pad_maximum_fusion
  63.1 1.0 collective-permute-start.11
  64.1 0.2 pad_maximum_fusion.1
  64.3 0.1 collective-permute-start.14
  64.4 3.5 %collective-permute-start.10 = (bf16[1536,384]{1,0:T(8,128)(2,1)S(1)}, bf16[1536,384]{1,0:T(8,128)(2,1)S(1)}, u32[]{:S(2)}, u32[]{:S(2)}) collective-permute-start(bf16[1536,384]{1,0:T(8,128)(2,1)S(1)} %collective-permute-done.4.refs_5_), channel_id=1, source_target_pairs={{0,2},{1,7},{2,4},{3,1},{4,6},{5,3},{6,0},{7,5},{8,10},{9,15},{10,... | collective-permute-start | bytes 3538952 | tf_op jit(solution)/shard_map/ppermute | solution.py:53
  67.9 2.0 %collective-permute-start.13 = (bf16[768,768]{1,0:T(8,128)(2,1)S(1)}, bf16[768,768]{1,0:T(8,128)(2,1)S(1)}, u32[]{:S(2)}, u32[]{:S(2)}) collective-permute-start(bf16[768,768]{1,0:T(8,128)(2,1)S(1)} %collective-permute-done.5.refs_13_.refs_15_), channel_id=1, source_target_pairs={{0,16},{1,49},{2,18},{3,51},{4,20},{5,53},{6,22},{7,55},{8,24},{9,... | collective-permute-start | bytes 3538952 | tf_op jit(solution)/shard_map/ppermute | solution.py:53
  69.9 24.3 %collective-permute-done.9.refs_16_.refs_18_ = bf16[768,768]{1,0:T(8,128)(2,1)S(1)} collective-permute-done((bf16[768,768]{1,0:T(8,128)(2,1)S(1)}, bf16[768,768]{1,0:T(8,128)(2,1)S(1)}, u32[]{:S(2)}, u32[]{:S(2)}) %collective-permute-start.9) | collective-permute-done | bytes 1179680 | tf_op jit(solution)/shard_map/ppermute | solution.py:53
  94.1 0.6 collective-permute-done.12.refs_7_.refs_8_
  94.7 0.2 pad_maximum_fusion.2
  95.0 0.1 collective-permute-start.15
  95.0 2.7 %collective-permute-start.16 = (bf16[1536,384]{1,0:T(8,128)(2,1)S(1)}, bf16[1536,384]{1,0:T(8,128)(2,1)S(1)}, u32[]{:S(2)}, u32[]{:S(2)}) collective-permute-start(bf16[1536,384]{1,0:T(8,128)(2,1)S(1)} %collective-permute-done.10.refs_6_), channel_id=1, source_target_pairs={{0,2},{1,7},{2,4},{3,1},{4,6},{5,3},{6,0},{7,5},{8,10},{9,15},{10,... | collective-permute-start | bytes 3538952 | tf_op jit(solution)/shard_map/ppermute | solution.py:53
  97.8 2.7 %collective-permute-start.18 = (bf16[768,768]{1,0:T(8,128)(2,1)S(1)}, bf16[768,768]{1,0:T(8,128)(2,1)S(1)}, u32[]{:S(2)}, u32[]{:S(2)}) collective-permute-start(bf16[768,768]{1,0:T(8,128)(2,1)S(1)} %collective-permute-done.9.refs_16_.refs_18_), channel_id=1, source_target_pairs={{0,16},{1,49},{2,18},{3,51},{4,20},{5,53},{6,22},{7,55},{8,24},{9,... | collective-permute-start | bytes 3538952 | tf_op jit(solution)/shard_map/ppermute | solution.py:53
  100.5 14.9 %shard_map.18.refs_22_ = f32[1500,750]{1,0:T(8,128)S(1)} custom-call(s32[5]{0:T(128)S(1)} %stack.23.spot.refs_0_, bf16[1536,384]{1,0:T(8,128)(2,1)S(1)} %get-tuple-element.33.refs_1_, bf16[1536,384]{1,0:T(8,128)(2,1)S(1)} %collective-permute-done.refs_2_, bf16[1536,384]{1,0:T(8,128)(2,1)S(1)} %collective-permute-done.7.refs_3_, ...), custom_call_target="tpu_custom_call" | custom-call | flops 8640000000 | bytes 22194720 | tf_op jit(solution)/shard_map/pallas_call | solution.py:203
  115.4 2.1 %copy-done = f32[1500,750]{1,0:T(8,128)} copy-done((f32[1500,750]{1,0:T(8,128)}, f32[1500,750]{1,0:T(8,128)S(1)}, u32[]{:S(2)}) %copy-start) | copy-done | bytes 4500024
  117.5 8.7 %collective-permute-done.19.refs_20_ = bf16[768,768]{1,0:T(8,128)(2,1)S(1)} collective-permute-done((bf16[768,768]{1,0:T(8,128)(2,1)S(1)}, bf16[768,768]{1,0:T(8,128)(2,1)S(1)}, u32[]{:S(2)}, u32[]{:S(2)}) %collective-permute-start.19) | collective-permute-done | bytes 1179680 | tf_op jit(solution)/shard_map/ppermute | solution.py:53
  126.2 0.3 collective-permute-done.20.refs_21_
  126.6 14.2 %shard_map.19 = f32[1500,750]{1,0:T(8,128)} custom-call(s32[5]{0:T(128)S(1)} %stack.23.spot.refs_0_, bf16[1536,384]{1,0:T(8,128)(2,1)S(1)} %get-tuple-element.33.refs_1_, bf16[1536,384]{1,0:T(8,128)(2,1)S(1)} %collective-permute-done.refs_2_, bf16[1536,384]{1,0:T(8,128)(2,1)S(1)} %collective-permute-done.7.refs_3_, ...), custom_call_target="tpu_custom_call" | custom-call | flops 6912000000 | bytes 23155776 | tf_op jit(solution)/shard_map/pallas_call | solution.py:203
  (23 shorter events, 0.1 us)
Async XLA Ops:
  0.1 1.3 copy-start.1
  2.5 26.4 %collective-permute-start.3 = (bf16[1536,384]{1,0:T(8,128)(2,1)S(1)}, bf16[1536,384]{1,0:T(8,128)(2,1)S(1)}, u32[]{:S(2)}, u32[]{:S(2)}) collective-permute-start(bf16[1536,384]{1,0:T(8,128)(2,1)S(1)} %get-tuple-element.33.refs_1_), channel_id=1, source_target_pairs={{0,1},{1,0},{2,3},{3,2},{4,5},{5,4},{6,7},{7,6},{8,9},{9,8},{10,11... | collective-permute-start | bytes 3538952 | tf_op jit(solution)/shard_map/ppermute | solution.py:53
  4.0 30.8 %collective-permute-start = (bf16[1536,384]{1,0:T(8,128)(2,1)S(1)}, bf16[1536,384]{1,0:T(8,128)(2,1)S(1)}, u32[]{:S(2)}, u32[]{:S(2)}) collective-permute-start(bf16[1536,384]{1,0:T(8,128)(2,1)S(1)} %get-tuple-element.33.refs_1_), channel_id=1, source_target_pairs={{0,2},{1,7},{2,4},{3,1},{4,6},{5,3},{6,0},{7,5},{8,10},{9,15},{10,... | collective-permute-start | bytes 3538952 | tf_op jit(solution)/shard_map/ppermute | solution.py:53
  7.9 17.0 %collective-permute-start.1 = (bf16[384,768]{1,0:T(8,128)(2,1)S(1)}, bf16[384,768]{1,0:T(8,128)(2,1)S(1)}, u32[]{:S(2)}, u32[]{:S(2)}) collective-permute-start(bf16[384,768]{1,0:T(8,128)(2,1)S(1)} %get-tuple-element.29), channel_id=1, source_target_pairs={{0,0},{1,97},{2,48},{3,81},{4,32},{5,65},{6,16},{7,113},{8,64},{9,... | collective-permute-start | bytes 1769480 | tf_op jit(solution)/shard_map/ppermute | solution.py:53
  13.6 15.3 %collective-permute-start.2 = (bf16[384,768]{1,0:T(8,128)(2,1)S(1)}, bf16[384,768]{1,0:T(8,128)(2,1)S(1)}, u32[]{:S(2)}, u32[]{:S(2)}) collective-permute-start(bf16[384,768]{1,0:T(8,128)(2,1)S(1)} %get-tuple-element.30), channel_id=1, source_target_pairs={{0,97},{1,0},{2,81},{3,48},{4,65},{5,32},{6,113},{7,16},{8,33},{9,... | collective-permute-start | bytes 1769480 | tf_op jit(solution)/shard_map/ppermute | solution.py:53
  29.0 28.2 %collective-permute-start.6 = (bf16[768,768]{1,0:T(8,128)(2,1)S(1)}, bf16[768,768]{1,0:T(8,128)(2,1)S(1)}, u32[]{:S(2)}, u32[]{:S(2)}) collective-permute-start(bf16[768,768]{1,0:T(8,128)(2,1)S(1)} %constant_dynamic-update-slice_fusion.refs_12_.refs_14_), channel_id=1, source_target_pairs={{0,48},{1,17},{2,50},{3,19},{4,52},{5,21},{6,54},{7,23},{8,56},{9,... | collective-permute-start | bytes 3538952 | tf_op jit(solution)/shard_map/ppermute | solution.py:53
  29.7 27.5 %collective-permute-start.5 = (bf16[768,768]{1,0:T(8,128)(2,1)S(1)}, bf16[768,768]{1,0:T(8,128)(2,1)S(1)}, u32[]{:S(2)}, u32[]{:S(2)}) collective-permute-start(bf16[768,768]{1,0:T(8,128)(2,1)S(1)} %constant_dynamic-update-slice_fusion.refs_12_.refs_14_), channel_id=1, source_target_pairs={{0,16},{1,49},{2,18},{3,51},{4,20},{5,53},{6,22},{7,55},{8,24},{9,... | collective-permute-start | bytes 3538952 | tf_op jit(solution)/shard_map/ppermute | solution.py:53
  33.6 23.6 %collective-permute-start.8 = (bf16[1536,384]{1,0:T(8,128)(2,1)S(1)}, bf16[1536,384]{1,0:T(8,128)(2,1)S(1)}, u32[]{:S(2)}, u32[]{:S(2)}) collective-permute-start(bf16[1536,384]{1,0:T(8,128)(2,1)S(1)} %get-tuple-element.33.refs_1_), channel_id=1, source_target_pairs={{0,6},{1,3},{2,0},{3,5},{4,2},{5,7},{6,4},{7,1},{8,14},{9,11},{10,... | collective-permute-start | bytes 3538952 | tf_op jit(solution)/shard_map/ppermute | solution.py:53
  33.6 23.6 %collective-permute-start.4 = (bf16[1536,384]{1,0:T(8,128)(2,1)S(1)}, bf16[1536,384]{1,0:T(8,128)(2,1)S(1)}, u32[]{:S(2)}, u32[]{:S(2)}) collective-permute-start(bf16[1536,384]{1,0:T(8,128)(2,1)S(1)} %get-tuple-element.33.refs_1_), channel_id=1, source_target_pairs={{0,8},{1,9},{2,10},{3,11},{4,12},{5,13},{6,14},{7,15},{8,0},{9,1},... | collective-permute-start | bytes 3538952 | tf_op jit(solution)/shard_map/ppermute | solution.py:53
  34.9 28.0 %collective-permute-start.7 = (bf16[1536,384]{1,0:T(8,128)(2,1)S(1)}, bf16[1536,384]{1,0:T(8,128)(2,1)S(1)}, u32[]{:S(2)}, u32[]{:S(2)}) collective-permute-start(bf16[1536,384]{1,0:T(8,128)(2,1)S(1)} %collective-permute-done.refs_2_), channel_id=1, source_target_pairs={{0,2},{1,7},{2,4},{3,1},{4,6},{5,3},{6,0},{7,5},{8,10},{9,15},{10,... | collective-permute-start | bytes 3538952 | tf_op jit(solution)/shard_map/ppermute | solution.py:53
  63.1 6.8 %collective-permute-start.11 = (bf16[3072,384]{1,0:T(8,128)(2,1)S(1)}, bf16[3072,384]{1,0:T(8,128)(2,1)S(1)}, u32[]{:S(2)}, u32[]{:S(2)}) collective-permute-start(bf16[3072,384]{1,0:T(8,128)(2,1)S(1)} %pad_maximum_fusion), channel_id=1, source_target_pairs={{0,1},{1,0},{2,3},{3,2},{4,5},{5,4},{6,7},{7,6},{8,9},{9,8},{10,11... | collective-permute-start | bytes 7077896 | tf_op jit(solution)/shard_map/ppermute | solution.py:53
  64.3 29.8 %collective-permute-start.14 = (bf16[3072,384]{1,0:T(8,128)(2,1)S(1)}, bf16[3072,384]{1,0:T(8,128)(2,1)S(1)}, u32[]{:S(2)}, u32[]{:S(2)}) collective-permute-start(bf16[3072,384]{1,0:T(8,128)(2,1)S(1)} %pad_maximum_fusion.1), channel_id=1, source_target_pairs={{0,1},{1,0},{2,3},{3,2},{4,5},{5,4},{6,7},{7,6},{8,9},{9,8},{10,11... | collective-permute-start | bytes 7077896 | tf_op jit(solution)/shard_map/ppermute | solution.py:53
  64.4 29.7 %collective-permute-start.10 = (bf16[1536,384]{1,0:T(8,128)(2,1)S(1)}, bf16[1536,384]{1,0:T(8,128)(2,1)S(1)}, u32[]{:S(2)}, u32[]{:S(2)}) collective-permute-start(bf16[1536,384]{1,0:T(8,128)(2,1)S(1)} %collective-permute-done.4.refs_5_), channel_id=1, source_target_pairs={{0,2},{1,7},{2,4},{3,1},{4,6},{5,3},{6,0},{7,5},{8,10},{9,15},{10,... | collective-permute-start | bytes 3538952 | tf_op jit(solution)/shard_map/ppermute | solution.py:53
  67.9 26.3 %collective-permute-start.9 = (bf16[768,768]{1,0:T(8,128)(2,1)S(1)}, bf16[768,768]{1,0:T(8,128)(2,1)S(1)}, u32[]{:S(2)}, u32[]{:S(2)}) collective-permute-start(bf16[768,768]{1,0:T(8,128)(2,1)S(1)} %constant_dynamic-update-slice_fusion.refs_12_.refs_14_), channel_id=1, source_target_pairs={{0,64},{1,65},{2,66},{3,67},{4,68},{5,69},{6,70},{7,71},{8,72},{9,... | collective-permute-start | bytes 3538952 | tf_op jit(solution)/shard_map/ppermute | solution.py:53
  67.9 26.3 %collective-permute-start.13 = (bf16[768,768]{1,0:T(8,128)(2,1)S(1)}, bf16[768,768]{1,0:T(8,128)(2,1)S(1)}, u32[]{:S(2)}, u32[]{:S(2)}) collective-permute-start(bf16[768,768]{1,0:T(8,128)(2,1)S(1)} %collective-permute-done.5.refs_13_.refs_15_), channel_id=1, source_target_pairs={{0,16},{1,49},{2,18},{3,51},{4,20},{5,53},{6,22},{7,55},{8,24},{9,... | collective-permute-start | bytes 3538952 | tf_op jit(solution)/shard_map/ppermute | solution.py:53
  69.9 24.9 %collective-permute-start.12 = (bf16[1536,384]{1,0:T(8,128)(2,1)S(1)}, bf16[1536,384]{1,0:T(8,128)(2,1)S(1)}, u32[]{:S(2)}, u32[]{:S(2)}) collective-permute-start(bf16[1536,384]{1,0:T(8,128)(2,1)S(1)} %collective-permute-done.4.refs_5_), channel_id=1, source_target_pairs={{0,6},{1,3},{2,0},{3,5},{4,2},{5,7},{6,4},{7,1},{8,14},{9,11},{10,... | collective-permute-start | bytes 3538952 | tf_op jit(solution)/shard_map/ppermute | solution.py:53
  95.0 5.5 %collective-permute-start.15 = (bf16[3072,384]{1,0:T(8,128)(2,1)S(1)}, bf16[3072,384]{1,0:T(8,128)(2,1)S(1)}, u32[]{:S(2)}, u32[]{:S(2)}) collective-permute-start(bf16[3072,384]{1,0:T(8,128)(2,1)S(1)} %pad_maximum_fusion.2), channel_id=1, source_target_pairs={{0,1},{1,0},{2,3},{3,2},{4,5},{5,4},{6,7},{7,6},{8,9},{9,8},{10,11... | collective-permute-start | bytes 7077896 | tf_op jit(solution)/shard_map/ppermute | solution.py:53
  95.0 22.5 %collective-permute-start.16 = (bf16[1536,384]{1,0:T(8,128)(2,1)S(1)}, bf16[1536,384]{1,0:T(8,128)(2,1)S(1)}, u32[]{:S(2)}, u32[]{:S(2)}) collective-permute-start(bf16[1536,384]{1,0:T(8,128)(2,1)S(1)} %collective-permute-done.10.refs_6_), channel_id=1, source_target_pairs={{0,2},{1,7},{2,4},{3,1},{4,6},{5,3},{6,0},{7,5},{8,10},{9,15},{10,... | collective-permute-start | bytes 3538952 | tf_op jit(solution)/shard_map/ppermute | solution.py:53
  97.8 28.8 %collective-permute-start.20 = (bf16[768,768]{1,0:T(8,128)(2,1)S(1)}, bf16[768,768]{1,0:T(8,128)(2,1)S(1)}, u32[]{:S(2)}, u32[]{:S(2)}) collective-permute-start(bf16[768,768]{1,0:T(8,128)(2,1)S(1)} %collective-permute-done.9.refs_16_.refs_18_), channel_id=1, source_target_pairs={{0,48},{1,17},{2,50},{3,19},{4,52},{5,21},{6,54},{7,23},{8,56},{9,... | collective-permute-start | bytes 3538952 | tf_op jit(solution)/shard_map/ppermute | solution.py:53
  97.8 28.8 %collective-permute-start.18 = (bf16[768,768]{1,0:T(8,128)(2,1)S(1)}, bf16[768,768]{1,0:T(8,128)(2,1)S(1)}, u32[]{:S(2)}, u32[]{:S(2)}) collective-permute-start(bf16[768,768]{1,0:T(8,128)(2,1)S(1)} %collective-permute-done.9.refs_16_.refs_18_), channel_id=1, source_target_pairs={{0,16},{1,49},{2,18},{3,51},{4,20},{5,53},{6,22},{7,55},{8,24},{9,... | collective-permute-start | bytes 3538952 | tf_op jit(solution)/shard_map/ppermute | solution.py:53
  100.5 25.8 %collective-permute-start.19 = (bf16[768,768]{1,0:T(8,128)(2,1)S(1)}, bf16[768,768]{1,0:T(8,128)(2,1)S(1)}, u32[]{:S(2)}, u32[]{:S(2)}) collective-permute-start(bf16[768,768]{1,0:T(8,128)(2,1)S(1)} %collective-permute-done.13.refs_14_.refs_16_), channel_id=1, source_target_pairs={{0,64},{1,65},{2,66},{3,67},{4,68},{5,69},{6,70},{7,71},{8,72},{9,... | collective-permute-start | bytes 3538952 | tf_op jit(solution)/shard_map/ppermute | solution.py:53
  115.4 2.1 %copy-start = (f32[1500,750]{1,0:T(8,128)}, f32[1500,750]{1,0:T(8,128)S(1)}, u32[]{:S(2)}) copy-start(f32[1500,750]{1,0:T(8,128)S(1)} %shard_map.18.refs_22_) | copy-start | bytes 13500004
  117.5 9.1 %collective-permute-start.17 = (bf16[1536,384]{1,0:T(8,128)(2,1)S(1)}, bf16[1536,384]{1,0:T(8,128)(2,1)S(1)}, u32[]{:S(2)}, u32[]{:S(2)}) collective-permute-start(bf16[1536,384]{1,0:T(8,128)(2,1)S(1)} %collective-permute-done.16.refs_7_), channel_id=1, source_target_pairs={{0,1},{1,0},{2,3},{3,2},{4,5},{5,4},{6,7},{7,6},{8,9},{9,8},{10,11... | collective-permute-start | bytes 3538952 | tf_op jit(solution)/shard_map/ppermute | solution.py:53

commit v6 on v5

--- a/solution.py
+++ b/solution.py
@@ -236,10 +236,11 @@
     b0, c1, c3, a2, a3 = (
         send(own, X_FAR), send(c0, Y_RING), send(c0, Y_BACK), send(after(a1, c0_cross), Z_RING), send(own, Z_BACK)
     )
+    e1 = send(jnp.concatenate([a1, a2]), CORES)
     c0, b0, c1, c3, a2, a3 = lax.optimization_barrier((c0, b0, c1, c3, a2, a3))
 
     d0, b1, c2 = send(c0, X_NEAR), send(b0, Z_RING), send(c1, Y_RING)
-    e1, e2 = send(jnp.concatenate([a1, a2]), CORES), send(jnp.concatenate([a3, b0]), CORES)
+    e2 = send(jnp.concatenate([a3, b0]), CORES)
     b3 = send(after(b0, e1), Z_BACK)
     d0, b1, b3, c2, e1, e2 = lax.optimization_barrier((d0, b1, b3, c2, e1, e2))
 

time: 141 us -> 146 us (1.035)
  starting transfers between devices: 31.7 us -> 37.9 us
    ppermute x21, starting transfers between devices: 31.7 us -> 37.9 us  [send(): return lax.ppermute(block, AXES, pairs)]
  transfers between devices with their start and end apart: 21 -> 21, of which waited for: 8 -> 11; matrix products, arithmetic and copies ran while one was open for 0% -> 0% of each run, Pallas kernels for 11% -> 10%
where the time goes in v6:
time: 146 us
  waiting for transfers between devices  73.3 us (50%)
  starting transfers between devices  37.9 us (26%)
  Pallas kernels  30.2 us (21%)
  local copies, waits for them, and re-layouts  3.52 us (2%)
    ppermute x21, waiting for transfers between devices, send(): return lax.ppermute(block, AXES, pairs)  73.3 us
    ppermute x21, starting transfers between devices, send(): return lax.ppermute(block, AXES, pairs)  37.9 us
    pallas_call x2, Pallas kernels, multiply(): pl.pallas_call(kernel, grid=(ROWS // TILE,), out_shape=jax.ShapeDtypeStru...  29.1 us
    unnamed x5, local copies, waits for them, and re-layouts  3.4 us
  transfers between devices with their start and end apart: 21, of which 11 were waited for; matrix products, arithmetic and copies ran while one was open for 0% of the time, Pallas kernels for 10%

profile of v6, /device:TPU:1, one launch (start us, length us, event | category | flops | bytes accessed | tf_op | source)
XLA Modules:
  0.0 146.0 jit_solution(8375988706420717837)
XLA Ops:
  0.1 1.3 copy-done.1
  1.4 1.2 shard_map.17
  2.5 1.5 %collective-permute-start.3 = (bf16[1536,384]{1,0:T(8,128)(2,1)S(1)}, bf16[1536,384]{1,0:T(8,128)(2,1)S(1)}, u32[]{:S(2)}, u32[]{:S(2)}) collective-permute-start(bf16[1536,384]{1,0:T(8,128)(2,1)S(1)} %get-tuple-element.33.refs_1_), channel_id=1, source_target_pairs={{0,1},{1,0},{2,3},{3,2},{4,5},{5,4},{6,7},{7,6},{8,9},{9,8},{10,11... | collective-permute-start | bytes 3538952 | tf_op jit(solution)/shard_map/ppermute | solution.py:53
  4.0 3.8 %collective-permute-start = (bf16[1536,384]{1,0:T(8,128)(2,1)S(1)}, bf16[1536,384]{1,0:T(8,128)(2,1)S(1)}, u32[]{:S(2)}, u32[]{:S(2)}) collective-permute-start(bf16[1536,384]{1,0:T(8,128)(2,1)S(1)} %get-tuple-element.33.refs_1_), channel_id=1, source_target_pairs={{0,2},{1,7},{2,4},{3,1},{4,6},{5,3},{6,0},{7,5},{8,10},{9,15},{10,... | collective-permute-start | bytes 3538952 | tf_op jit(solution)/shard_map/ppermute | solution.py:53
  7.9 5.7 %collective-permute-start.1 = (bf16[384,768]{1,0:T(8,128)(2,1)S(1)}, bf16[384,768]{1,0:T(8,128)(2,1)S(1)}, u32[]{:S(2)}, u32[]{:S(2)}) collective-permute-start(bf16[384,768]{1,0:T(8,128)(2,1)S(1)} %get-tuple-element.29), channel_id=1, source_target_pairs={{0,0},{1,97},{2,48},{3,81},{4,32},{5,65},{6,16},{7,113},{8,64},{9,... | collective-permute-start | bytes 1769480 | tf_op jit(solution)/shard_map/ppermute | solution.py:53
  13.7 11.1 %collective-permute-done.1 = bf16[384,768]{1,0:T(8,128)(2,1)S(1)} collective-permute-done((bf16[384,768]{1,0:T(8,128)(2,1)S(1)}, bf16[384,768]{1,0:T(8,128)(2,1)S(1)}, u32[]{:S(2)}, u32[]{:S(2)}) %collective-permute-start.1) | collective-permute-done | bytes 589856 | tf_op jit(solution)/shard_map/ppermute | solution.py:53
  24.8 4.0 %collective-permute-done.2 = bf16[384,768]{1,0:T(8,128)(2,1)S(1)} collective-permute-done((bf16[384,768]{1,0:T(8,128)(2,1)S(1)}, bf16[384,768]{1,0:T(8,128)(2,1)S(1)}, u32[]{:S(2)}, u32[]{:S(2)}) %collective-permute-start.2) | collective-permute-done | bytes 589856 | tf_op jit(solution)/shard_map/ppermute | solution.py:53
  28.9 4.8 %collective-permute-done.refs_2_ = bf16[1536,384]{1,0:T(8,128)(2,1)S(1)} collective-permute-done((bf16[1536,384]{1,0:T(8,128)(2,1)S(1)}, bf16[1536,384]{1,0:T(8,128)(2,1)S(1)}, u32[]{:S(2)}, u32[]{:S(2)}) %collective-permute-start) | collective-permute-done | bytes 1179680 | tf_op jit(solution)/shard_map/ppermute | solution.py:53
  33.7 3.1 %collective-permute-start.7 = (bf16[1536,384]{1,0:T(8,128)(2,1)S(1)}, bf16[1536,384]{1,0:T(8,128)(2,1)S(1)}, u32[]{:S(2)}, u32[]{:S(2)}) collective-permute-start(bf16[1536,384]{1,0:T(8,128)(2,1)S(1)} %collective-permute-done.refs_2_), channel_id=1, source_target_pairs={{0,2},{1,7},{2,4},{3,1},{4,6},{5,3},{6,0},{7,5},{8,10},{9,15},{10,... | collective-permute-start | bytes 3538952 | tf_op jit(solution)/shard_map/ppermute | solution.py:53
  36.9 1.4 collective-permute-start.6
  38.2 1.5 %collective-permute-start.5 = (bf16[768,768]{1,0:T(8,128)(2,1)S(1)}, bf16[768,768]{1,0:T(8,128)(2,1)S(1)}, u32[]{:S(2)}, u32[]{:S(2)}) collective-permute-start(bf16[768,768]{1,0:T(8,128)(2,1)S(1)} %constant_dynamic-update-slice_fusion.refs_12_.refs_14_), channel_id=1, source_target_pairs={{0,16},{1,49},{2,18},{3,51},{4,20},{5,53},{6,22},{7,55},{8,24},{9,... | collective-permute-start | bytes 3538952 | tf_op jit(solution)/shard_map/ppermute | solution.py:53
  39.8 2.7 %collective-permute-start.4 = (bf16[1536,384]{1,0:T(8,128)(2,1)S(1)}, bf16[1536,384]{1,0:T(8,128)(2,1)S(1)}, u32[]{:S(2)}, u32[]{:S(2)}) collective-permute-start(bf16[1536,384]{1,0:T(8,128)(2,1)S(1)} %get-tuple-element.33.refs_1_), channel_id=1, source_target_pairs={{0,8},{1,9},{2,10},{3,11},{4,12},{5,13},{6,14},{7,15},{8,0},{9,1},... | collective-permute-start | bytes 3538952 | tf_op jit(solution)/shard_map/ppermute | solution.py:53
  42.5 15.1 %collective-permute-done.7.refs_3_ = bf16[1536,384]{1,0:T(8,128)(2,1)S(1)} collective-permute-done((bf16[1536,384]{1,0:T(8,128)(2,1)S(1)}, bf16[1536,384]{1,0:T(8,128)(2,1)S(1)}, u32[]{:S(2)}, u32[]{:S(2)}) %collective-permute-start.7) | collective-permute-done | bytes 1179680 | tf_op jit(solution)/shard_map/ppermute | solution.py:53
  57.9 3.3 %collective-permute-start.11 = (bf16[3072,384]{1,0:T(8,128)(2,1)S(1)}, bf16[3072,384]{1,0:T(8,128)(2,1)S(1)}, u32[]{:S(2)}, u32[]{:S(2)}) collective-permute-start(bf16[3072,384]{1,0:T(8,128)(2,1)S(1)} %pad_maximum_fusion), channel_id=1, source_target_pairs={{0,1},{1,0},{2,3},{3,2},{4,5},{5,4},{6,7},{7,6},{8,9},{9,8},{10,11... | collective-permute-start | bytes 7077896 | tf_op jit(solution)/shard_map/ppermute | solution.py:53
  61.1 3.3 %collective-permute-done.6.refs_15_.refs_17_ = bf16[768,768]{1,0:T(8,128)(2,1)S(1)} collective-permute-done((bf16[768,768]{1,0:T(8,128)(2,1)S(1)}, bf16[768,768]{1,0:T(8,128)(2,1)S(1)}, u32[]{:S(2)}, u32[]{:S(2)}) %collective-permute-start.6) | collective-permute-done | bytes 1179680 | tf_op jit(solution)/shard_map/ppermute | solution.py:53
  64.4 0.3 collective-permute-done.8.refs_4_
  64.7 2.3 %collective-permute-done.4.refs_5_ = bf16[1536,384]{1,0:T(8,128)(2,1)S(1)} collective-permute-done((bf16[1536,384]{1,0:T(8,128)(2,1)S(1)}, bf16[1536,384]{1,0:T(8,128)(2,1)S(1)}, u32[]{:S(2)}, u32[]{:S(2)}) %collective-permute-start.4) | collective-permute-done | bytes 1179680 | tf_op jit(solution)/shard_map/ppermute | solution.py:53
  67.0 0.2 pad_maximum_fusion.1
  67.3 2.7 %collective-permute-start.14 = (bf16[3072,384]{1,0:T(8,128)(2,1)S(1)}, bf16[3072,384]{1,0:T(8,128)(2,1)S(1)}, u32[]{:S(2)}, u32[]{:S(2)}) collective-permute-start(bf16[3072,384]{1,0:T(8,128)(2,1)S(1)} %pad_maximum_fusion.1), channel_id=1, source_target_pairs={{0,1},{1,0},{2,3},{3,2},{4,5},{5,4},{6,7},{7,6},{8,9},{9,8},{10,11... | collective-permute-start | bytes 7077896 | tf_op jit(solution)/shard_map/ppermute | solution.py:53
  70.0 2.7 %collective-permute-start.10 = (bf16[1536,384]{1,0:T(8,128)(2,1)S(1)}, bf16[1536,384]{1,0:T(8,128)(2,1)S(1)}, u32[]{:S(2)}, u32[]{:S(2)}) collective-permute-start(bf16[1536,384]{1,0:T(8,128)(2,1)S(1)} %collective-permute-done.4.refs_5_), channel_id=1, source_target_pairs={{0,2},{1,7},{2,4},{3,1},{4,6},{5,3},{6,0},{7,5},{8,10},{9,15},{10,... | collective-permute-start | bytes 3538952 | tf_op jit(solution)/shard_map/ppermute | solution.py:53
  72.6 1.2 collective-permute-start.9
  73.9 1.4 collective-permute-start.13
  75.3 23.1 %collective-permute-done.9.refs_16_.refs_18_ = bf16[768,768]{1,0:T(8,128)(2,1)S(1)} collective-permute-done((bf16[768,768]{1,0:T(8,128)(2,1)S(1)}, bf16[768,768]{1,0:T(8,128)(2,1)S(1)}, u32[]{:S(2)}, u32[]{:S(2)}) %collective-permute-start.9) | collective-permute-done | bytes 1179680 | tf_op jit(solution)/shard_map/ppermute | solution.py:53
  98.3 1.1 collective-permute-done.12.refs_7_.refs_8_
  99.8 2.8 %collective-permute-start.16 = (bf16[1536,384]{1,0:T(8,128)(2,1)S(1)}, bf16[1536,384]{1,0:T(8,128)(2,1)S(1)}, u32[]{:S(2)}, u32[]{:S(2)}) collective-permute-start(bf16[1536,384]{1,0:T(8,128)(2,1)S(1)} %collective-permute-done.10.refs_6_), channel_id=1, source_target_pairs={{0,2},{1,7},{2,4},{3,1},{4,6},{5,3},{6,0},{7,5},{8,10},{9,15},{10,... | collective-permute-start | bytes 3538952 | tf_op jit(solution)/shard_map/ppermute | solution.py:53
  102.6 2.7 %collective-permute-start.18 = (bf16[768,768]{1,0:T(8,128)(2,1)S(1)}, bf16[768,768]{1,0:T(8,128)(2,1)S(1)}, u32[]{:S(2)}, u32[]{:S(2)}) collective-permute-start(bf16[768,768]{1,0:T(8,128)(2,1)S(1)} %collective-permute-done.9.refs_16_.refs_18_), channel_id=1, source_target_pairs={{0,16},{1,49},{2,18},{3,51},{4,20},{5,53},{6,22},{7,55},{8,24},{9,... | collective-permute-start | bytes 3538952 | tf_op jit(solution)/shard_map/ppermute | solution.py:53
  105.2 1.2 collective-permute-start.19
  106.5 14.9 %shard_map.18.refs_22_ = f32[1500,750]{1,0:T(8,128)S(1)} custom-call(s32[5]{0:T(128)S(1)} %stack.23.spot.refs_0_, bf16[1536,384]{1,0:T(8,128)(2,1)S(1)} %get-tuple-element.33.refs_1_, bf16[1536,384]{1,0:T(8,128)(2,1)S(1)} %collective-permute-done.refs_2_, bf16[1536,384]{1,0:T(8,128)(2,1)S(1)} %collective-permute-done.7.refs_3_, ...), custom_call_target="tpu_custom_call" | custom-call | flops 8640000000 | bytes 22194720 | tf_op jit(solution)/shard_map/pallas_call | solution.py:203
  121.4 2.1 %copy-done = f32[1500,750]{1,0:T(8,128)} copy-done((f32[1500,750]{1,0:T(8,128)}, f32[1500,750]{1,0:T(8,128)S(1)}, u32[]{:S(2)}) %copy-start) | copy-done | bytes 4500024
  123.5 7.5 %collective-permute-done.19.refs_20_ = bf16[768,768]{1,0:T(8,128)(2,1)S(1)} collective-permute-done((bf16[768,768]{1,0:T(8,128)(2,1)S(1)}, bf16[768,768]{1,0:T(8,128)(2,1)S(1)}, u32[]{:S(2)}, u32[]{:S(2)}) %collective-permute-start.19) | collective-permute-done | bytes 1179680 | tf_op jit(solution)/shard_map/ppermute | solution.py:53
  131.0 0.7 collective-permute-done.20.refs_21_
  131.7 14.2 %shard_map.19 = f32[1500,750]{1,0:T(8,128)} custom-call(s32[5]{0:T(128)S(1)} %stack.23.spot.refs_0_, bf16[1536,384]{1,0:T(8,128)(2,1)S(1)} %get-tuple-element.33.refs_1_, bf16[1536,384]{1,0:T(8,128)(2,1)S(1)} %collective-permute-done.refs_2_, bf16[1536,384]{1,0:T(8,128)(2,1)S(1)} %collective-permute-done.7.refs_3_, ...), custom_call_target="tpu_custom_call" | custom-call | flops 6912000000 | bytes 23155776 | tf_op jit(solution)/shard_map/pallas_call | solution.py:203
  (23 shorter events, 0.8 us)
Async XLA Ops:
  0.1 1.3 copy-start.1
  2.5 26.4 %collective-permute-start.3 = (bf16[1536,384]{1,0:T(8,128)(2,1)S(1)}, bf16[1536,384]{1,0:T(8,128)(2,1)S(1)}, u32[]{:S(2)}, u32[]{:S(2)}) collective-permute-start(bf16[1536,384]{1,0:T(8,128)(2,1)S(1)} %get-tuple-element.33.refs_1_), channel_id=1, source_target_pairs={{0,1},{1,0},{2,3},{3,2},{4,5},{5,4},{6,7},{7,6},{8,9},{9,8},{10,11... | collective-permute-start | bytes 3538952 | tf_op jit(solution)/shard_map/ppermute | solution.py:53
  4.0 29.6 %collective-permute-start = (bf16[1536,384]{1,0:T(8,128)(2,1)S(1)}, bf16[1536,384]{1,0:T(8,128)(2,1)S(1)}, u32[]{:S(2)}, u32[]{:S(2)}) collective-permute-start(bf16[1536,384]{1,0:T(8,128)(2,1)S(1)} %get-tuple-element.33.refs_1_), channel_id=1, source_target_pairs={{0,2},{1,7},{2,4},{3,1},{4,6},{5,3},{6,0},{7,5},{8,10},{9,15},{10,... | collective-permute-start | bytes 3538952 | tf_op jit(solution)/shard_map/ppermute | solution.py:53
  7.9 17.0 %collective-permute-start.1 = (bf16[384,768]{1,0:T(8,128)(2,1)S(1)}, bf16[384,768]{1,0:T(8,128)(2,1)S(1)}, u32[]{:S(2)}, u32[]{:S(2)}) collective-permute-start(bf16[384,768]{1,0:T(8,128)(2,1)S(1)} %get-tuple-element.29), channel_id=1, source_target_pairs={{0,0},{1,97},{2,48},{3,81},{4,32},{5,65},{6,16},{7,113},{8,64},{9,... | collective-permute-start | bytes 1769480 | tf_op jit(solution)/shard_map/ppermute | solution.py:53
  13.6 15.3 %collective-permute-start.2 = (bf16[384,768]{1,0:T(8,128)(2,1)S(1)}, bf16[384,768]{1,0:T(8,128)(2,1)S(1)}, u32[]{:S(2)}, u32[]{:S(2)}) collective-permute-start(bf16[384,768]{1,0:T(8,128)(2,1)S(1)} %get-tuple-element.30), channel_id=1, source_target_pairs={{0,97},{1,0},{2,81},{3,48},{4,65},{5,32},{6,113},{7,16},{8,33},{9,... | collective-permute-start | bytes 1769480 | tf_op jit(solution)/shard_map/ppermute | solution.py:53
  33.7 24.0 %collective-permute-start.7 = (bf16[1536,384]{1,0:T(8,128)(2,1)S(1)}, bf16[1536,384]{1,0:T(8,128)(2,1)S(1)}, u32[]{:S(2)}, u32[]{:S(2)}) collective-permute-start(bf16[1536,384]{1,0:T(8,128)(2,1)S(1)} %collective-permute-done.refs_2_), channel_id=1, source_target_pairs={{0,2},{1,7},{2,4},{3,1},{4,6},{5,3},{6,0},{7,5},{8,10},{9,15},{10,... | collective-permute-start | bytes 3538952 | tf_op jit(solution)/shard_map/ppermute | solution.py:53
  36.9 27.6 %collective-permute-start.6 = (bf16[768,768]{1,0:T(8,128)(2,1)S(1)}, bf16[768,768]{1,0:T(8,128)(2,1)S(1)}, u32[]{:S(2)}, u32[]{:S(2)}) collective-permute-start(bf16[768,768]{1,0:T(8,128)(2,1)S(1)} %constant_dynamic-update-slice_fusion.refs_12_.refs_14_), channel_id=1, source_target_pairs={{0,48},{1,17},{2,50},{3,19},{4,52},{5,21},{6,54},{7,23},{8,56},{9,... | collective-permute-start | bytes 3538952 | tf_op jit(solution)/shard_map/ppermute | solution.py:53
  38.2 26.2 %collective-permute-start.5 = (bf16[768,768]{1,0:T(8,128)(2,1)S(1)}, bf16[768,768]{1,0:T(8,128)(2,1)S(1)}, u32[]{:S(2)}, u32[]{:S(2)}) collective-permute-start(bf16[768,768]{1,0:T(8,128)(2,1)S(1)} %constant_dynamic-update-slice_fusion.refs_12_.refs_14_), channel_id=1, source_target_pairs={{0,16},{1,49},{2,18},{3,51},{4,20},{5,53},{6,22},{7,55},{8,24},{9,... | collective-permute-start | bytes 3538952 | tf_op jit(solution)/shard_map/ppermute | solution.py:53
  39.8 25.0 %collective-permute-start.8 = (bf16[1536,384]{1,0:T(8,128)(2,1)S(1)}, bf16[1536,384]{1,0:T(8,128)(2,1)S(1)}, u32[]{:S(2)}, u32[]{:S(2)}) collective-permute-start(bf16[1536,384]{1,0:T(8,128)(2,1)S(1)} %get-tuple-element.33.refs_1_), channel_id=1, source_target_pairs={{0,6},{1,3},{2,0},{3,5},{4,2},{5,7},{6,4},{7,1},{8,14},{9,11},{10,... | collective-permute-start | bytes 3538952 | tf_op jit(solution)/shard_map/ppermute | solution.py:53
  39.8 27.2 %collective-permute-start.4 = (bf16[1536,384]{1,0:T(8,128)(2,1)S(1)}, bf16[1536,384]{1,0:T(8,128)(2,1)S(1)}, u32[]{:S(2)}, u32[]{:S(2)}) collective-permute-start(bf16[1536,384]{1,0:T(8,128)(2,1)S(1)} %get-tuple-element.33.refs_1_), channel_id=1, source_target_pairs={{0,8},{1,9},{2,10},{3,11},{4,12},{5,13},{6,14},{7,15},{8,0},{9,1},... | collective-permute-start | bytes 3538952 | tf_op jit(solution)/shard_map/ppermute | solution.py:53
  57.9 17.4 %collective-permute-start.11 = (bf16[3072,384]{1,0:T(8,128)(2,1)S(1)}, bf16[3072,384]{1,0:T(8,128)(2,1)S(1)}, u32[]{:S(2)}, u32[]{:S(2)}) collective-permute-start(bf16[3072,384]{1,0:T(8,128)(2,1)S(1)} %pad_maximum_fusion), channel_id=1, source_target_pairs={{0,1},{1,0},{2,3},{3,2},{4,5},{5,4},{6,7},{7,6},{8,9},{9,8},{10,11... | collective-permute-start | bytes 7077896 | tf_op jit(solution)/shard_map/ppermute | solution.py:53
  67.3 31.1 %collective-permute-start.14 = (bf16[3072,384]{1,0:T(8,128)(2,1)S(1)}, bf16[3072,384]{1,0:T(8,128)(2,1)S(1)}, u32[]{:S(2)}, u32[]{:S(2)}) collective-permute-start(bf16[3072,384]{1,0:T(8,128)(2,1)S(1)} %pad_maximum_fusion.1), channel_id=1, source_target_pairs={{0,1},{1,0},{2,3},{3,2},{4,5},{5,4},{6,7},{7,6},{8,9},{9,8},{10,11... | collective-permute-start | bytes 7077896 | tf_op jit(solution)/shard_map/ppermute | solution.py:53
  70.0 28.3 %collective-permute-start.10 = (bf16[1536,384]{1,0:T(8,128)(2,1)S(1)}, bf16[1536,384]{1,0:T(8,128)(2,1)S(1)}, u32[]{:S(2)}, u32[]{:S(2)}) collective-permute-start(bf16[1536,384]{1,0:T(8,128)(2,1)S(1)} %collective-permute-done.4.refs_5_), channel_id=1, source_target_pairs={{0,2},{1,7},{2,4},{3,1},{4,6},{5,3},{6,0},{7,5},{8,10},{9,15},{10,... | collective-permute-start | bytes 3538952 | tf_op jit(solution)/shard_map/ppermute | solution.py:53
  72.6 25.7 %collective-permute-start.9 = (bf16[768,768]{1,0:T(8,128)(2,1)S(1)}, bf16[768,768]{1,0:T(8,128)(2,1)S(1)}, u32[]{:S(2)}, u32[]{:S(2)}) collective-permute-start(bf16[768,768]{1,0:T(8,128)(2,1)S(1)} %constant_dynamic-update-slice_fusion.refs_12_.refs_14_), channel_id=1, source_target_pairs={{0,64},{1,65},{2,66},{3,67},{4,68},{5,69},{6,70},{7,71},{8,72},{9,... | collective-permute-start | bytes 3538952 | tf_op jit(solution)/shard_map/ppermute | solution.py:53
  73.9 24.4 %collective-permute-start.13 = (bf16[768,768]{1,0:T(8,128)(2,1)S(1)}, bf16[768,768]{1,0:T(8,128)(2,1)S(1)}, u32[]{:S(2)}, u32[]{:S(2)}) collective-permute-start(bf16[768,768]{1,0:T(8,128)(2,1)S(1)} %collective-permute-done.5.refs_13_.refs_15_), channel_id=1, source_target_pairs={{0,16},{1,49},{2,18},{3,51},{4,20},{5,53},{6,22},{7,55},{8,24},{9,... | collective-permute-start | bytes 3538952 | tf_op jit(solution)/shard_map/ppermute | solution.py:53
  75.2 24.2 %collective-permute-start.12 = (bf16[1536,384]{1,0:T(8,128)(2,1)S(1)}, bf16[1536,384]{1,0:T(8,128)(2,1)S(1)}, u32[]{:S(2)}, u32[]{:S(2)}) collective-permute-start(bf16[1536,384]{1,0:T(8,128)(2,1)S(1)} %collective-permute-done.4.refs_5_), channel_id=1, source_target_pairs={{0,6},{1,3},{2,0},{3,5},{4,2},{5,7},{6,4},{7,1},{8,14},{9,11},{10,... | collective-permute-start | bytes 3538952 | tf_op jit(solution)/shard_map/ppermute | solution.py:53
  99.7 6.8 %collective-permute-start.15 = (bf16[3072,384]{1,0:T(8,128)(2,1)S(1)}, bf16[3072,384]{1,0:T(8,128)(2,1)S(1)}, u32[]{:S(2)}, u32[]{:S(2)}) collective-permute-start(bf16[3072,384]{1,0:T(8,128)(2,1)S(1)} %pad_maximum_fusion.2), channel_id=1, source_target_pairs={{0,1},{1,0},{2,3},{3,2},{4,5},{5,4},{6,7},{7,6},{8,9},{9,8},{10,11... | collective-permute-start | bytes 7077896 | tf_op jit(solution)/shard_map/ppermute | solution.py:53
  99.8 23.7 %collective-permute-start.16 = (bf16[1536,384]{1,0:T(8,128)(2,1)S(1)}, bf16[1536,384]{1,0:T(8,128)(2,1)S(1)}, u32[]{:S(2)}, u32[]{:S(2)}) collective-permute-start(bf16[1536,384]{1,0:T(8,128)(2,1)S(1)} %collective-permute-done.10.refs_6_), channel_id=1, source_target_pairs={{0,2},{1,7},{2,4},{3,1},{4,6},{5,3},{6,0},{7,5},{8,10},{9,15},{10,... | collective-permute-start | bytes 3538952 | tf_op jit(solution)/shard_map/ppermute | solution.py:53
  102.6 29.1 %collective-permute-start.20 = (bf16[768,768]{1,0:T(8,128)(2,1)S(1)}, bf16[768,768]{1,0:T(8,128)(2,1)S(1)}, u32[]{:S(2)}, u32[]{:S(2)}) collective-permute-start(bf16[768,768]{1,0:T(8,128)(2,1)S(1)} %collective-permute-done.9.refs_16_.refs_18_), channel_id=1, source_target_pairs={{0,48},{1,17},{2,50},{3,19},{4,52},{5,21},{6,54},{7,23},{8,56},{9,... | collective-permute-start | bytes 3538952 | tf_op jit(solution)/shard_map/ppermute | solution.py:53
  102.6 29.1 %collective-permute-start.18 = (bf16[768,768]{1,0:T(8,128)(2,1)S(1)}, bf16[768,768]{1,0:T(8,128)(2,1)S(1)}, u32[]{:S(2)}, u32[]{:S(2)}) collective-permute-start(bf16[768,768]{1,0:T(8,128)(2,1)S(1)} %collective-permute-done.9.refs_16_.refs_18_), channel_id=1, source_target_pairs={{0,16},{1,49},{2,18},{3,51},{4,20},{5,53},{6,22},{7,55},{8,24},{9,... | collective-permute-start | bytes 3538952 | tf_op jit(solution)/shard_map/ppermute | solution.py:53
  105.2 25.8 %collective-permute-start.19 = (bf16[768,768]{1,0:T(8,128)(2,1)S(1)}, bf16[768,768]{1,0:T(8,128)(2,1)S(1)}, u32[]{:S(2)}, u32[]{:S(2)}) collective-permute-start(bf16[768,768]{1,0:T(8,128)(2,1)S(1)} %collective-permute-done.13.refs_14_.refs_16_), channel_id=1, source_target_pairs={{0,64},{1,65},{2,66},{3,67},{4,68},{5,69},{6,70},{7,71},{8,72},{9,... | collective-permute-start | bytes 3538952 | tf_op jit(solution)/shard_map/ppermute | solution.py:53
  121.4 2.1 %copy-start = (f32[1500,750]{1,0:T(8,128)}, f32[1500,750]{1,0:T(8,128)S(1)}, u32[]{:S(2)}) copy-start(f32[1500,750]{1,0:T(8,128)S(1)} %shard_map.18.refs_22_) | copy-start | bytes 13500004
  123.5 8.2 %collective-permute-start.17 = (bf16[1536,384]{1,0:T(8,128)(2,1)S(1)}, bf16[1536,384]{1,0:T(8,128)(2,1)S(1)}, u32[]{:S(2)}, u32[]{:S(2)}) collective-permute-start(bf16[1536,384]{1,0:T(8,128)(2,1)S(1)} %collective-permute-done.16.refs_7_), channel_id=1, source_target_pairs={{0,1},{1,0},{2,3},{3,2},{4,5},{5,4},{6,7},{7,6},{8,9},{9,8},{10,11... | collective-permute-start | bytes 3538952 | tf_op jit(solution)/shard_map/ppermute | solution.py:53
